TPU v7x, 256 devices: a whole 4x4x8 slice. The times are simulated.
256 devices in a mesh: hst: 32 (over y, z_hi, x), local: 8 (over z_lo, core).
Axes of the slice: x: 4, y: 4, z: 8 (z_hi: 2, z_lo: 4; z = z_hi * 4 + z_lo), core: 2. Of those that a mesh axis runs over, the one named last changes fastest.
Arguments:
- pooled: bfloat16 [32768, 64, 128], P(('hst', 'local')), may hold values from -6 to 6
- cotangent: bfloat16 [32768, 64, 128], P(('hst', 'local')), may hold values from -6 to 6
- projection: bfloat16 [64, 16], replicated, may hold values from -0.75 to 0.75
- w_up: bfloat16 [1024, 512], replicated, may hold values from -0.1875 to 0.1875
- w_down: bfloat16 [512, 4096], replicated, may hold values from -0.25 to 0.25
- w_compress: bfloat16 [32, 64], replicated, may hold values from -0.75 to 0.75
- ln_gain: float32 [128], replicated, may hold values from 0.5 to 1.5
- feature_map: int32 [64], replicated, may hold values from 0 to 63, each once
- bag_row_index: int32 [32768, 64, 2], P(('hst', 'local')), may hold values from 0 to 4095
Outputs:
- table_grad: float32 [64, 4096, 128], P('hst', 'local')
- grad_w_up: float32 [1024, 512], P(('hst', 'local'))
- grad_w_down: float32 [512, 4096], P(('hst', 'local'))
- grad_projection: float32 [64, 16], replicated
- compress_weight_gradient: float32 [32, 64], replicated
- grad_gain: float32 [128], replicated
Inputs may be any that keep to these rules, and one draw needn't show every extreme that they name: feature_map names every feature once.
All inputs are finite; a program needn't handle non-finite values.
Results may differ from a plain program's by a relative error of at most 0.0095.
Values may be sent and summed in bfloat16 or wider, within the bound.
No kernel may reach another device: no remote copies, remote signals or barrier semaphores. Data moves between devices by JAX's collectives and lax.ppermute only.
A program may use at most 128 MiB of HBM per device.

v0:
```python
import math

import jax
import jax.numpy as jnp
from jax import lax
from jax.sharding import PartitionSpec as P

ROWS_DEV = 512


def product(form, left, right):
    return jnp.einsum(form, left, right, preferred_element_type=jnp.float32)


def row_norm(values, axis_sel):
    centered_values = values - jnp.mean(values, axis=axis_sel, keepdims=True)
    inverse = lax.rsqrt(
        jnp.mean(centered_values * centered_values, axis=axis_sel, keepdims=True) + 1e-05
    )
    return (centered_values * inverse, inverse)


def norm_back(grad_in, normed, inverse, axis_sel):
    first = jnp.mean(grad_in, axis=axis_sel, keepdims=True)
    second = jnp.mean(grad_in * normed, axis=axis_sel, keepdims=True)
    return inverse * (grad_in - first - normed * second)


def forward_backward(pooled, cotangent, projection, w_up, w_down, w_compress, ln_gain):
    batch, width_n, width_d = pooled.shape
    rank = projection.shape[1]
    fm_rows = width_n - w_compress.shape[0]
    proj_part = product("bnd,nk->bdk", pooled, projection).astype(jnp.bfloat16)
    inter = product("bnd,bdk->bnk", pooled, proj_part).reshape(batch, width_n * rank)
    normed_fm, inverse_fm = row_norm(inter, 1)
    normalized_feature_map_batch = normed_fm.astype(jnp.bfloat16)
    preact = product("bi,ih->bh", normalized_feature_map_batch, w_up)
    hidden = jax.nn.silu(preact).astype(jnp.bfloat16)
    fm_out = product("bh,hj->bj", hidden, w_down).reshape(batch, fm_rows, width_d)
    lc_out = product("mn,bnd->bmd", w_compress, pooled)
    summed = jnp.concatenate([fm_out, lc_out], axis=1) + pooled.astype(jnp.float32)
    normed_out, inverse_out = row_norm(summed, 2)
    cot_float = cotangent.astype(jnp.float32)
    grad_gain = jnp.sum(cot_float * normed_out, axis=(0, 1))
    dsum = norm_back(cot_float * ln_gain, normed_out, inverse_out, 2)
    dfm = dsum[:, :fm_rows].reshape(batch, fm_rows * width_d).astype(jnp.bfloat16)
    dlc = dsum[:, fm_rows:].astype(jnp.bfloat16)
    hidden_gradient = product("bj,hj->bh", dfm, w_down)
    sigmoid_pre = jax.nn.sigmoid(preact)
    dpre = (hidden_gradient * sigmoid_pre * (1.0 + preact * (1.0 - sigmoid_pre))).astype(
        jnp.bfloat16
    )
    dnormed = product("bh,ih->bi", dpre, w_up)
    dinter = (
        norm_back(dnormed, normed_fm, inverse_fm, 1)
        .reshape(batch, width_n, rank)
        .astype(jnp.bfloat16)
    )
    dproj = product("bnd,bnk->bdk", pooled, dinter).astype(jnp.bfloat16)
    dpooled = dsum + product("mn,bmd->bnd", w_compress, dlc)
    dpooled = (
        dpooled
        + product("bnk,bdk->bnd", dinter, proj_part)
        + product("nk,bdk->bnd", projection, dproj)
    )
    grad_projection = product("bnd,bdk->nk", pooled, dproj)
    compress_weight_gradient = product("bmd,bnd->mn", dlc, pooled)
    return (
        dpooled.astype(jnp.bfloat16),
        (normalized_feature_map_batch, dpre, hidden, dfm),
        (grad_projection, compress_weight_gradient, grad_gain),
    )


def block_rows(gradient_list, idents, row_start, row_count):
    step_rows = math.gcd(row_count, 128)
    offsets = row_start + jnp.arange(row_count // step_rows, dtype=jnp.int32) * step_rows
    columns = jnp.arange(step_rows, dtype=jnp.int32)

    def one_offset(offset):
        shifted = idents - offset
        member_matches = jnp.sum((shifted[..., None] == columns).astype(jnp.int32), axis=2).astype(
            jnp.bfloat16
        )
        return jnp.einsum(
            "itz,itn->ztn", member_matches, gradient_list, preferred_element_type=jnp.float32
        )

    row_blocks = lax.map(one_offset, offsets)
    return row_blocks.reshape(row_count, gradient_list.shape[1], gradient_list.shape[2])


def shards(
    pooled, cotangent, projection, w_up, w_down, w_compress, ln_gain, feature_map, bag_row_index
):
    host_count = lax.axis_size("hst")
    local_count = lax.axis_size("local")
    batch, width_n, width_d = pooled.shape
    grad_scale = float(batch * host_count * local_count) ** (-0.5)
    dpooled, (normed_b, dpre, hidden, dfm), small_terms = forward_backward(
        pooled, cotangent, projection, w_up, w_down, w_compress, ln_gain
    )
    picker = (feature_map[:, None] == jnp.arange(width_n, dtype=jnp.int32)[None, :]).astype(
        jnp.bfloat16
    )
    ordered = jnp.einsum("sf,bfe->bse", picker, dpooled, preferred_element_type=jnp.float32).astype(
        jnp.bfloat16
    )
    ordered_ids = jnp.take(bag_row_index, feature_map, axis=1)
    per_host = width_n // host_count
    bag_width = bag_row_index.shape[2]
    ordered = ordered.reshape(batch, host_count, per_host, width_d)
    ordered_ids = ordered_ids.reshape(batch, host_count, per_host, bag_width)
    bags, bag_rows = (
        lax.all_to_all(ordered, "hst", split_axis=1, concat_axis=0, tiled=True),
        lax.all_to_all(ordered_ids, "hst", split_axis=1, concat_axis=0, tiled=True),
    )
    bags = bags.reshape(host_count * batch, per_host, width_d)
    bag_rows = bag_rows.reshape(host_count * batch, per_host, bag_width)
    row_base = lax.axis_index("local") * ROWS_DEV
    own_rows = block_rows(
        lax.all_gather(bags, "local", axis=0, tiled=True),
        lax.all_gather(bag_rows, "local", axis=0, tiled=True),
        row_base,
        ROWS_DEV,
    )
    table_grad = jnp.transpose(own_rows, (1, 0, 2))
    sliced = normed_b
    grad_w_up = lax.psum_scatter(
        grad_scale * product("bi,bh->ih", sliced, dpre),
        ("hst", "local"),
        scatter_dimension=0,
        tiled=True,
    )
    sliced = hidden
    grad_w_down = lax.psum_scatter(
        grad_scale * product("bh,bj->hj", sliced, dfm),
        ("hst", "local"),
        scatter_dimension=0,
        tiled=True,
    )
    grad_projection, compress_weight_gradient, grad_gain = lax.psum(
        (small_terms[0] * grad_scale, small_terms[1] * grad_scale, small_terms[2] * grad_scale),
        ("hst", "local"),
    )
    return (
        table_grad,
        grad_w_up,
        grad_w_down,
        grad_projection,
        compress_weight_gradient,
        grad_gain,
    )


def solution(mesh):
    placed = (
        P(("hst", "local"), None, None),
        P(("hst", "local"), None, None),
        P(),
        P(),
        P(),
        P(),
        P(),
        P(),
        P(("hst", "local"), None, None),
    )
    return jax.shard_map(
        shards,
        mesh=mesh,
        in_specs=placed,
        out_specs=(
            P("hst", "local", None),
            P(("hst", "local"), None),
            P(("hst", "local"), None),
            P(),
            P(),
            P(),
        ),
        check_vma=False,
    )
```

profile of v0, /device:TPU:7, one launch (start us, length us, event | category | flops | bytes accessed | tf_op | source)
XLA Modules:
  0.0 733.7 jit_solution(3205491123123110288)
XLA Ops:
  8.1 2.1 convolution_convert_fusion.2
  10.9 3.0 fusion.48
  14.0 1.9 multiply_reduce_fusion.1
  17.8 3.1 convolution_bitcast_fusion.1
  22.9 2.7 multiply_reduce_fusion
  26.0 5.5 fusion.16
  31.5 4.9 fusion.20
  37.9 1.5 fusion.23
  39.5 4.5 convolution_multiply_fusion
  44.0 1.9 convolution_multiply_fusion.1
  46.2 1.7 fusion.46
  47.9 4.0 fusion.32
  53.6 1.7 fusion.21
  55.4 3.8 fusion.49
  59.2 9.8 %convolution_convert_fusion = bf16[128,128,64]{1,2,0:T(8,128)(2,1)} fusion(f32[128,64,128]{2,1,0:T(8,128)} %fusion.49, f32[128,128,64]{1,2,0:T(8,128)} %fusion.32, bf16[128,128,16]{1,2,0:T(8,128)(2,1)S(1)} %fusion.21, bf16[128,64,128]{2,1,0:T(8,128)(2,1)} %param.12, f32[128,64,128]{2,1,0:T(8,128)} %copy-done.3, f32[128,64]{1,0:T(8,128)S(1)} %get-tuple-element.76, ...), kind=kOutput, calls=%fused_computation.26 | convolution fusion | flops 181407744 | bytes 17435392 | tf_op jit(solution)/shard_map/sf,bfe->bse/dot_general | solution.py:106
  69.0 3.8 copy.56
  72.8 69.7 %all_to_all.30 = bf16[128,32,2,128]{3,2,0,1:T(2,128)(2,1)S(1)} all-to-all(bf16[128,32,2,128]{3,2,0,1:T(2,128)(2,1)S(1)} %copy.56), channel_id=1, replica_groups=mesh['hst'=32,'local'=8] {'hst'}, dimensions={1} | all-to-all | bytes 4194304 | tf_op jit(solution)/shard_map/all_to_all | solution.py:115
  142.5 1.6 copy.57
  145.7 11.2 %all-to-all-start = ((s32[128,32,2,2]{0,3,2,1:T(2,128)}), s32[128,32,2,2]{0,3,2,1:T(2,128)S(1)}, u32[]{:S(2)}, u32[]{:S(2)}) async-start(s32[128,32,2,2]{0,3,2,1:T(2,128)} %broadcast_select_fusion), calls=%async_computation | async-start | bytes 131072 | tf_op jit(solution)/shard_map/all_to_all | solution.py:116
  157.5 1.9 fusion.24
  159.5 80.6 %all-reduce.2 = (f32[64,16]{0,1:T(8,128)}, f32[32,64]{1,0:T(8,128)}, f32[128]{0:T(128)}) all-reduce(f32[64,16]{0,1:T(8,128)S(1)} %fusion.26, f32[32,64]{1,0:T(8,128)S(1)} %fusion.24, f32[128]{0:T(128)S(1)} %broadcast_multiply_fusion.3), channel_id=1, replica_groups=mesh['hst'=32,'local'=8] {'hst','local'}, use_global_device_ids=true, to_apply=%region_13.14 | all-reduce | flops 3200 | bytes 25600 | tf_op jit(solution)/shard_map/psum | solution.py:142
  240.1 18.1 %all_gather.6 = s32[32768,2,2]{0,2,1:T(2,128)S(1)} all-gather(s32[4096,2,2]{0,2,1:T(2,128)S(1)} %reshape.96), channel_id=1, replica_groups=mesh['hst'=32,'local'=8] {'local'}, dimensions={0}, use_global_device_ids=true | all-gather | bytes 589824 | tf_op jit(solution)/shard_map/all_gather | solution.py:123
  258.2 247.1 %all-reduce.6.cloned.1.call-done = (f32[1024,512]{1,0:T(8,128)}, f32[512,4096]{1,0:T(8,128)}) async-done(((f32[1024,512]{1,0:T(8,128)}, f32[512,4096]{1,0:T(8,128)}), (f32[1024,512]{1,0:T(8,128)}, f32[512,4096]{1,0:T(8,128)})) %all-reduce.6.cloned.1.call-update) | async-done | bytes 10485776
  508.2 216.6 %while.11 = (s32[]{:T(128)}, f32[4,128,2,128]{3,1,0,2:T(8,128)S(1)}, s32[4]{0:T(128)S(1)}, s32[32768,2,2]{0,2,1:T(2,128)S(1)}, bf16[32768,2,128]{2,0,1:T(8,128)(2,1)}, /*index=5*/s32[]{:T(128)}) while((s32[]{:T(128)}, f32[4,128,2,128]{3,1,0,2:T(8,128)S(1)}, s32[4]{0:T(128)S(1)}, s32[32768,2,2]{0,2,1:T(2,128)S(1)}, ...), condition=%wide.region_10.11_spmd.clone, body=%wide.region_8.0_spmd.clone.sunk | while | flops 2197946368 | bytes 85590104 | solution.py:89
  509.6 35.3 %convert_reduce_fusion.2 = s32[32768,2,128]{2,0,1:T(8,128)} fusion(s32[32768,2,2]{0,2,1:T(2,128)S(1)} %broadcast_subtract_fusion.2), kind=kLoop, calls=%fused_computation.3.clone.1 | loop fusion | flops 41943040 | bytes 34078720 | tf_op jit(solution)/shard_map/while/body/eval_jaxpr/reduce_sum | solution.py:82
  545.0 17.4 %fusion.74 = f32[4,128,2,128]{3,1,0,2:T(8,128)S(1)} fusion(f32[4,128,2,128]{3,1,0,2:T(8,128)S(1)} %get-tuple-element.116, s32[]{:T(128)} %get-tuple-element.115, bf16[32768,2,128]{2,0,1:T(8,128)(2,1)} %get-tuple-element.125, s32[32768,2,128]{2,0,1:T(8,128)} %convert_reduce_fusion.2), kind=kOutput, calls=%fused_computation.7.clone.1 | convolution fusion | flops 2155872256 | bytes 50462724 | tf_op jit(solution)/shard_map/while/body/eval_jaxpr/itz,itn->ztn/dot_general | solution.py:85
  563.8 35.3 %convert_reduce_fusion.2 = s32[32768,2,128]{2,0,1:T(8,128)} fusion(s32[32768,2,2]{0,2,1:T(2,128)S(1)} %broadcast_subtract_fusion.2), kind=kLoop, calls=%fused_computation.3.clone.1 | loop fusion | flops 41943040 | bytes 34078720 | tf_op jit(solution)/shard_map/while/body/eval_jaxpr/reduce_sum | solution.py:82
  599.1 17.4 %fusion.74 = f32[4,128,2,128]{3,1,0,2:T(8,128)S(1)} fusion(f32[4,128,2,128]{3,1,0,2:T(8,128)S(1)} %get-tuple-element.116, s32[]{:T(128)} %get-tuple-element.115, bf16[32768,2,128]{2,0,1:T(8,128)(2,1)} %get-tuple-element.125, s32[32768,2,128]{2,0,1:T(8,128)} %convert_reduce_fusion.2), kind=kOutput, calls=%fused_computation.7.clone.1 | convolution fusion | flops 2155872256 | bytes 50462724 | tf_op jit(solution)/shard_map/while/body/eval_jaxpr/itz,itn->ztn/dot_general | solution.py:85
  617.9 35.3 %convert_reduce_fusion.2 = s32[32768,2,128]{2,0,1:T(8,128)} fusion(s32[32768,2,2]{0,2,1:T(2,128)S(1)} %broadcast_subtract_fusion.2), kind=kLoop, calls=%fused_computation.3.clone.1 | loop fusion | flops 41943040 | bytes 34078720 | tf_op jit(solution)/shard_map/while/body/eval_jaxpr/reduce_sum | solution.py:82
  653.3 17.4 %fusion.74 = f32[4,128,2,128]{3,1,0,2:T(8,128)S(1)} fusion(f32[4,128,2,128]{3,1,0,2:T(8,128)S(1)} %get-tuple-element.116, s32[]{:T(128)} %get-tuple-element.115, bf16[32768,2,128]{2,0,1:T(8,128)(2,1)} %get-tuple-element.125, s32[32768,2,128]{2,0,1:T(8,128)} %convert_reduce_fusion.2), kind=kOutput, calls=%fused_computation.7.clone.1 | convolution fusion | flops 2155872256 | bytes 50462724 | tf_op jit(solution)/shard_map/while/body/eval_jaxpr/itz,itn->ztn/dot_general | solution.py:85
  672.1 35.3 %convert_reduce_fusion.2 = s32[32768,2,128]{2,0,1:T(8,128)} fusion(s32[32768,2,2]{0,2,1:T(2,128)S(1)} %broadcast_subtract_fusion.2), kind=kLoop, calls=%fused_computation.3.clone.1 | loop fusion | flops 41943040 | bytes 34078720 | tf_op jit(solution)/shard_map/while/body/eval_jaxpr/reduce_sum | solution.py:82
  707.4 17.4 %fusion.74 = f32[4,128,2,128]{3,1,0,2:T(8,128)S(1)} fusion(f32[4,128,2,128]{3,1,0,2:T(8,128)S(1)} %get-tuple-element.116, s32[]{:T(128)} %get-tuple-element.115, bf16[32768,2,128]{2,0,1:T(8,128)(2,1)} %get-tuple-element.125, s32[32768,2,128]{2,0,1:T(8,128)} %convert_reduce_fusion.2), kind=kOutput, calls=%fused_computation.7.clone.1 | convolution fusion | flops 2155872256 | bytes 50462724 | tf_op jit(solution)/shard_map/while/body/eval_jaxpr/itz,itn->ztn/dot_general | solution.py:85
  (85 shorter events, 20.6 us)
Async XLA Ops:
  8.0 9.5 %copy-start = (bf16[1024,512]{1,0:T(8,128)(2,1)S(1)}, bf16[1024,512]{1,0:T(8,128)(2,1)}, u32[]{:S(2)}) copy-start(bf16[1024,512]{1,0:T(8,128)(2,1)} %param.14) | copy-start | bytes 3145732
  8.0 497.3 %all-reduce.6.cloned.1.call-start = ((), (), s32[]{:S(2)}) async-start(), calls=%async_computation.3 | async-start | bytes 20971520
  10.1 0.8 copy-start.10
  16.7 0.8 copy-start.7
  17.8 3.5 copy-start.4
  17.8 3.5 copy-start.13
  22.9 8.6 %copy-start.3 = (f32[128,64,128]{2,1,0:T(8,128)}, f32[128,64,128]{2,1,0:T(8,128)S(1)}, u32[]{:S(2)}) copy-start(f32[128,64,128]{2,1,0:T(8,128)S(1)} %get-tuple-element.72) | copy-start | bytes 12582916
  22.9 3.1 copy-start.5
  22.9 3.1 copy-start.15
  31.5 6.4 copy-start.12
  36.5 1.3 copy-start.6
  39.5 4.6 copy-start.8
  46.0 462.3 %all-gather.2.cloned.1.call-start = ((), (), s32[]{:S(2)}) async-start(), calls=%async_computation.2 | async-start | bytes 18874368 | tf_op jit(solution)/shard_map/all_gather | solution.py:122
  46.2 5.7 copy-start.9
  51.9 3.5 copy-start.11
  53.6 5.6 copy-start.14
  53.6 5.6 copy-start.16
  53.6 5.6 copy-start.17
  142.5 1.8 copy-start.2
  145.0 14.5 %copy-start.18 = (f32[128]{0:T(128)S(1)}, f32[128]{0:T(128)}, u32[]{:S(2)}) copy-start(f32[128]{0:T(128)} %get-tuple-element.51) | copy-start | bytes 1540
  145.7 94.4 %all-to-all-start = ((s32[128,32,2,2]{0,3,2,1:T(2,128)}), s32[128,32,2,2]{0,3,2,1:T(2,128)S(1)}, u32[]{:S(2)}, u32[]{:S(2)}) async-start(s32[128,32,2,2]{0,3,2,1:T(2,128)} %broadcast_select_fusion), calls=%async_computation | async-start | bytes 131072 | tf_op jit(solution)/shard_map/all_to_all | solution.py:116
  724.8 0.8 copy-start.19
  724.8 1.4 copy-start.1
Sparse Core Ops, SparseCore 0:
  46.1 459.2 all-reduce.5
Sparse Core Ops, SparseCore 1:
  144.2 183.2 all-gather.1
where the time goes:
time: 736 us; the launch traced here: 734 us
  waiting for transfers between devices  247 us (34%)
  blocking collectives  168 us (23%)
  other arithmetic  162 us (22%)
  matrix products  110 us (15%)
  local copies, waits for them, and re-layouts  18.8 us (3%)
  between operations  15.9 us (2%)
  starting transfers between devices  11.4 us (2%)
    unnamed x3, waiting for transfers between devices  247 us
    reduce_sum x4, other arithmetic, one_offset(): jnp.sum((shifted[..., None] == columns).astype(jnp.int32), axis=2)  141 us
    psum x1, blocking collectives, shards(): lax.psum((small_terms[0] * grad_scale, small_terms[1] * grad_scale, small...  80.6 us
    all_to_all x1, blocking collectives, shards(): lax.all_to_all(ordered, 'hst', split_axis=1, concat_axis=0, tiled=True)  69.7 us
    dot_general x4, matrix products, one_offset(): jnp.einsum('itz,itn->ztn', member_matches, gradient_list, preferred_eleme...  69.5 us
    dot_general x14, matrix products, product(): return jnp.einsum(form, left, right, preferred_element_type=jnp.float32)  30.7 us
    all_gather x1, blocking collectives, shards(): lax.all_gather(bag_rows, 'local', axis=0, tiled=True)  18.1 us
  transfers between devices with their start and end apart: 3, of which 1 were waited for; matrix products, arithmetic and copies ran while one was open for 5% of the time, Pallas kernels for 0%

commit v1 on v0

v1 whole, which is shorter than its diff:
```python
import functools

import jax
import jax.numpy as jnp
from jax import lax
from jax.experimental import pallas as pl
from jax.experimental.pallas import tpu as pltpu
from jax.sharding import Mesh
from jax.sharding import PartitionSpec as P

BF, F32 = jnp.bfloat16, jnp.float32

def dot_nn(a, b):
    return lax.dot_general(a, b, (((1,), (0,)), ((), ())), preferred_element_type=F32)
def dot_nt(a, b):
    return lax.dot_general(a, b, (((1,), (1,)), ((), ())), preferred_element_type=F32)
def dot_tn(a, b):
    return lax.dot_general(a, b, (((0,), (0,)), ((), ())), preferred_element_type=F32)

def out_norm(summed, cot, gain):
    centered = summed - jnp.mean(summed, axis=-1, keepdims=True)
    inverse = lax.rsqrt(jnp.mean(centered * centered, axis=-1, keepdims=True) + 1e-5)
    normed = centered * inverse
    cn = cot * normed
    dnorm = cot * gain
    first = jnp.mean(dnorm, axis=-1, keepdims=True)
    second = jnp.mean(cn * gain, axis=-1, keepdims=True)
    return inverse * (dnorm - first - normed * second), cn

def fold8(v):
    return jnp.sum(v.reshape(v.shape[0] // 8, 8, 128), axis=0)

def fb_kernel(scale, b, fm_ref, pooled_ref, cot_ref, projt_ref, wup_ref, wdown_ref, wc_ref, gain_ref,
              bags_ref, w_ref,
              pf, cf, ds, it, gus, gsmall_ref, ggain_ref, nb_s, dpre_s, hid_s, dfm_s):
    step = pl.program_id(0)
    nsteps = pl.num_programs(0)
    rows = pl.ds(pl.multiple_of(step * b, b), b)
    x = pooled_ref[...]
    pf[...] = x.astype(F32).reshape(b * 64, 128)
    cf[...] = cot_ref[...].astype(F32).reshape(b * 64, 128)
    gain = gain_ref[...]
    projt = projt_ref[...]
    wc = wc_ref[...]
    xcat = jnp.concatenate([x[s] for s in range(b)], axis=1)
    head = dot_nn(jnp.concatenate([projt, wc], axis=0), xcat)
    pts, lcs = [], []
    for s in range(b):
        pts.append(head[0:16, s * 128:(s + 1) * 128].astype(BF))
        lcs.append(head[16:48, s * 128:(s + 1) * 128])
        it[s * 16:(s + 1) * 16, 0:64] = dot_nt(pts[s], x[s])
    inter = jnp.concatenate([it[pl.ds(k, b, stride=16), :][:, 0:64] for k in range(16)], axis=1)
    cen = inter - jnp.mean(inter, axis=1, keepdims=True)
    inv_fm = lax.rsqrt(jnp.mean(cen * cen, axis=1, keepdims=True) + 1e-5)
    normed = cen * inv_fm
    nb = normed.astype(BF)
    nb_s[rows, :] = nb
    preact = dot_nn(nb, wup_ref[...])
    sig = jax.nn.sigmoid(preact)
    hidden = (preact * sig).astype(BF)
    hid_s[rows, :] = hidden
    fm_out = dot_nn(hidden, wdown_ref[...])
    gg = jnp.zeros((8, 128), F32)
    dfms = []
    for m in range(32):
        p_m = pf[pl.ds(m, b, stride=64), :]
        c_m = cf[pl.ds(m, b, stride=64), :]
        dsum, cn = out_norm(fm_out[:, m * 128:(m + 1) * 128] + p_m, c_m, gain)
        gg += fold8(cn)
        ds[pl.ds(m, b, stride=64), :] = dsum
        dfms.append(dsum.astype(BF))
    dlcs = []
    for s in range(b):
        dsum, cn = out_norm(lcs[s] + pf[s * 64 + 32:(s + 1) * 64, :], cf[s * 64 + 32:(s + 1) * 64, :], gain)
        gg += fold8(cn)
        ds[s * 64 + 32:(s + 1) * 64, :] = dsum
        dlcs.append(dsum.astype(BF))
    dfm = jnp.concatenate(dfms, axis=1)
    dfm_s[rows, :] = dfm
    hg = dot_nt(dfm, wdown_ref[...])
    dpre = (hg * sig * (1.0 + preact * (1.0 - sig))).astype(BF)
    dpre_s[rows, :] = dpre
    dnormed = dot_nt(dpre, wup_ref[...])
    first = jnp.mean(dnormed, axis=1, keepdims=True)
    second = jnp.mean(dnormed * normed, axis=1, keepdims=True)
    dinter = (inv_fm * (dnormed - first - normed * second)).astype(BF).astype(F32)
    for k in range(16):
        it[pl.ds(k, b, stride=16), 0:64] = dinter[:, k * 64:(k + 1) * 64]
    tails = []
    for s in range(b):
        dit = it[s * 16:(s + 1) * 16, 0:64].astype(BF)
        dprojt = dot_nn(dit, x[s]).astype(BF)
        tails.append(jnp.concatenate([dlcs[s], dprojt], axis=0))
        left = jnp.concatenate([wc, projt, dit], axis=0)
        right = jnp.concatenate([tails[s], pts[s]], axis=0)
        ds[s * 64:(s + 1) * 64, :] += dot_tn(left, right)
    gsm = dot_nt(jnp.concatenate(tails, axis=1), xcat)
    for j in range(64):
        bags_ref[j, :, :] = ds[pl.ds(fm_ref[j], b, stride=64), :].astype(BF)

    @pl.when(step == 0)
    def _():
        gsmall_ref[...] = gsm
        ggain_ref[...] = gg

    @pl.when(step > 0)
    def _():
        gsmall_ref[...] += gsm
        ggain_ref[...] += gg

    @pl.when(step == nsteps - 1)
    def _():
        for k in range(16):
            part = dot_tn(nb_s[:, k * 64:(k + 1) * 64], dpre_s[...]) * scale
            for q in range(4):
                gus[pl.ds(q * 1024 + k, 64, stride=16), :] = part[:, q * 128:(q + 1) * 128]
        tail = jnp.concatenate([
            jnp.concatenate([gsmall_ref[...], jnp.zeros((48, 64), F32)], axis=1),
            jnp.broadcast_to(jnp.sum(ggain_ref[...], axis=0, keepdims=True), (8, 128)),
            jnp.zeros((8, 128), F32)], axis=0) * scale
        tail = jnp.concatenate([tail[q * 16:(q + 1) * 16, :] for q in range(4)], axis=1).astype(BF)
        for g in range(16):
            for q in range(4):
                w_ref[g, 0:64, q * 128:(q + 1) * 128] = gus[pl.ds(q * 1024 + g * 64, 64), :].astype(BF)
            w_ref[g, 320:336, :] = tail
        for q in range(8):
            part = (dot_tn(hid_s[...], dfm_s[:, q * 512:(q + 1) * 512]) * scale).astype(BF)
            for g in range(16):
                w_ref[g, 64 + q * 32:96 + q * 32, :] = part[g * 32:(g + 1) * 32, :]


def interaction(pooled, cotangent, projection, w_up, w_down, w_compress, ln_gain, feature_map, scale, b=32):
    batch = pooled.shape[0]
    wup = w_up.reshape(64, 16, 512).transpose(1, 0, 2).reshape(1024, 512)
    full = lambda *sh: pl.BlockSpec(sh, lambda i: (0,) * len(sh))
    return pl.pallas_call(
        functools.partial(fb_kernel, scale, b),
        grid=(batch // b,),
        in_specs=[pl.BlockSpec(memory_space=pltpu.SMEM),
                  pl.BlockSpec((b, 64, 128), lambda i: (i, 0, 0)),
                  pl.BlockSpec((b, 64, 128), lambda i: (i, 0, 0)),
                  full(16, 64), full(1024, 512), full(512, 4096), full(32, 64), full(1, 128)],
        out_specs=[pl.BlockSpec((64, b, 128), lambda i: (0, i, 0)),
                   full(16, 336, 512)],
        out_shape=[jax.ShapeDtypeStruct((64, batch, 128), BF),
                   jax.ShapeDtypeStruct((16, 336, 512), BF)],
        scratch_shapes=[pltpu.VMEM((b * 64, 128), F32), pltpu.VMEM((b * 64, 128), F32), pltpu.VMEM((b * 64, 128), F32),
                        pltpu.VMEM((b * 16, 128), F32), pltpu.VMEM((4096, 128), F32),
                        pltpu.VMEM((48, 64), F32), pltpu.VMEM((8, 128), F32),
                        pltpu.VMEM((batch, 1024), BF), pltpu.VMEM((batch, 512), BF),
                        pltpu.VMEM((batch, 512), BF), pltpu.VMEM((batch, 4096), BF)],
        compiler_params=pltpu.CompilerParams(vmem_limit_bytes=56 << 20),
        name="interaction",
    )(feature_map, pooled, cotangent, projection.T, wup, w_down, w_compress, ln_gain.reshape(1, 128))

def table_kernel(mode, src_blk, ids_ref, bags_ref, out_ref, acc):
    step = pl.program_id(1)
    LO, HI = 4, 1024
    ids = ids_ref[:, 0].reshape(src_blk * 2, 128)
    lo = lax.shift_right_logical(ids, 10)
    hi = jnp.bitwise_and(ids, HI - 1)
    cols = jnp.transpose(lo.astype(jnp.float32), (1, 0))
    a_parts, b_parts = [], []
    if mode == "i16":
        iota = lax.broadcasted_iota(jnp.int16, (HI, 128), 0)
        hi16 = hi.astype(jnp.int16)
    else:
        iota = lax.broadcasted_iota(jnp.int32, (HI, 128), 0)
    for i in range(src_blk):
        v = bags_ref[i, 0]
        for t in range(2):
            r = 2 * i + t
            if mode == "i16":
                a = jnp.where(iota == hi16[r:r + 1, :], jnp.bfloat16(1), jnp.bfloat16(0))
            else:
                a = (iota == hi[r:r + 1, :]).astype(jnp.bfloat16)
            a_parts.append(a)
            c = jnp.broadcast_to(cols[:, r:r + 1], (128, 128)).astype(jnp.bfloat16)
            b_parts.append(jnp.concatenate(
                [jnp.where(c == jnp.bfloat16(q), v, jnp.bfloat16(0)) for q in range(LO)], axis=1))
    a = jnp.concatenate(a_parts, axis=1)
    b = jnp.concatenate(b_parts, axis=0)
    part = jnp.dot(a, b, preferred_element_type=jnp.float32)
    @pl.when(step == 0)
    def _():
        acc[...] = part
    @pl.when(step > 0)
    def _():
        acc[...] += part
    @pl.when(step == pl.num_programs(1) - 1)
    def _():
        for q in range(LO):
            out_ref[0, q * HI:(q + 1) * HI, :] = acc[:, q * 128:(q + 1) * 128].astype(out_ref.dtype)

def table_call(ids, bags, mode="i16", src_blk=8, dt=jnp.bfloat16):
    n = bags.shape[0]
    return pl.pallas_call(
        functools.partial(table_kernel, mode, src_blk),
        grid=(2, n // src_blk),
        in_specs=[pl.BlockSpec((src_blk, 1, 2, 128), lambda j, i: (i, j, 0, 0)),
                  pl.BlockSpec((src_blk, 1, 128, 128), lambda j, i: (i, j, 0, 0))],
        out_specs=pl.BlockSpec((1, 4096, 128), lambda j, i: (j, 0, 0)),
        out_shape=jax.ShapeDtypeStruct((2, 4096, 128), dt),
        scratch_shapes=[pltpu.VMEM((1024, 512), jnp.float32)],
        compiler_params=pltpu.CompilerParams(vmem_limit_bytes=48 << 20),
        name="table_" + mode + str(src_blk),
    )(ids, bags)

AXES = ("y", "zh", "x", "zl", "c")
HST = ("y", "zh", "x")
LOCAL = ("zl", "c")
SIZES = (4, 2, 4, 4, 2)


def weight_moves():
    moves = []
    for d in range(256):
        y, zh, x, zl, c = (d // 64, d // 32 % 2, d // 8 % 4, d // 2 % 4, d % 2)
        moves.append((d, ((c * 2 + zh) * 4 + zl) * 16 + y * 4 + x))
    return moves


def shards(pooled, cotangent, projection, w_up, w_down, w_compress, ln_gain, feature_map, bag_row_index):
    batch = pooled.shape[0]
    scale = float(batch * 256) ** (-0.5)
    ids = jnp.take(jnp.transpose(bag_row_index, (1, 2, 0)), feature_map, axis=0)
    ids = lax.all_to_all(ids, ("y", "c", "x"), 0, 0, tiled=True).reshape(32, 2, 2, batch)
    bags, weights = interaction(
        pooled, cotangent, projection, w_up, w_down, w_compress, ln_gain, feature_map, scale)
    halves = lax.all_to_all(weights.reshape(2, 8, 336, 512), "c", 0, 0, tiled=True)
    weights = (halves[0].astype(F32) + halves[1].astype(F32)).astype(BF)
    weights = lax.psum_scatter(weights, ("zh", "zl"), scatter_dimension=0, tiled=True)[0]
    bags = lax.all_to_all(bags, ("y", "c", "x"), 0, 0, tiled=True).reshape(32, 2, batch, 128)
    part = table_call(ids, bags)
    part = lax.psum_scatter(part, ("zl", "zh"), scatter_dimension=1, tiled=True)
    table_grad = lax.ppermute(part, ("zh", "c"), [(0, 0), (1, 2), (2, 1), (3, 3)]).astype(F32)
    pieces = jnp.concatenate(
        [weights[0:64].reshape(16, 4, 512),
         weights[64:320].reshape(8, 16, 2, 512).transpose(1, 0, 2, 3).reshape(16, 16, 512),
         jnp.broadcast_to(weights[320:336], (16, 16, 512))], axis=1)
    pieces = lax.all_to_all(pieces, ("y", "x"), 0, 0, tiled=True)
    total = jnp.sum(pieces.astype(F32), axis=0)
    tail = total[20:36].reshape(16, 4, 128).transpose(1, 0, 2).reshape(64, 128)
    own = lax.ppermute(total[0:20], AXES, weight_moves())
    gd = own[4:20].reshape(8, 2, 512).transpose(1, 0, 2).reshape(2, 4096)
    return (table_grad, own[0:4], gd, tail[32:48, :64].T, tail[:32, :64], tail[48])


def solution(mesh):
    inner = Mesh(mesh.devices.reshape(SIZES), AXES)
    split = P(AXES, None, None)
    return jax.shard_map(
        shards,
        mesh=inner,
        in_specs=(split, split, P(), P(), P(), P(), P(), P(), split),
        out_specs=(P(HST, LOCAL, None), P(AXES, None), P(AXES, None), P(), P(), P()),
        check_vma=False,
    )
```

time: 736 us -> 276 us (0.38)
  other arithmetic: 162 us -> 3.61 us
  waiting for transfers between devices: 247 us -> 94.8 us
  matrix products: 110 us -> 0 us
  blocking collectives: 168 us -> 69.2 us
  Pallas kernels: 0 us -> 63.1 us
  starting transfers between devices: 11.4 us -> 20.6 us
  local copies, waits for them, and re-layouts: 18.8 us -> 10.2 us
    unnamed x3 -> x2, waiting for transfers between devices: 247 us -> 0.03 us
    reduce_sum x8 -> x1, other arithmetic: 153 us -> 0.11 us  [shards(): total = jnp.sum(pieces.astype(F32), axis=0)]
    dot_general x19 -> x0, matrix products: 110 us -> none  [the longest x4 69.5 us: one_offset(): jnp.einsum('itz,itn->ztn', member_matches, gradient_list, preferred_eleme...]
    reduce_scatter x0 -> x2, waiting for transfers between devices: none -> 90.7 us  [the longest x1 90.7 us: shards(): part = lax.psum_scatter(part, ('zl', 'zh'), scatter_dimension=1, tiled=True)]
    psum x1 -> x0, blocking collectives: 80.6 us -> none  [shards(): lax.psum((small_terms[0] * grad_scale, small_terms[1] * grad_scale, small...]
    pallas_call x0 -> x2, Pallas kernels: none -> 63.1 us  [the longest x1 40 us: interaction(): pl.pallas_call(functools.partial(fb_kernel, scale, b), grid=(batch // b,)...]
    ppermute x0 -> x2, starting transfers between devices: none -> 20.5 us  [the longest x1 14.6 us: shards(): lax.ppermute(part, ('zh', 'c'), [(0, 0), (1, 2), (2, 1), (3, 3)])]
    all_gather x1 -> x0, blocking collectives: 18.1 us -> none  [shards(): lax.all_gather(bag_rows, 'local', axis=0, tiled=True)]
  transfers between devices with their start and end apart: 3 -> 4, of which waited for: 1 -> 2; matrix products, arithmetic and copies ran while one was open for 5% -> 3% of each run, Pallas kernels for 0% -> 8%
where the time goes in v1:
time: 276 us
  waiting for transfers between devices  94.8 us (34%)
  blocking collectives  69.2 us (25%)
  Pallas kernels  63.1 us (23%)
  starting transfers between devices  20.6 us (7%)
  between operations  14.2 us (5%)
  local copies, waits for them, and re-layouts  10.2 us (4%)
  other arithmetic  3.61 us (1%)
    reduce_scatter x1, waiting for transfers between devices, shards(): part = lax.psum_scatter(part, ('zl', 'zh'), scatter_dimension=1, tiled=True)  90.7 us
    pallas_call x1, Pallas kernels, interaction(): pl.pallas_call(functools.partial(fb_kernel, scale, b), grid=(batch // b,)...  40 us
    all_to_all x1, blocking collectives, shards(): lax.all_to_all(bags, ('y', 'c', 'x'), 0, 0, tiled=True)  32.1 us
    pallas_call x1, Pallas kernels, table_call(): pl.pallas_call(functools.partial(table_kernel, mode, src_blk), grid=(2, n...  23.1 us
    ppermute x1, starting transfers between devices, shards(): lax.ppermute(part, ('zh', 'c'), [(0, 0), (1, 2), (2, 1), (3, 3)])  14.6 us
    all_to_all x1, blocking collectives, shards(): pieces = lax.all_to_all(pieces, ('y', 'x'), 0, 0, tiled=True)  14.5 us
    all_to_all x1, blocking collectives, shards(): lax.all_to_all(ids, ('y', 'c', 'x'), 0, 0, tiled=True)  12.7 us
    all_to_all x1, blocking collectives, shards(): lax.all_to_all(weights.reshape(2, 8, 336, 512), 'c', 0, 0, tiled=True)  9.91 us
  transfers between devices with their start and end apart: 4, of which 2 were waited for; matrix products, arithmetic and copies ran while one was open for 3% of the time, Pallas kernels for 8%

profile of v1, /device:TPU:7, one launch (start us, length us, event | category | flops | bytes accessed | tf_op | source)
XLA Modules:
  0.0 275.6 jit_solution(10508496685628683223)
XLA Ops:
  7.2 0.0 reduce-scatter.5.cloned.1.call-start
  7.2 2.8 %copy.26 = bf16[64,16,512]{2,0,1:T(8,128)(2,1)} copy(bf16[64,16,512]{2,1,0:T(8,128)(2,1)} %bitcast.38) | data formatting | bytes 2097152 | tf_op jit(solution)/shard_map/reshape | solution.py:134
  10.1 40.0 %interaction.1 = (bf16[64,128,128]{2,1,0:T(8,128)(2,1)}, bf16[16,336,512]{2,1,0:T(8,128)(2,1)}) custom-call(s32[64]{0:T(128)} %fm_ref.1, bf16[128,64,128]{2,1,0:T(8,128)(2,1)} %pooled_ref.1, bf16[128,64,128]{2,1,0:T(8,128)(2,1)} %cot_ref.1, bf16[16,64]{1,0:T(8,128)(2,1)} %bitcast.46, bf16[1024,512]{1,0:T(8,128)(2,1)} %bitcast.37, ...), custom_call_target="tpu_custom_call" | custom-call | tf_op jit(solution)/shard_map/interaction/pallas_call | solution.py:136
  50.1 9.9 %all_to_all.20 = bf16[2,8,336,512]{3,2,1,0:T(8,128)(2,1)S(1)} all-to-all(bf16[2,8,336,512]{3,2,1,0:T(8,128)(2,1)} %bitcast.36), channel_id=1, replica_groups=mesh['y'=4,'zh'=2,'x'=4,'zl'=4,'c'=2] {'c'}, dimensions={0} | all-to-all | bytes 11010048 | tf_op jit(solution)/shard_map/all_to_all | solution.py:230
  60.0 2.5 fusion
  62.5 0.0 reduce-scatter.5.cloned.1.call-update
  62.5 0.0 reduce-scatter.3.cloned.1.call-start
  62.5 0.6 copy-done.2
  63.1 0.7 gather_fusion
  63.8 0.1 broadcast_select_fusion
  64.0 12.7 %all_to_all.21 = s32[64,2,128]{2,1,0:T(2,128)S(1)} all-to-all(s32[64,2,128]{2,1,0:T(2,128)S(1)} %broadcast_select_fusion), channel_id=1, replica_groups=mesh['y'=4,'zh'=2,'x'=4,'zl'=4,'c'=2] {'y','c','x'}, dimensions={0} | all-to-all | bytes 131072 | tf_op jit(solution)/shard_map/all_to_all | solution.py:227
  76.6 32.1 %all_to_all.22 = bf16[64,128,128]{2,1,0:T(8,128)(2,1)S(1)} all-to-all(bf16[64,128,128]{2,1,0:T(8,128)(2,1)S(1)} %copy-done.1), channel_id=1, replica_groups=mesh['y'=4,'zh'=2,'x'=4,'zl'=4,'c'=2] {'y','c','x'}, dimensions={0} | all-to-all | bytes 4194304 | tf_op jit(solution)/shard_map/all_to_all | solution.py:233
  108.8 23.1 %table_i168.1 = bf16[2,4096,128]{2,1,0:T(8,128)(2,1)} custom-call(s32[32,2,2,128]{3,2,1,0:T(2,128)S(1)} %bitcast.35, bf16[32,2,128,128]{3,2,1,0:T(8,128)(2,1)S(1)} %bitcast.34), custom_call_target="tpu_custom_call" | custom-call | tf_op jit(solution)/shard_map/table_i168/pallas_call | solution.py:197
  131.9 0.0 reduce-scatter.5.cloned.1.call-done
  131.9 1.0 slice.59
  132.9 0.1 reshape.72
  133.1 0.8 slice.58
  134.0 0.7 slice_bitcast_fusion.1
  134.7 0.1 pad_maximum_fusion
  134.8 0.3 copy.29
  135.1 14.5 %all_to_all.23 = bf16[16,36,512]{2,1,0:T(8,128)(2,1)S(1)} all-to-all(bf16[16,36,512]{2,1,0:T(8,128)(2,1)S(1)} %copy.29), channel_id=1, replica_groups=mesh['y'=4,'zh'=2,'x'=4,'zl'=4,'c'=2] {'y','x'}, dimensions={0} | all-to-all | bytes 1179648 | tf_op jit(solution)/shard_map/all_to_all | solution.py:241
  149.6 0.1 convert_reduce_fusion
  149.7 5.8 %collective-permute-start.1 = (f32[20,512]{1,0:T(8,128)S(1)}, f32[20,512]{1,0:T(8,128)S(1)}, u32[]{:S(2)}, u32[]{:S(2)}) collective-permute-start(f32[20,512]{1,0:T(8,128)S(1)} %slice.61), channel_id=1, source_target_pairs={{0,0},{1,128},{2,16},{3,144},{4,32},{5,160},{6,48},{7,176},{8,1},{... | collective-permute-start | bytes 122888 | tf_op jit(solution)/shard_map/ppermute | solution.py:244
  155.6 90.7 %reduce-scatter.3.cloned.1.call-done = bf16[2,512,128]{2,1,0:T(8,128)(2,1)} async-done(((bf16[2,4096,128]{2,1,0:T(8,128)(2,1)}), bf16[2,512,128]{2,1,0:T(8,128)(2,1)}) %reduce-scatter.3.cloned.1.call-update) | async-done | bytes 262160 | tf_op jit(solution)/shard_map/reduce_scatter | solution.py:235
  246.3 14.6 %collective-permute-start = (bf16[2,512,128]{2,1,0:T(8,128)(2,1)}, bf16[2,512,128]{2,1,0:T(8,128)(2,1)S(1)}, u32[]{:S(2)}, u32[]{:S(2)}) collective-permute-start(bf16[2,512,128]{2,1,0:T(8,128)(2,1)} %reduce-scatter.3.cloned.1.call-done), channel_id=1, source_target_pairs={{0,0},{1,32},{32,1},{33,33},{2,2},{3,34},{34,3},{35,35},{4,4},{5,3... | collective-permute-start | bytes 786440 | tf_op jit(solution)/shard_map/ppermute | solution.py:236
  260.9 0.6 slice_bitcast_fusion.2
  261.5 0.5 slice_bitcast_fusion.3
  262.0 0.6 slice.66
  262.7 0.6 copy.33
  263.3 0.6 slice.62
  263.9 4.0 %collective-permute-done = bf16[2,512,128]{2,1,0:T(8,128)(2,1)S(1)} collective-permute-done((bf16[2,512,128]{2,1,0:T(8,128)(2,1)}, bf16[2,512,128]{2,1,0:T(8,128)(2,1)S(1)}, u32[]{:S(2)}, u32[]{:S(2)}) %collective-permute-start) | collective-permute-done | bytes 262176 | tf_op jit(solution)/shard_map/ppermute | solution.py:236
  268.0 0.8 convert_element_type.20
  (19 shorter events, 0.2 us)
Async XLA Ops:
  7.2 56.0 %copy-start = (s32[128,64,2]{0,2,1:T(2,128)S(1)}, s32[128,64,2]{0,2,1:T(2,128)}, u32[]{:S(2)}) copy-start(s32[128,64,2]{0,2,1:T(2,128)} %param.17) | copy-start | bytes 196612
  7.2 124.8 %reduce-scatter.5.cloned.1.call-start = ((), (), s32[]{:S(2)}) async-start(), calls=%async_computation.7 | async-start | bytes 3096576 | tf_op jit(solution)/shard_map/reduce_scatter | solution.py:232
  62.5 0.7 copy-start.2
  62.5 14.2 %copy-start.1 = (bf16[64,128,128]{2,1,0:T(8,128)(2,1)S(1)}, bf16[64,128,128]{2,1,0:T(8,128)(2,1)}, u32[]{:S(2)}) copy-start(bf16[64,128,128]{2,1,0:T(8,128)(2,1)} %get-tuple-element.8) | copy-start | bytes 6291460
  62.5 183.8 %reduce-scatter.3.cloned.1.call-start = ((), (), s32[]{:S(2)}) async-start(), calls=%async_computation.6 | async-start | bytes 2359296 | tf_op jit(solution)/shard_map/reduce_scatter | solution.py:235
  149.7 112.9 %collective-permute-start.1 = (f32[20,512]{1,0:T(8,128)S(1)}, f32[20,512]{1,0:T(8,128)S(1)}, u32[]{:S(2)}, u32[]{:S(2)}) collective-permute-start(f32[20,512]{1,0:T(8,128)S(1)} %slice.61), channel_id=1, source_target_pairs={{0,0},{1,128},{2,16},{3,144},{4,32},{5,160},{6,48},{7,176},{8,1},{... | collective-permute-start | bytes 122888 | tf_op jit(solution)/shard_map/ppermute | solution.py:244
  246.3 21.7 %collective-permute-start = (bf16[2,512,128]{2,1,0:T(8,128)(2,1)}, bf16[2,512,128]{2,1,0:T(8,128)(2,1)S(1)}, u32[]{:S(2)}, u32[]{:S(2)}) collective-permute-start(bf16[2,512,128]{2,1,0:T(8,128)(2,1)} %reduce-scatter.3.cloned.1.call-done), channel_id=1, source_target_pairs={{0,0},{1,32},{32,1},{33,33},{2,2},{3,34},{34,3},{35,35},{4,4},{5,3... | collective-permute-start | bytes 786440 | tf_op jit(solution)/shard_map/ppermute | solution.py:236
Sparse Core Ops, SparseCore 0:
  62.6 43.4 reduce-scatter.4
  132.0 114.1 reduce-scatter.2

commit v2 on v1

v2 whole, which is shorter than its diff:
```python
import functools

import jax
import jax.numpy as jnp
from jax import lax
from jax.experimental import pallas as pl
from jax.experimental.pallas import tpu as pltpu
from jax.sharding import Mesh
from jax.sharding import PartitionSpec as P

BF, F32 = jnp.bfloat16, jnp.float32


def dot_nn(a, b):
    return lax.dot_general(a, b, (((1,), (0,)), ((), ())), preferred_element_type=F32)


def dot_nt(a, b):
    return lax.dot_general(a, b, (((1,), (1,)), ((), ())), preferred_element_type=F32)


def dot_tn(a, b):
    return lax.dot_general(a, b, (((0,), (0,)), ((), ())), preferred_element_type=F32)


def out_norm(summed, cot, gain):
    centered = summed - jnp.mean(summed, axis=-1, keepdims=True)
    inverse = lax.rsqrt(jnp.mean(centered * centered, axis=-1, keepdims=True) + 1e-5)
    normed = centered * inverse
    cot_normed = cot * normed
    dnorm = cot * gain
    first = jnp.mean(dnorm, axis=-1, keepdims=True)
    second = jnp.mean(cot_normed * gain, axis=-1, keepdims=True)
    return inverse * (dnorm - first - normed * second), cot_normed


def fold8(v):
    return jnp.sum(v.reshape(v.shape[0] // 8, 8, 128), axis=0)


def layer_kernel(scale, b, fm_ref, pooled_ref, cot_ref, proj_ref, wup_ref, wdown_ref, wc_ref, gain_ref,
                 bags_ref, acts_ref, tail_ref, inv_ref, ds1, ds2, wups, wupr):
    for j in range(64):
        inv_ref[fm_ref[j]] = j
    for q in range(4):
        wups[...] = wup_ref[:, q * 128:(q + 1) * 128].astype(F32)
        for k in range(16):
            wupr[k * 64:(k + 1) * 64, q * 128:(q + 1) * 128] = wups[pl.ds(k, 64, stride=16), :].astype(BF)
    x = pooled_ref[...]
    gain = gain_ref[...]
    proj = proj_ref[...]
    wc = wc_ref[...]
    projt = jnp.transpose(proj.astype(F32)).astype(BF)
    consts = jnp.concatenate([jnp.transpose(wc.astype(F32)).astype(BF), proj], axis=1)
    xcat = jnp.concatenate([x[s] for s in range(b)], axis=1)
    head = dot_nn(jnp.concatenate([projt, wc], axis=0), xcat)
    pts = [head[0:16, s * 128:(s + 1) * 128].astype(BF) for s in range(b)]
    inter = jnp.stack([dot_nt(pts[s], x[s]) for s in range(b)], axis=0)
    inter = jnp.swapaxes(inter, 0, 1)
    inter = jnp.concatenate([inter[k] for k in range(16)], axis=1)
    cen = inter - jnp.mean(inter, axis=1, keepdims=True)
    inv_fm = lax.rsqrt(jnp.mean(cen * cen, axis=1, keepdims=True) + 1e-5)
    normed = cen * inv_fm
    nb = normed.astype(BF)
    preact = dot_nn(nb, wupr[...])
    sig = jax.nn.sigmoid(preact)
    hidden = (preact * sig).astype(BF)
    fm_out = dot_nn(hidden, wdown_ref[...])
    gg = jnp.zeros((8, 128), F32)
    dfms = []
    for m in range(32):
        if m % 16 == 0:
            xf = jnp.swapaxes(pooled_ref[:, m:m + 16, :], 0, 1)
            cf = jnp.swapaxes(cot_ref[:, m:m + 16, :], 0, 1)
        dsum, cot_normed = out_norm(
            fm_out[:, m * 128:(m + 1) * 128] + xf[m % 16].astype(F32), cf[m % 16].astype(F32), gain)
        gg += fold8(cot_normed)
        ds1[m] = dsum
        dfms.append(dsum.astype(BF))
    dlcs = []
    for s in range(b):
        dsum, cot_normed = out_norm(
            head[16:48, s * 128:(s + 1) * 128] + x[s, 32:64].astype(F32), cot_ref[s, 32:64, :].astype(F32), gain)
        gg += fold8(cot_normed)
        ds2[s] = dsum
        dlcs.append(dsum.astype(BF))
    dfm = jnp.concatenate(dfms, axis=1)
    hg = dot_nt(dfm, wdown_ref[...])
    dpre = (hg * sig * (1.0 + preact * (1.0 - sig))).astype(BF)
    for h in range(2):
        acts_ref[h, :, 0:512] = nb[:, h * 512:(h + 1) * 512]
        acts_ref[h, :, 512:1024] = dpre
        acts_ref[h, :, 1024:1280] = hidden[:, h * 256:(h + 1) * 256]
        acts_ref[h, :, 1280:5376] = dfm
    dnormed = dot_nt(dpre, wupr[...])
    first = jnp.mean(dnormed, axis=1, keepdims=True)
    second = jnp.mean(dnormed * normed, axis=1, keepdims=True)
    dinter = (inv_fm * (dnormed - first - normed * second)).astype(BF).astype(F32)
    dinter = jnp.swapaxes(jnp.stack([dinter[:, k * 64:(k + 1) * 64] for k in range(16)], axis=0), 0, 1)
    zero = jnp.zeros((16, 128), BF)
    tails = []
    for g in range(b // 16):
        outs = []
        for half in range(2):
            group = [g * 16 + half * 8 + i for i in range(8)]
            for s in group:
                dproj = dot_nn(dinter[s].astype(BF), x[s]).astype(BF)
                tails.append(jnp.concatenate([dlcs[s], dproj], axis=0))
            block = dinter[group[0]:group[0] + 8].reshape(128, 64)
            left = jnp.concatenate([jnp.transpose(block).astype(BF), consts], axis=1)
            right = jnp.concatenate(
                [jnp.concatenate([pts[s] if i == r else zero for i, s in enumerate(group)], axis=1) for r in range(8)]
                + [jnp.concatenate([tails[s] for s in group], axis=1)], axis=0)
            res = dot_nn(left, right)
            outs += [res[:, i * 128:(i + 1) * 128] for i in range(8)]
        for n in range(8):
            rows = [v[n * 8:(n + 1) * 8] for v in outs]
            if n >= 4:
                rows = [v + ds2[g * 16 + i, (n - 4) * 8:(n - 3) * 8, :] for i, v in enumerate(rows)]
            turned = jnp.swapaxes(jnp.stack(rows, axis=0), 0, 1)
            for i in range(8):
                v = turned[i]
                if n < 4:
                    v = v + ds1[n * 8 + i, g * 16:(g + 1) * 16, :]
                bags_ref[inv_ref[n * 8 + i], g * 16:(g + 1) * 16, :] = v.astype(BF)
    gsm = dot_nt(jnp.concatenate(tails, axis=1), xcat)
    tail_ref[...] = jnp.concatenate([
        jnp.concatenate([gsm, jnp.zeros((48, 64), F32)], axis=1),
        jnp.broadcast_to(jnp.sum(gg, axis=0, keepdims=True), (16, 128))], axis=0) * scale


def layer_call(part, batch, feature_map, pooled, cotangent, projection, w_up, w_down, w_compress, gain, scale):
    full = lambda *sh: pl.BlockSpec(sh, lambda i: (0,) * len(sh))
    half = lambda: pl.BlockSpec((batch, 64, 128), lambda i: (part, 0, 0))
    return pl.pallas_call(
        functools.partial(layer_kernel, scale, batch),
        grid=(1,),
        in_specs=[pl.BlockSpec(memory_space=pltpu.SMEM), half(), half(),
                  full(64, 16), full(1024, 512), full(512, 4096), full(32, 64), full(1, 128)],
        out_specs=[full(64, batch, 128), full(2, batch, 5376), full(64, 128)],
        out_shape=[jax.ShapeDtypeStruct((64, batch, 128), BF),
                   jax.ShapeDtypeStruct((2, batch, 5376), BF),
                   jax.ShapeDtypeStruct((64, 128), F32)],
        scratch_shapes=[pltpu.SMEM((64,), jnp.int32),
                        pltpu.VMEM((32, batch, 128), F32), pltpu.VMEM((batch, 32, 128), F32),
                        pltpu.VMEM((1024, 128), F32), pltpu.VMEM((1024, 512), BF)],
        compiler_params=pltpu.CompilerParams(vmem_limit_bytes=50 << 20),
        cost_estimate=pl.CostEstimate(flops=15 * 10**9, bytes_accessed=10 << 20, transcendentals=0),
        name="layer",
    )(feature_map, pooled, cotangent, projection, w_up, w_down, w_compress, gain)


def weight_kernel(scale, acts0_ref, acts1_ref, tail0_ref, tail1_ref, w_ref, gus):
    acts = jnp.concatenate([acts0_ref[0], acts0_ref[1], acts1_ref[0], acts1_ref[1]], axis=0)
    tail = tail0_ref[...] + tail1_ref[...]
    tail = jnp.concatenate([tail[q * 16:(q + 1) * 16, :] for q in range(4)], axis=1).astype(BF)
    up = dot_tn(acts[:, 0:512], acts[:, 512:1024]) * scale
    for q in range(4):
        for k in range(8):
            gus[pl.ds(k, 64, stride=8), :] = up[k * 64:(k + 1) * 64, q * 128:(q + 1) * 128]
        for z in range(16):
            w_ref[z, 0:32, q * 128:(q + 1) * 128] = gus[z * 32:(z + 1) * 32, :].astype(BF)
    hid = acts[:, 1024:1280]
    for q in range(8):
        down = (dot_tn(hid, acts[:, 1280 + q * 512:1792 + q * 512]) * scale).astype(BF)
        for z in range(16):
            w_ref[z, 32 + q * 16:48 + q * 16, :] = down[z * 16:(z + 1) * 16, :]
    for z in range(16):
        w_ref[z, 160:176, :] = tail


def weight_call(acts0, acts1, tail0, tail1, scale):
    return pl.pallas_call(
        functools.partial(weight_kernel, scale),
        out_shape=jax.ShapeDtypeStruct((16, 176, 512), BF),
        scratch_shapes=[pltpu.VMEM((512, 128), F32)],
        compiler_params=pltpu.CompilerParams(vmem_limit_bytes=40 << 20),
        cost_estimate=pl.CostEstimate(flops=5 * 10**9, bytes_accessed=6 << 20, transcendentals=0),
        name="weight_grads",
    )(acts0, acts1, tail0, tail1)


def table_kernel(pairs, last, *refs):
    if last:
        ids_ref, bags_ref, start_ref, out_ref, acc = refs
    else:
        ids_ref, bags_ref, acc = refs
        acc = acc.at[0]
    step = pl.program_id(1)
    ids = ids_ref[:, 0].reshape(pairs * 2, 128)
    low = jnp.transpose(lax.shift_right_logical(ids, 10).astype(F32), (1, 0))
    high = jnp.bitwise_and(ids, 1023).astype(jnp.int16)
    iota = lax.broadcasted_iota(jnp.int16, (1024, 128), 0)
    left, right = [], []
    for i in range(pairs):
        values = bags_ref[i, :, 0].reshape(128, 128)
        for t in range(2):
            r = 2 * i + t
            left.append(jnp.where(iota == high[r:r + 1, :], jnp.bfloat16(1), jnp.bfloat16(0)))
            column = jnp.broadcast_to(low[:, r:r + 1], (128, 128)).astype(BF)
            right.append(jnp.concatenate(
                [jnp.where(column == jnp.bfloat16(q), values, jnp.bfloat16(0)) for q in range(4)], axis=1))
    part = jnp.dot(jnp.concatenate(left, axis=1), jnp.concatenate(right, axis=0), preferred_element_type=F32)

    @pl.when(step == 0)
    def _():
        acc[...] = start_ref[0] + part if last else part

    @pl.when(step > 0)
    def _():
        acc[...] += part

    if last:
        @pl.when(step == pl.num_programs(1) - 1)
        def _():
            for q in range(4):
                for h in range(2):
                    out_ref[h * 4 + q, 0] = acc[h * 512:(h + 1) * 512, q * 128:(q + 1) * 128].astype(BF)


def table_call(ids, bags, start=None, pairs=8):
    last = start is not None
    sums = pl.BlockSpec((1, 1024, 512), lambda j, i: (j, 0, 0))
    return pl.pallas_call(
        functools.partial(table_kernel, pairs, last),
        grid=(2, ids.shape[0] // pairs),
        in_specs=[pl.BlockSpec((pairs, 1, 2, 128), lambda j, i: (i, j, 0, 0)),
                  pl.BlockSpec((pairs, 2, 1, 64, 128), lambda j, i: (i, 0, j, 0, 0))] + ([sums] if last else []),
        out_specs=pl.BlockSpec((8, 1, 512, 128), lambda j, i: (0, j, 0, 0)) if last else sums,
        out_shape=jax.ShapeDtypeStruct((8, 2, 512, 128), BF) if last else jax.ShapeDtypeStruct((2, 1024, 512), F32),
        scratch_shapes=[pltpu.VMEM((1024, 512), F32)] if last else [],
        compiler_params=pltpu.CompilerParams(vmem_limit_bytes=48 << 20),
        cost_estimate=pl.CostEstimate(flops=9 * 10**9, bytes_accessed=5 << 20, transcendentals=0),
        name="table_last" if last else "table_first",
    )(*([ids, bags] + ([start] if last else [])))


AXES = ("y", "zh", "x", "zl", "c")
HST = ("y", "zh", "x")
LOCAL = ("zl", "c")
SIZES = (4, 2, 4, 4, 2)
PLANE = ("y", "c", "x")


def weight_moves():
    up, down = [], []
    for d in range(256):
        y, zh, x, zl, c = (d // 64, d // 32 % 2, d // 8 % 4, d // 2 % 4, d % 2)
        unit = (y * 4 + x) * 8 + zh * 4 + zl
        up.append((d, (unit // 2) * 4 + 2 * c + unit % 2))
        down.append((d, c * 128 + unit))
    return up, down


def shards(pooled, cotangent, projection, w_up, w_down, w_compress, ln_gain, feature_map, bag_row_index):
    batch = pooled.shape[0] // 2
    scale = float(batch * 512) ** (-0.5)
    ids = jnp.take(jnp.transpose(bag_row_index, (1, 2, 0)), feature_map, axis=0)
    ids = lax.all_to_all(ids, PLANE, 0, 0, tiled=True).reshape(16, 2, 2, 2, 2, batch)
    ids = jnp.transpose(ids, (4, 0, 2, 3, 1, 5)).reshape(2, 16, 2, 2, 128)
    bags, acts, tails = [], [], []
    for part in range(2):
        bag, act, tail = layer_call(
            part, batch, feature_map, pooled, cotangent, projection, w_up, w_down, w_compress,
            ln_gain.reshape(1, 128), scale)
        bags.append(lax.all_to_all(bag, PLANE, 0, 0, tiled=True).reshape(16, 2, 2, batch, 128))
        acts.append(lax.all_to_all(act, "c", 0, 0, tiled=True))
        tails.append(tail)
    weights = weight_call(acts[0], acts[1], tails[0], tails[1], scale)
    weights = lax.all_to_all(weights, ("y", "x"), 0, 0, tiled=True)
    sums = table_call(ids[0], bags[0])
    rows = table_call(ids[1], bags[1], sums)
    rows = lax.psum_scatter(rows, ("zh", "zl"), scatter_dimension=0, tiled=True)[0]
    weights = jnp.sum(weights.astype(F32), axis=0).astype(BF)
    pieces = jnp.concatenate(
        [weights[0:32].reshape(8, 4, 512),
         weights[32:160].reshape(8, 8, 2, 512).transpose(1, 0, 2, 3).reshape(8, 16, 512),
         jnp.broadcast_to(weights[160:176], (8, 16, 512))], axis=1)
    pieces = lax.all_to_all(pieces, ("zh", "zl"), 0, 0, tiled=True)
    total = jnp.sum(pieces.astype(F32), axis=0)
    up_moves, down_moves = weight_moves()
    gu = lax.ppermute(total[0:4], AXES, up_moves)
    gd = lax.ppermute(total[4:20], AXES, down_moves).reshape(8, 2, 512).transpose(1, 0, 2).reshape(2, 4096)
    tail = total[20:36].reshape(16, 4, 128).transpose(1, 0, 2).reshape(64, 128)
    tail = tail + lax.ppermute(tail, "c", [(0, 1), (1, 0)])
    small = (tail[32:48, :64].T, tail[:32, :64], tail[48])
    rows, gu, gd, small = lax.optimization_barrier((rows, gu, gd, small))
    table_grad = lax.ppermute(rows, ("zh", "c"), [(0, 0), (1, 2), (2, 1), (3, 3)]).astype(F32)
    return (table_grad, gu, gd) + tuple(small)


def solution(mesh):
    inner = Mesh(mesh.devices.reshape(SIZES), AXES)
    split = P(AXES, None, None)
    return jax.shard_map(
        shards,
        mesh=inner,
        in_specs=(split, split, P(), P(), P(), P(), P(), P(), split),
        out_specs=(P(HST, LOCAL, None), P(AXES, None), P(AXES, None), P(), P(), P()),
        check_vma=False,
    )
```

time: 276 us -> 215 us (0.78)
  waiting for transfers between devices: 94.8 us -> 55.8 us
  blocking collectives: 69.2 us -> 37.5 us
  starting transfers between devices: 20.6 us -> 36.5 us
  Pallas kernels: 63.1 us -> 52.8 us
  local copies, waits for them, and re-layouts: 10.2 us -> 13.5 us
    reduce_scatter x2 -> x1, waiting for transfers between devices: 90.7 us -> 0.01 us  [shards(): lax.psum_scatter(rows, ('zh', 'zl'), scatter_dimension=0, tiled=True)[0]]
    all_to_all x0 -> x4, waiting for transfers between devices: none -> 39.6 us  [the longest x1 25.8 us: shards(): weights = lax.all_to_all(weights, ('y', 'x'), 0, 0, tiled=True)]
    all_to_all x4 -> x3, blocking collectives: 69.2 us -> 37.5 us  [the longest x1 19.2 us: shards(): pieces = lax.all_to_all(pieces, ('zh', 'zl'), 0, 0, tiled=True)]
    all_to_all x0 -> x4, starting transfers between devices: none -> 22.3 us  [the longest x2 12.6 us: shards(): lax.all_to_all(bag, PLANE, 0, 0, tiled=True).reshape(16, 2, 2, batch, 128)]
    ppermute x2 -> x4, waiting for transfers between devices: 4.04 us -> 16.2 us  [the longest x1 12.8 us: shards(): lax.ppermute(rows, ('zh', 'c'), [(0, 0), (1, 2), (2, 1), (3, 3)])]
    pallas_call x2 -> x5, Pallas kernels: 63.1 us -> 52.8 us  [the longest x2 25.6 us: table_call(): pl.pallas_call(functools.partial(table_kernel, pairs, last), grid=(2, ids...]
    unnamed x7 -> x30, local copies, waits for them, and re-layouts: 1.23 us -> 10.4 us
    ppermute x2 -> x4, starting transfers between devices: 20.5 us -> 14.2 us  [the longest x1 4.53 us: shards(): gu = lax.ppermute(total[0:4], AXES, up_moves)]
  transfers between devices with their start and end apart: 4 -> 9, of which waited for: 2 -> 5; matrix products, arithmetic and copies ran while one was open for 3% -> 3% of each run, Pallas kernels for 8% -> 19%
where the time goes in v2:
time: 215 us; the launch traced here: 214 us
  waiting for transfers between devices  55.8 us (26%)
  Pallas kernels  52.8 us (25%)
  blocking collectives  37.5 us (17%)
  starting transfers between devices  36.5 us (17%)
  between operations  14.3 us (7%)
  local copies, waits for them, and re-layouts  13.5 us (6%)
  other arithmetic  3.33 us (2%)
    all_to_all x1, waiting for transfers between devices, shards(): weights = lax.all_to_all(weights, ('y', 'x'), 0, 0, tiled=True)  25.8 us
    pallas_call x2, Pallas kernels, table_call(): pl.pallas_call(functools.partial(table_kernel, pairs, last), grid=(2, ids...  25.6 us
    pallas_call x2, Pallas kernels, layer_call(): pl.pallas_call(functools.partial(layer_kernel, scale, batch), grid=(1,),...  24.5 us
    all_to_all x1, blocking collectives, shards(): pieces = lax.all_to_all(pieces, ('zh', 'zl'), 0, 0, tiled=True)  19.2 us
    all_to_all x2, waiting for transfers between devices, shards(): lax.all_to_all(bag, PLANE, 0, 0, tiled=True).reshape(16, 2, 2, batch, 128)  13.9 us
    all_to_all x1, blocking collectives, shards(): lax.all_to_all(ids, PLANE, 0, 0, tiled=True).reshape(16, 2, 2, 2, 2, batch)  12.8 us
    ppermute x1, waiting for transfers between devices, shards(): lax.ppermute(rows, ('zh', 'c'), [(0, 0), (1, 2), (2, 1), (3, 3)])  12.8 us
    all_to_all x2, starting transfers between devices, shards(): lax.all_to_all(bag, PLANE, 0, 0, tiled=True).reshape(16, 2, 2, batch, 128)  12.6 us
  transfers between devices with their start and end apart: 9, of which 5 were waited for; matrix products, arithmetic and copies ran while one was open for 3% of the time, Pallas kernels for 19%

profile of v2, /device:TPU:7, one launch (start us, length us, event | category | flops | bytes accessed | tf_op | source)
XLA Modules:
  0.0 213.9 jit_solution(5079493564040210523)
XLA Ops:
  7.2 0.8 copy.33.proj_ref
  8.0 1.2 copy-done.4
  9.2 0.7 copy-done.6
  9.9 0.7 copy-done.8
  11.2 12.6 %layer.3 = (bf16[64,64,128]{2,1,0:T(8,128)(2,1)S(1)}, bf16[2,64,5376]{2,1,0:T(8,128)(2,1)}, f32[64,128]{1,0:T(8,128)S(1)}) custom-call(s32[64]{0:T(128)S(1)} %copy-done.10, bf16[128,64,128]{2,1,0:T(8,128)(2,1)} %pooled_ref.3, bf16[128,64,128]{2,1,0:T(8,128)(2,1)} %cot_ref.3, bf16[64,16]{1,0:T(8,128)(2,1)S(1)} %copy.33.proj_ref, ...), custom_call_target="tpu_custom_call" | custom-call | flops 15000000512 | bytes 10485760 | tf_op jit(solution)/shard_map/layer/pallas_call | solution.py:135
  23.9 1.0 copy-done.3
  24.8 4.4 %all-to-all-start.3 = ((bf16[2,64,5376]{2,1,0:T(8,128)(2,1)}), bf16[2,64,5376]{2,1,0:T(8,128)(2,1)S(1)}, u32[]{:S(2)}, u32[]{:S(2)}) async-start(bf16[2,64,5376]{2,1,0:T(8,128)(2,1)} %get-tuple-element.20), calls=%async_computation.4 | async-start | bytes 2752512 | tf_op jit(solution)/shard_map/all_to_all | solution.py:267
  29.3 1.2 copy-done.5
  30.5 11.9 %layer.2 = (bf16[64,64,128]{2,1,0:T(8,128)(2,1)S(1)}, bf16[2,64,5376]{2,1,0:T(8,128)(2,1)S(1)}, f32[64,128]{1,0:T(8,128)S(1)}) custom-call(s32[64]{0:T(128)S(1)} %copy-done.11, bf16[128,64,128]{2,1,0:T(8,128)(2,1)} %pooled_ref.3, bf16[128,64,128]{2,1,0:T(8,128)(2,1)} %cot_ref.3, bf16[64,16]{1,0:T(8,128)(2,1)S(1)} %copy.33.proj_ref, ...), custom_call_target="tpu_custom_call" | custom-call | flops 15000000512 | bytes 10485760 | tf_op jit(solution)/shard_map/layer/pallas_call | solution.py:135
  42.4 1.0 copy-done.2
  43.4 0.7 gather_fusion
  44.2 5.5 %all_to_all.35.acts1_ref = bf16[2,64,5376]{2,1,0:T(8,128)(2,1)} all-to-all(bf16[2,64,5376]{2,1,0:T(8,128)(2,1)S(1)} %get-tuple-element.21), channel_id=1, replica_groups=mesh['y'=4,'zh'=2,'x'=4,'zl'=4,'c'=2] {'c'}, dimensions={0} | all-to-all | bytes 2752512 | tf_op jit(solution)/shard_map/all_to_all | solution.py:267
  49.8 12.8 %all_to_all.36 = s32[64,2,128]{2,1,0:T(2,128)S(1)} all-to-all(s32[64,2,128]{2,1,0:T(2,128)S(1)} %broadcast_select_fusion), channel_id=1, replica_groups=mesh['y'=4,'zh'=2,'x'=4,'zl'=4,'c'=2] {'y','c','x'}, dimensions={0} | all-to-all | bytes 131072 | tf_op jit(solution)/shard_map/all_to_all | solution.py:259
  62.6 6.6 %all-to-all-start.2 = ((bf16[64,64,128]{2,1,0:T(8,128)(2,1)}), bf16[64,64,128]{2,1,0:T(8,128)(2,1)}, u32[]{:S(2)}, u32[]{:S(2)}) async-start(bf16[64,64,128]{2,1,0:T(8,128)(2,1)} %copy-done.3), calls=%async_computation.2 | async-start | bytes 2097152 | tf_op jit(solution)/shard_map/all_to_all | solution.py:266
  69.2 2.7 %weight_grads.1 = bf16[16,176,512]{2,1,0:T(8,128)(2,1)} custom-call(bf16[2,64,5376]{2,1,0:T(8,128)(2,1)S(1)} %all-to-all-done.3.acts0_ref, bf16[2,64,5376]{2,1,0:T(8,128)(2,1)S(1)} %copy-done.1, f32[64,128]{1,0:T(8,128)S(1)} %get-tuple-element.22.tail0_ref, f32[64,128]{1,0:T(8,128)S(1)} %get-tuple-element.23.tail1_ref), custom_call_target="tpu_custom_call" | custom-call | flops 5000000000 | bytes 6291456 | tf_op jit(solution)/shard_map/weight_grads/pallas_call | solution.py:173
  72.2 12.5 %all-to-all-done.2 = bf16[64,64,128]{2,1,0:T(8,128)(2,1)} async-done(((bf16[64,64,128]{2,1,0:T(8,128)(2,1)}), bf16[64,64,128]{2,1,0:T(8,128)(2,1)}, u32[]{:S(2)}, u32[]{:S(2)}) %all-to-all-start.2) | async-done | bytes 1048608 | tf_op jit(solution)/shard_map/all_to_all | solution.py:266
  84.6 6.0 %all-to-all-start.1 = ((bf16[64,64,128]{2,1,0:T(8,128)(2,1)}), bf16[64,64,128]{2,1,0:T(8,128)(2,1)S(1)}, u32[]{:S(2)}, u32[]{:S(2)}) async-start(bf16[64,64,128]{2,1,0:T(8,128)(2,1)} %copy-done.2), calls=%async_computation.1 | async-start | bytes 2097152 | tf_op jit(solution)/shard_map/all_to_all | solution.py:266
  90.9 11.6 %table_first.1.refs_2_ = f32[2,1024,512]{2,1,0:T(8,128)S(1)} custom-call(s32[16,2,2,128]{3,2,1,0:T(2,128)S(1)} %squeeze.13.refs_0_, bf16[16,2,2,64,128]{4,3,2,1,0:T(8,128)(2,1)} %bitcast.4.refs_1_), custom_call_target="tpu_custom_call" | custom-call | flops 8999999488 | bytes 5242880 | tf_op jit(solution)/shard_map/table_first/pallas_call | solution.py:224
  102.6 1.9 copy-done.12
  104.5 1.4 all-to-all-done.1
  105.9 5.2 %all-to-all-start.5 = ((bf16[16,176,512]{2,1,0:T(8,128)(2,1)}), bf16[16,176,512]{2,1,0:T(8,128)(2,1)}, u32[]{:S(2)}, u32[]{:S(2)}) async-start(bf16[16,176,512]{2,1,0:T(8,128)(2,1)} %weight_grads.1), calls=%async_computation.6 | async-start | bytes 5767168 | tf_op jit(solution)/shard_map/all_to_all | solution.py:270
  111.2 13.9 %table_last.1 = bf16[8,2,512,128]{3,2,1,0:T(8,128)(2,1)} custom-call(s32[16,2,2,128]{3,2,1,0:T(2,128)S(1)} %squeeze.12.refs_0_, bf16[16,2,2,64,128]{4,3,2,1,0:T(8,128)(2,1)S(1)} %bitcast.29, f32[2,1024,512]{2,1,0:T(8,128)} %copy-done.12), custom_call_target="tpu_custom_call" | custom-call | flops 8999999488 | bytes 5242880 | tf_op jit(solution)/shard_map/table_last/pallas_call | solution.py:224
  125.2 25.8 %all-to-all-done.5 = bf16[16,176,512]{2,1,0:T(8,128)(2,1)} async-done(((bf16[16,176,512]{2,1,0:T(8,128)(2,1)}), bf16[16,176,512]{2,1,0:T(8,128)(2,1)}, u32[]{:S(2)}, u32[]{:S(2)}) %all-to-all-start.5) | async-done | bytes 2883616 | tf_op jit(solution)/shard_map/all_to_all | solution.py:270
  150.9 2.3 %reduce_sum.21 = bf16[176,512]{1,0:T(8,128)(2,1)S(1)} reduce(bf16[16,176,512]{2,1,0:T(8,128)(2,1)} %all-to-all-done.5, bf16[]{:T(256)} %constant.18.clone.1), dimensions={0}, to_apply=%region_1.2 | reduce | flops 1351680 | bytes 3063810 | tf_op jit(solution)/shard_map/reduce_sum | solution.py:274
  153.5 19.2 %all_to_all.37 = bf16[8,36,512]{2,1,0:T(8,128)(2,1)S(1)} all-to-all(bf16[8,36,512]{2,1,0:T(8,128)(2,1)S(1)} %copy.37), channel_id=1, replica_groups=mesh['y'=4,'zh'=2,'x'=4,'zl'=4,'c'=2] {'zh','zl'}, dimensions={0} | all-to-all | bytes 589824 | tf_op jit(solution)/shard_map/all_to_all | solution.py:279
  172.7 4.0 %collective-permute-start.2 = (f32[64,128]{1,0:T(8,128)S(1)}, f32[64,128]{1,0:T(8,128)S(1)}, u32[]{:S(2)}, u32[]{:S(2)}) collective-permute-start(f32[64,128]{1,0:T(8,128)S(1)} %bitcast.35), channel_id=1, source_target_pairs={{0,1},{1,0},{2,3},{3,2},{4,5},{5,4},{6,7},{7,6},{8,9},{9,8},{10,11... | collective-permute-start | bytes 98312 | tf_op jit(solution)/shard_map/ppermute | solution.py:285
  176.8 3.7 %collective-permute-start.1 = (f32[16,512]{1,0:T(8,128)S(1)}, f32[16,512]{1,0:T(8,128)S(1)}, u32[]{:S(2)}, u32[]{:S(2)}) collective-permute-start(f32[16,512]{1,0:T(8,128)S(1)} %get-tuple-element.33), channel_id=1, source_target_pairs={{0,0},{1,128},{2,1},{3,129},{4,2},{5,130},{6,3},{7,131},{8,8},{9,1... | collective-permute-start | bytes 98312 | tf_op jit(solution)/shard_map/ppermute | solution.py:283
  180.5 4.5 %collective-permute-start = (f32[4,512]{1,0:T(4,128)S(1)}, f32[4,512]{1,0:T(4,128)S(1)}, u32[]{:S(2)}, u32[]{:S(2)}) collective-permute-start(f32[4,512]{1,0:T(4,128)S(1)} %slice.53), channel_id=1, source_target_pairs={{0,0},{1,2},{2,1},{3,3},{4,4},{5,6},{6,5},{7,7},{8,16},{9,18},{10,... | collective-permute-start | bytes 24584 | tf_op jit(solution)/shard_map/ppermute | solution.py:282
  187.5 3.4 %collective-permute-done = f32[4,512]{1,0:T(4,128)S(1)} collective-permute-done((f32[4,512]{1,0:T(4,128)S(1)}, f32[4,512]{1,0:T(4,128)S(1)}, u32[]{:S(2)}, u32[]{:S(2)}) %collective-permute-start) | collective-permute-done | bytes 8224 | tf_op jit(solution)/shard_map/ppermute | solution.py:282
  190.9 1.9 collective-permute-start.3
  192.8 12.8 %collective-permute-done.3 = bf16[2,512,128]{2,1,0:T(8,128)(2,1)S(1)} collective-permute-done((bf16[2,512,128]{2,1,0:T(8,128)(2,1)}, bf16[2,512,128]{2,1,0:T(8,128)(2,1)S(1)}, u32[]{:S(2)}, u32[]{:S(2)}) %collective-permute-start.3) | collective-permute-done | bytes 262176 | tf_op jit(solution)/shard_map/ppermute | solution.py:288
  205.6 0.8 convert_element_type.9
  (56 shorter events, 4.7 us)
Async XLA Ops:
  7.2 36.3 %copy-start = (s32[128,64,2]{0,2,1:T(2,128)S(1)}, s32[128,64,2]{0,2,1:T(2,128)}, u32[]{:S(2)}) copy-start(s32[128,64,2]{0,2,1:T(2,128)} %param.17) | copy-start | bytes 196612
  8.0 1.2 copy-start.4
  9.2 0.7 copy-start.6
  9.9 0.7 copy-start.8
  10.6 0.7 copy-start.10
  23.9 1.0 copy-start.3
  24.8 4.4 %copy-start.7 = (bf16[32,64]{1,0:T(8,128)(2,1)S(1)}, bf16[32,64]{1,0:T(8,128)(2,1)}, u32[]{:S(2)}) copy-start(bf16[32,64]{1,0:T(8,128)(2,1)} %wc_ref.3) | copy-start | bytes 12292
  24.8 4.4 %copy-start.9 = (f32[128]{0:T(128)S(1)}, f32[128]{0:T(128)}, u32[]{:S(2)}) copy-start(f32[128]{0:T(128)} %param.15) | copy-start | bytes 1540
  24.8 4.5 %copy-start.11 = (s32[64]{0:T(128)S(1)}, s32[64]{0:T(128)}, u32[]{:S(2)}) copy-start(s32[64]{0:T(128)} %fm_ref.3) | copy-start | bytes 772
  24.8 19.4 %all-to-all-start.3 = ((bf16[2,64,5376]{2,1,0:T(8,128)(2,1)}), bf16[2,64,5376]{2,1,0:T(8,128)(2,1)S(1)}, u32[]{:S(2)}, u32[]{:S(2)}) async-start(bf16[2,64,5376]{2,1,0:T(8,128)(2,1)} %get-tuple-element.20), calls=%async_computation.4 | async-start | bytes 2752512 | tf_op jit(solution)/shard_map/all_to_all | solution.py:267
  29.3 1.2 copy-start.5
  42.4 1.0 copy-start.2
  49.8 19.4 %copy-start.1 = (bf16[2,64,5376]{2,1,0:T(8,128)(2,1)S(1)}, bf16[2,64,5376]{2,1,0:T(8,128)(2,1)}, u32[]{:S(2)}) copy-start(bf16[2,64,5376]{2,1,0:T(8,128)(2,1)} %all_to_all.35.acts1_ref) | copy-start | bytes 4128772
  62.6 22.0 %all-to-all-start.2 = ((bf16[64,64,128]{2,1,0:T(8,128)(2,1)}), bf16[64,64,128]{2,1,0:T(8,128)(2,1)}, u32[]{:S(2)}, u32[]{:S(2)}) async-start(bf16[64,64,128]{2,1,0:T(8,128)(2,1)} %copy-done.3), calls=%async_computation.2 | async-start | bytes 2097152 | tf_op jit(solution)/shard_map/all_to_all | solution.py:266
  84.6 21.3 %all-to-all-start.1 = ((bf16[64,64,128]{2,1,0:T(8,128)(2,1)}), bf16[64,64,128]{2,1,0:T(8,128)(2,1)S(1)}, u32[]{:S(2)}, u32[]{:S(2)}) async-start(bf16[64,64,128]{2,1,0:T(8,128)(2,1)} %copy-done.2), calls=%async_computation.1 | async-start | bytes 2097152 | tf_op jit(solution)/shard_map/all_to_all | solution.py:266
  102.5 1.9 copy-start.12
  105.9 45.0 %all-to-all-start.5 = ((bf16[16,176,512]{2,1,0:T(8,128)(2,1)}), bf16[16,176,512]{2,1,0:T(8,128)(2,1)}, u32[]{:S(2)}, u32[]{:S(2)}) async-start(bf16[16,176,512]{2,1,0:T(8,128)(2,1)} %weight_grads.1), calls=%async_computation.6 | async-start | bytes 5767168 | tf_op jit(solution)/shard_map/all_to_all | solution.py:270
  111.2 79.7 %reduce-scatter.2.cloned.1.call-start = ((), (), s32[]{:S(2)}) async-start(), calls=%async_computation.8 | async-start | bytes 2359296 | tf_op jit(solution)/shard_map/reduce_scatter | solution.py:273
  172.7 12.3 %collective-permute-start.2 = (f32[64,128]{1,0:T(8,128)S(1)}, f32[64,128]{1,0:T(8,128)S(1)}, u32[]{:S(2)}, u32[]{:S(2)}) collective-permute-start(f32[64,128]{1,0:T(8,128)S(1)} %bitcast.35), channel_id=1, source_target_pairs={{0,1},{1,0},{2,3},{3,2},{4,5},{5,4},{6,7},{7,6},{8,9},{9,8},{10,11... | collective-permute-start | bytes 98312 | tf_op jit(solution)/shard_map/ppermute | solution.py:285
  176.8 10.0 %collective-permute-start.1 = (f32[16,512]{1,0:T(8,128)S(1)}, f32[16,512]{1,0:T(8,128)S(1)}, u32[]{:S(2)}, u32[]{:S(2)}) collective-permute-start(f32[16,512]{1,0:T(8,128)S(1)} %get-tuple-element.33), channel_id=1, source_target_pairs={{0,0},{1,128},{2,1},{3,129},{4,2},{5,130},{6,3},{7,131},{8,8},{9,1... | collective-permute-start | bytes 98312 | tf_op jit(solution)/shard_map/ppermute | solution.py:283
  180.5 10.4 %collective-permute-start = (f32[4,512]{1,0:T(4,128)S(1)}, f32[4,512]{1,0:T(4,128)S(1)}, u32[]{:S(2)}, u32[]{:S(2)}) collective-permute-start(f32[4,512]{1,0:T(4,128)S(1)} %slice.53), channel_id=1, source_target_pairs={{0,0},{1,2},{2,1},{3,3},{4,4},{5,6},{6,5},{7,7},{8,16},{9,18},{10,... | collective-permute-start | bytes 24584 | tf_op jit(solution)/shard_map/ppermute | solution.py:282
  190.9 14.7 %collective-permute-start.3 = (bf16[2,512,128]{2,1,0:T(8,128)(2,1)}, bf16[2,512,128]{2,1,0:T(8,128)(2,1)S(1)}, u32[]{:S(2)}, u32[]{:S(2)}) collective-permute-start(bf16[2,512,128]{2,1,0:T(8,128)(2,1)} %bitcast.39), channel_id=1, source_target_pairs={{0,0},{1,32},{32,1},{33,33},{2,2},{3,34},{34,3},{35,35},{4,4},{5,3... | collective-permute-start | bytes 786440 | tf_op jit(solution)/shard_map/ppermute | solution.py:288
Sparse Core Ops, SparseCore 0:
  125.3 41.7 reduce-scatter.1

commit v3 on v2

--- a/solution.py
+++ b/solution.py
@@ -38,8 +38,8 @@
     return jnp.sum(v.reshape(v.shape[0] // 8, 8, 128), axis=0)
 
 
-def layer_kernel(scale, b, fm_ref, pooled_ref, cot_ref, proj_ref, wup_ref, wdown_ref, wc_ref, gain_ref,
-                 bags_ref, acts_ref, tail_ref, inv_ref, ds1, ds2, wups, wupr):
+def layer_kernel(scale, b, fm_ref, core_ref, pooled_ref, cot_ref, proj_ref, wup_ref, wdown_ref, wc_ref, gain_ref,
+                 bags_ref, keep_ref, send_ref, tail_ref, inv_ref, ds1, ds2, wups, wupr):
     for j in range(64):
         inv_ref[fm_ref[j]] = j
     for q in range(4):
@@ -87,11 +87,12 @@
     dfm = jnp.concatenate(dfms, axis=1)
     hg = dot_nt(dfm, wdown_ref[...])
     dpre = (hg * sig * (1.0 + preact * (1.0 - sig))).astype(BF)
-    for h in range(2):
-        acts_ref[h, :, 0:512] = nb[:, h * 512:(h + 1) * 512]
-        acts_ref[h, :, 512:1024] = dpre
-        acts_ref[h, :, 1024:1280] = hidden[:, h * 256:(h + 1) * 256]
-        acts_ref[h, :, 1280:5376] = dfm
+    first_core = core_ref[0] == 0
+    for ref, flag in ((keep_ref, first_core), (send_ref, jnp.logical_not(first_core))):
+        ref[:, 0:512] = jnp.where(flag, nb[:, 0:512], nb[:, 512:1024])
+        ref[:, 512:1024] = dpre
+        ref[:, 1024:1280] = jnp.where(flag, hidden[:, 0:256], hidden[:, 256:512])
+        ref[:, 1280:5376] = dfm
     dnormed = dot_nt(dpre, wupr[...])
     first = jnp.mean(dnormed, axis=1, keepdims=True)
     second = jnp.mean(dnormed * normed, axis=1, keepdims=True)
@@ -129,17 +130,18 @@
         jnp.broadcast_to(jnp.sum(gg, axis=0, keepdims=True), (16, 128))], axis=0) * scale
 
 
-def layer_call(part, batch, feature_map, pooled, cotangent, projection, w_up, w_down, w_compress, gain, scale):
+def layer_call(part, batch, feature_map, core, pooled, cotangent, projection, w_up, w_down, w_compress, gain, scale):
     full = lambda *sh: pl.BlockSpec(sh, lambda i: (0,) * len(sh))
     half = lambda: pl.BlockSpec((batch, 64, 128), lambda i: (part, 0, 0))
     return pl.pallas_call(
         functools.partial(layer_kernel, scale, batch),
         grid=(1,),
-        in_specs=[pl.BlockSpec(memory_space=pltpu.SMEM), half(), half(),
+        in_specs=[pl.BlockSpec(memory_space=pltpu.SMEM), pl.BlockSpec(memory_space=pltpu.SMEM), half(), half(),
                   full(64, 16), full(1024, 512), full(512, 4096), full(32, 64), full(1, 128)],
-        out_specs=[full(64, batch, 128), full(2, batch, 5376), full(64, 128)],
+        out_specs=[full(64, batch, 128), full(batch, 5376), full(batch, 5376), full(64, 128)],
         out_shape=[jax.ShapeDtypeStruct((64, batch, 128), BF),
-                   jax.ShapeDtypeStruct((2, batch, 5376), BF),
+                   jax.ShapeDtypeStruct((batch, 5376), BF),
+                   jax.ShapeDtypeStruct((batch, 5376), BF),
                    jax.ShapeDtypeStruct((64, 128), F32)],
         scratch_shapes=[pltpu.SMEM((64,), jnp.int32),
                         pltpu.VMEM((32, batch, 128), F32), pltpu.VMEM((batch, 32, 128), F32),
@@ -147,37 +149,37 @@
         compiler_params=pltpu.CompilerParams(vmem_limit_bytes=50 << 20),
         cost_estimate=pl.CostEstimate(flops=15 * 10**9, bytes_accessed=10 << 20, transcendentals=0),
         name="layer",
-    )(feature_map, pooled, cotangent, projection, w_up, w_down, w_compress, gain)
-
-
-def weight_kernel(scale, acts0_ref, acts1_ref, tail0_ref, tail1_ref, w_ref, gus):
-    acts = jnp.concatenate([acts0_ref[0], acts0_ref[1], acts1_ref[0], acts1_ref[1]], axis=0)
+    )(feature_map, core, pooled, cotangent, projection, w_up, w_down, w_compress, gain)
+
+
+def weight_kernel(scale, a0_ref, b0_ref, a1_ref, b1_ref, tail0_ref, tail1_ref, w_ref, gus):
+    acts = jnp.concatenate([a0_ref[...], b0_ref[...], a1_ref[...], b1_ref[...]], axis=0)
     tail = tail0_ref[...] + tail1_ref[...]
     tail = jnp.concatenate([tail[q * 16:(q + 1) * 16, :] for q in range(4)], axis=1).astype(BF)
     up = dot_tn(acts[:, 0:512], acts[:, 512:1024]) * scale
     for q in range(4):
         for k in range(8):
             gus[pl.ds(k, 64, stride=8), :] = up[k * 64:(k + 1) * 64, q * 128:(q + 1) * 128]
-        for z in range(16):
-            w_ref[z, 0:32, q * 128:(q + 1) * 128] = gus[z * 32:(z + 1) * 32, :].astype(BF)
+        for z in range(8):
+            w_ref[z, 0:64, q * 128:(q + 1) * 128] = gus[z * 64:(z + 1) * 64, :].astype(BF)
     hid = acts[:, 1024:1280]
     for q in range(8):
         down = (dot_tn(hid, acts[:, 1280 + q * 512:1792 + q * 512]) * scale).astype(BF)
-        for z in range(16):
-            w_ref[z, 32 + q * 16:48 + q * 16, :] = down[z * 16:(z + 1) * 16, :]
-    for z in range(16):
-        w_ref[z, 160:176, :] = tail
-
-
-def weight_call(acts0, acts1, tail0, tail1, scale):
+        for z in range(8):
+            w_ref[z, 64 + q * 32:96 + q * 32, :] = down[z * 32:(z + 1) * 32, :]
+    for z in range(8):
+        w_ref[z, 320:336, :] = tail
+
+
+def weight_call(acts, tails, scale):
     return pl.pallas_call(
         functools.partial(weight_kernel, scale),
-        out_shape=jax.ShapeDtypeStruct((16, 176, 512), BF),
+        out_shape=jax.ShapeDtypeStruct((8, 336, 512), BF),
         scratch_shapes=[pltpu.VMEM((512, 128), F32)],
         compiler_params=pltpu.CompilerParams(vmem_limit_bytes=40 << 20),
-        cost_estimate=pl.CostEstimate(flops=5 * 10**9, bytes_accessed=6 << 20, transcendentals=0),
+        cost_estimate=pl.CostEstimate(flops=3 * 10**9, bytes_accessed=6 << 20, transcendentals=0),
         name="weight_grads",
-    )(acts0, acts1, tail0, tail1)
+    )(*acts, *tails)
 
 
 def table_kernel(pairs, last, *refs):
@@ -246,47 +248,57 @@
     up, down = [], []
     for d in range(256):
         y, zh, x, zl, c = (d // 64, d // 32 % 2, d // 8 % 4, d // 2 % 4, d % 2)
-        unit = (y * 4 + x) * 8 + zh * 4 + zl
-        up.append((d, (unit // 2) * 4 + 2 * c + unit % 2))
-        down.append((d, c * 128 + unit))
+        z, sub = zh * 4 + zl, y * 4 + x
+        up.append((d, z * 32 + (sub // 2) * 4 + 2 * c + sub % 2))
+        down.append((d, c * 128 + z * 16 + sub))
     return up, down
 
 
 def shards(pooled, cotangent, projection, w_up, w_down, w_compress, ln_gain, feature_map, bag_row_index):
     batch = pooled.shape[0] // 2
     scale = float(batch * 512) ** (-0.5)
+    core = lax.axis_index("c").astype(jnp.int32).reshape(1)
     ids = jnp.take(jnp.transpose(bag_row_index, (1, 2, 0)), feature_map, axis=0)
-    ids = lax.all_to_all(ids, PLANE, 0, 0, tiled=True).reshape(16, 2, 2, 2, 2, batch)
-    ids = jnp.transpose(ids, (4, 0, 2, 3, 1, 5)).reshape(2, 16, 2, 2, 128)
-    bags, acts, tails = [], [], []
-    for part in range(2):
-        bag, act, tail = layer_call(
-            part, batch, feature_map, pooled, cotangent, projection, w_up, w_down, w_compress,
-            ln_gain.reshape(1, 128), scale)
-        bags.append(lax.all_to_all(bag, PLANE, 0, 0, tiled=True).reshape(16, 2, 2, batch, 128))
-        acts.append(lax.all_to_all(act, "c", 0, 0, tiled=True))
-        tails.append(tail)
-    weights = weight_call(acts[0], acts[1], tails[0], tails[1], scale)
-    weights = lax.all_to_all(weights, ("y", "x"), 0, 0, tiled=True)
-    sums = table_call(ids[0], bags[0])
-    rows = table_call(ids[1], bags[1], sums)
-    rows = lax.psum_scatter(rows, ("zh", "zl"), scatter_dimension=0, tiled=True)[0]
-    weights = jnp.sum(weights.astype(F32), axis=0).astype(BF)
+    ids = lax.all_to_all(ids, PLANE, 0, 0, tiled=True)
+    swap = [(0, 1), (1, 0)]
+
+    def layer(part):
+        return layer_call(part, batch, feature_map, core, pooled, cotangent, projection, w_up, w_down, w_compress,
+                          ln_gain.reshape(1, 128), scale)
+
+    def exchange(bag):
+        return lax.all_to_all(bag, PLANE, 0, 0, tiled=True)
+
+    bag0, keep0, send0, tail0 = layer(0)
+    bag0, ids = lax.optimization_barrier((bag0, ids))
+    ids = jnp.transpose(ids.reshape(16, 2, 2, 2, 2, batch), (4, 0, 2, 3, 1, 5)).reshape(2, 16, 2, 2, 128)
+    first = exchange(bag0)
+    bag1, keep1, send1, tail1 = layer(1)
+    send1, first = lax.optimization_barrier((send1, first))
+    acts = (keep0, lax.ppermute(send0, "c", swap), keep1, lax.ppermute(send1, "c", swap))
+    weights = weight_call(acts, (tail0, tail1), scale)
+    bag1, weights = lax.optimization_barrier((bag1, weights))
+    weights = lax.psum_scatter(weights.reshape(8 * 336, 512), ("zh", "zl"), scatter_dimension=0, tiled=True)
+    second = exchange(bag1)
+    rows = table_call(ids[0], first.reshape(16, 2, 2, batch, 128))
+    rows = table_call(ids[1], second.reshape(16, 2, 2, batch, 128), rows)
+    weights, _ = lax.optimization_barrier((weights, rows))
+    rows = lax.psum_scatter(rows.reshape(8192, 128), ("zh", "zl"), scatter_dimension=0, tiled=True)
     pieces = jnp.concatenate(
-        [weights[0:32].reshape(8, 4, 512),
-         weights[32:160].reshape(8, 8, 2, 512).transpose(1, 0, 2, 3).reshape(8, 16, 512),
-         jnp.broadcast_to(weights[160:176], (8, 16, 512))], axis=1)
-    pieces = lax.all_to_all(pieces, ("zh", "zl"), 0, 0, tiled=True)
+        [weights[0:64].reshape(16, 4, 512),
+         weights[64:320].reshape(8, 16, 2, 512).transpose(1, 0, 2, 3).reshape(16, 16, 512),
+         jnp.broadcast_to(weights[320:336], (16, 16, 512))], axis=1)
+    pieces = lax.all_to_all(pieces, ("y", "x"), 0, 0, tiled=True)
     total = jnp.sum(pieces.astype(F32), axis=0)
     up_moves, down_moves = weight_moves()
     gu = lax.ppermute(total[0:4], AXES, up_moves)
     gd = lax.ppermute(total[4:20], AXES, down_moves).reshape(8, 2, 512).transpose(1, 0, 2).reshape(2, 4096)
     tail = total[20:36].reshape(16, 4, 128).transpose(1, 0, 2).reshape(64, 128)
-    tail = tail + lax.ppermute(tail, "c", [(0, 1), (1, 0)])
+    tail = tail + lax.ppermute(tail, "c", swap)
     small = (tail[32:48, :64].T, tail[:32, :64], tail[48])
     rows, gu, gd, small = lax.optimization_barrier((rows, gu, gd, small))
     table_grad = lax.ppermute(rows, ("zh", "c"), [(0, 0), (1, 2), (2, 1), (3, 3)]).astype(F32)
-    return (table_grad, gu, gd) + tuple(small)
+    return (table_grad.reshape(2, 512, 128), gu, gd) + tuple(small)
 
 
 def solution(mesh):

time: 215 us -> 184 us (0.86)
  waiting for transfers between devices: 55.8 us -> 22.7 us
  blocking collectives: 37.5 us -> 14.7 us
  starting transfers between devices: 36.5 us -> 51 us
  local copies, waits for them, and re-layouts: 13.5 us -> 24.1 us
    all_to_all x4 -> x3, waiting for transfers between devices: 39.6 us -> 2.04 us  [the longest x2 2.04 us: exchange(): return lax.all_to_all(bag, PLANE, 0, 0, tiled=True)]
    all_to_all x3 -> x1, blocking collectives: 37.5 us -> 14.7 us  [shards(): pieces = lax.all_to_all(pieces, ('y', 'x'), 0, 0, tiled=True)]
    reduce_scatter x1 -> x2, waiting for transfers between devices: 0.01 us -> 9.36 us  [the longest x1 5.35 us: shards(): lax.psum_scatter(weights.reshape(8 * 336, 512), ('zh', 'zl'), scatter_dim...]
    unnamed x30 -> x46, local copies, waits for them, and re-layouts: 10.4 us -> 18.2 us
    ppermute x1, starting transfers between devices: 1.91 us -> 9.57 us  [shards(): lax.ppermute(rows, ('zh', 'c'), [(0, 0), (1, 2), (2, 1), (3, 3)])]
    ppermute x1, waiting for transfers between devices: 12.8 us -> 6.53 us  [shards(): lax.ppermute(rows, ('zh', 'c'), [(0, 0), (1, 2), (2, 1), (3, 3)])]
    ppermute x1, waiting for transfers between devices: 3.41 us -> 0.01 us  [shards(): gu = lax.ppermute(total[0:4], AXES, up_moves)]
    ppermute x1, waiting for transfers between devices: 0.01 us -> 2.78 us  [shards(): lax.ppermute(total[4:20], AXES, down_moves).reshape(8, 2, 512)]
  transfers between devices with their start and end apart: 9 -> 11, of which waited for: 5 -> 6; matrix products, arithmetic and copies ran while one was open for 3% -> 4% of each run, Pallas kernels for 19% -> 27%
where the time goes in v3:
time: 184 us; the launch traced here: 182 us
  Pallas kernels  52.5 us (29%)
  starting transfers between devices  51 us (28%)
  local copies, waits for them, and re-layouts  24.1 us (13%)
  waiting for transfers between devices  22.7 us (12%)
  blocking collectives  14.7 us (8%)
  between operations  14.3 us (8%)
  other arithmetic  3.14 us (2%)
    pallas_call x2, Pallas kernels, layer_call(): pl.pallas_call(functools.partial(layer_kernel, scale, batch), grid=(1,),...  25.1 us
    pallas_call x2, Pallas kernels, table_call(): pl.pallas_call(functools.partial(table_kernel, pairs, last), grid=(2, ids...  24.8 us
    unnamed x46, local copies, waits for them, and re-layouts  18.2 us
    all_to_all x1, blocking collectives, shards(): pieces = lax.all_to_all(pieces, ('y', 'x'), 0, 0, tiled=True)  14.7 us
    all_to_all x2, starting transfers between devices, exchange(): return lax.all_to_all(bag, PLANE, 0, 0, tiled=True)  14.6 us
    ppermute x1, starting transfers between devices, shards(): lax.ppermute(rows, ('zh', 'c'), [(0, 0), (1, 2), (2, 1), (3, 3)])  9.57 us
    all_to_all x1, starting transfers between devices, shards(): ids = lax.all_to_all(ids, PLANE, 0, 0, tiled=True)  7.88 us
    ppermute x1, waiting for transfers between devices, shards(): lax.ppermute(rows, ('zh', 'c'), [(0, 0), (1, 2), (2, 1), (3, 3)])  6.53 us
  transfers between devices with their start and end apart: 11, of which 6 were waited for; matrix products, arithmetic and copies ran while one was open for 4% of the time, Pallas kernels for 27%

profile of v3, /device:TPU:7, one launch (start us, length us, event | category | flops | bytes accessed | tf_op | source)
XLA Modules:
  0.0 182.4 jit_solution(10773869231701991517)
XLA Ops:
  9.2 0.8 broadcast_select_fusion
  10.0 7.9 %all-to-all-start = ((s32[64,2,128]{2,1,0:T(2,128)}), s32[64,2,128]{2,1,0:T(2,128)S(1)}, u32[]{:S(2)}, u32[]{:S(2)}) async-start(s32[64,2,128]{2,1,0:T(2,128)} %broadcast_select_fusion), calls=%async_computation | async-start | bytes 131072 | tf_op jit(solution)/shard_map/all_to_all | solution.py:262
  17.9 0.8 copy.32.proj_ref
  18.6 1.2 copy-done.1
  21.9 12.5 %layer.2 = (bf16[64,64,128]{2,1,0:T(8,128)(2,1)}, bf16[64,5376]{1,0:T(8,128)(2,1)S(1)}, bf16[64,5376]{1,0:T(8,128)(2,1)S(1)}, f32[64,128]{1,0:T(8,128)S(1)}) custom-call(s32[64]{0:T(128)S(1)} %copy-done.6, s32[1]{0:T(128)} %bitcast.core_ref, bf16[128,64,128]{2,1,0:T(8,128)(2,1)} %pooled_ref.3, bf16[128,64,128]{2,1,0:T(8,128)(2,1)} %cot_ref.3, ...), custom_call_target="tpu_custom_call" | custom-call | flops 15000000512 | bytes 10485760 | tf_op jit(solution)/shard_map/layer/pallas_call | solution.py:136
  34.4 0.9 copy-done.10
  36.9 7.2 %all-to-all-start.1 = ((bf16[64,64,128]{2,1,0:T(8,128)(2,1)}), bf16[64,64,128]{2,1,0:T(8,128)(2,1)S(1)}, u32[]{:S(2)}, u32[]{:S(2)}) async-start(bf16[64,64,128]{2,1,0:T(8,128)(2,1)} %get-tuple-element.34), calls=%async_computation.1 | async-start | bytes 2097152 | tf_op jit(solution)/shard_map/all_to_all | solution.py:270
  46.3 12.6 %layer.3 = (bf16[64,64,128]{2,1,0:T(8,128)(2,1)}, bf16[64,5376]{1,0:T(8,128)(2,1)S(1)}, bf16[64,5376]{1,0:T(8,128)(2,1)S(1)}, f32[64,128]{1,0:T(8,128)S(1)}) custom-call(s32[64]{0:T(128)S(1)} %copy-done.7, s32[1]{0:T(128)} %bitcast.core_ref, bf16[128,64,128]{2,1,0:T(8,128)(2,1)} %pooled_ref.3, bf16[128,64,128]{2,1,0:T(8,128)(2,1)} %cot_ref.3, ...), custom_call_target="tpu_custom_call" | custom-call | flops 15000000512 | bytes 10485760 | tf_op jit(solution)/shard_map/layer/pallas_call | solution.py:136
  58.9 0.9 copy-done.3
  59.7 0.8 copy-done.12
  61.5 2.0 %collective-permute-done.1.b1_ref = bf16[64,5376]{1,0:T(8,128)(2,1)S(1)} collective-permute-done((bf16[64,5376]{1,0:T(8,128)(2,1)}, bf16[64,5376]{1,0:T(8,128)(2,1)S(1)}, u32[]{:S(2)}, u32[]{:S(2)}) %collective-permute-start.1) | collective-permute-done | bytes 688160 | tf_op jit(solution)/shard_map/ppermute | solution.py:278
  63.5 1.1 copy-done.11
  64.6 1.1 copy-done.13
  67.3 2.7 %weight_grads.1 = bf16[8,336,512]{2,1,0:T(8,128)(2,1)} custom-call(bf16[64,5376]{1,0:T(8,128)(2,1)S(1)} %copy-done.11, bf16[64,5376]{1,0:T(8,128)(2,1)S(1)} %collective-permute-done.b0_ref, bf16[64,5376]{1,0:T(8,128)(2,1)S(1)} %copy-done.13, bf16[64,5376]{1,0:T(8,128)(2,1)S(1)} %collective-permute-done.1.b1_ref, f32[64,128]{1,0:T(8,128)S(1)} %copy-done.16, ...), custom_call_target="tpu_custom_call" | custom-call | flops 3000000000 | bytes 6291456 | tf_op jit(solution)/shard_map/weight_grads/pallas_call | solution.py:175
  69.9 0.8 copy-done.20
  71.0 7.4 %all-to-all-start.2 = ((bf16[64,64,128]{2,1,0:T(8,128)(2,1)}), bf16[64,64,128]{2,1,0:T(8,128)(2,1)S(1)}, u32[]{:S(2)}, u32[]{:S(2)}) async-start(bf16[64,64,128]{2,1,0:T(8,128)(2,1)} %get-tuple-element.38), calls=%async_computation.2 | async-start | bytes 2097152 | tf_op jit(solution)/shard_map/all_to_all | solution.py:270
  78.9 10.7 %table_first.1.refs_2_ = f32[2,1024,512]{2,1,0:T(8,128)S(1)} custom-call(s32[16,2,2,128]{3,2,1,0:T(2,128)S(1)} %squeeze.10.refs_0_, bf16[16,2,2,64,128]{4,3,2,1,0:T(8,128)(2,1)S(1)} %bitcast.33), custom_call_target="tpu_custom_call" | custom-call | flops 8999999488 | bytes 5242880 | tf_op jit(solution)/shard_map/table_first/pallas_call | solution.py:226
  89.7 1.9 %copy-done.14 = f32[2,1024,512]{2,1,0:T(8,128)} copy-done((f32[2,1024,512]{2,1,0:T(8,128)}, f32[2,1024,512]{2,1,0:T(8,128)S(1)}, u32[]{:S(2)}) %copy-start.14) | copy-done | bytes 4194328
  91.6 2.0 %all-to-all-done.2 = bf16[64,64,128]{2,1,0:T(8,128)(2,1)S(1)} async-done(((bf16[64,64,128]{2,1,0:T(8,128)(2,1)}), bf16[64,64,128]{2,1,0:T(8,128)(2,1)S(1)}, u32[]{:S(2)}, u32[]{:S(2)}) %all-to-all-start.2) | async-done | bytes 1048608 | tf_op jit(solution)/shard_map/all_to_all | solution.py:270
  93.7 14.0 %table_last.1 = bf16[8,2,512,128]{3,2,1,0:T(8,128)(2,1)} custom-call(s32[16,2,2,128]{3,2,1,0:T(2,128)S(1)} %squeeze.9.refs_0_, bf16[16,2,2,64,128]{4,3,2,1,0:T(8,128)(2,1)S(1)} %bitcast.34, f32[2,1024,512]{2,1,0:T(8,128)} %copy-done.14), custom_call_target="tpu_custom_call" | custom-call | flops 8999999488 | bytes 5242880 | tf_op jit(solution)/shard_map/table_last/pallas_call | solution.py:226
  107.7 5.3 %reduce-scatter.5.cloned.1.call-done = bf16[336,512]{1,0:T(8,128)(2,1)} async-done(((bf16[2688,512]{1,0:T(8,128)(2,1)}), bf16[336,512]{1,0:T(8,128)(2,1)}) %reduce-scatter.5.cloned.1.call-update) | async-done | bytes 344080 | tf_op jit(solution)/shard_map/reduce_scatter | solution.py:281
  113.8 0.8 slice.37
  114.6 1.0 slice.38
  116.2 14.7 %all_to_all.20 = bf16[16,36,512]{2,1,0:T(8,128)(2,1)S(1)} all-to-all(bf16[16,36,512]{2,1,0:T(8,128)(2,1)S(1)} %copy.37), channel_id=1, replica_groups=mesh['y'=4,'zh'=2,'x'=4,'zl'=4,'c'=2] {'y','x'}, dimensions={0} | all-to-all | bytes 1179648 | tf_op jit(solution)/shard_map/all_to_all | solution.py:291
  131.0 5.7 %collective-permute-start.4 = (f32[64,128]{1,0:T(8,128)S(1)}, f32[64,128]{1,0:T(8,128)S(1)}, u32[]{:S(2)}, u32[]{:S(2)}) collective-permute-start(f32[64,128]{1,0:T(8,128)S(1)} %bitcast.41), channel_id=1, source_target_pairs={{0,1},{1,0},{2,3},{3,2},{4,5},{5,4},{6,7},{7,6},{8,9},{9,8},{10,11... | collective-permute-start | bytes 98312 | tf_op jit(solution)/shard_map/ppermute | solution.py:297
  136.7 6.0 %collective-permute-start.2 = (f32[4,512]{1,0:T(4,128)S(1)}, f32[4,512]{1,0:T(4,128)S(1)}, u32[]{:S(2)}, u32[]{:S(2)}) collective-permute-start(f32[4,512]{1,0:T(4,128)S(1)} %slice.50), channel_id=1, source_target_pairs={{0,0},{1,2},{2,32},{3,34},{4,64},{5,66},{6,96},{7,98},{8,1},{9,3},... | collective-permute-start | bytes 24584 | tf_op jit(solution)/shard_map/ppermute | solution.py:294
  142.8 6.0 %collective-permute-start.3 = (f32[16,512]{1,0:T(8,128)S(1)}, f32[16,512]{1,0:T(8,128)S(1)}, u32[]{:S(2)}, u32[]{:S(2)}) collective-permute-start(f32[16,512]{1,0:T(8,128)S(1)} %get-tuple-element.51), channel_id=1, source_target_pairs={{0,0},{1,128},{2,16},{3,144},{4,32},{5,160},{6,48},{7,176},{8,1},{... | collective-permute-start | bytes 98312 | tf_op jit(solution)/shard_map/ppermute | solution.py:295
  150.5 2.8 %collective-permute-done.3 = f32[16,512]{1,0:T(8,128)S(1)} collective-permute-done((f32[16,512]{1,0:T(8,128)S(1)}, f32[16,512]{1,0:T(8,128)S(1)}, u32[]{:S(2)}, u32[]{:S(2)}) %collective-permute-start.3) | collective-permute-done | bytes 32800 | tf_op jit(solution)/shard_map/ppermute | solution.py:295
  154.0 4.0 %reduce-scatter.3.cloned.1.call-done = bf16[1024,128]{1,0:T(8,128)(2,1)} async-done(((bf16[8192,128]{1,0:T(8,128)(2,1)}), bf16[1024,128]{1,0:T(8,128)(2,1)}) %reduce-scatter.3.cloned.1.call-update) | async-done | bytes 262160 | tf_op jit(solution)/shard_map/reduce_scatter | solution.py:286
  158.0 9.6 %collective-permute-start.5 = (bf16[1024,128]{1,0:T(8,128)(2,1)}, bf16[1024,128]{1,0:T(8,128)(2,1)S(1)}, u32[]{:S(2)}, u32[]{:S(2)}) collective-permute-start(bf16[1024,128]{1,0:T(8,128)(2,1)} %reduce-scatter.3.cloned.1.call-done), channel_id=1, source_target_pairs={{0,0},{1,32},{32,1},{33,33},{2,2},{3,34},{34,3},{35,35},{4,4},{5,3... | collective-permute-start | bytes 786440 | tf_op jit(solution)/shard_map/ppermute | solution.py:300
  167.6 6.5 %collective-permute-done.5 = bf16[1024,128]{1,0:T(8,128)(2,1)S(1)} collective-permute-done((bf16[1024,128]{1,0:T(8,128)(2,1)}, bf16[1024,128]{1,0:T(8,128)(2,1)S(1)}, u32[]{:S(2)}, u32[]{:S(2)}) %collective-permute-start.5) | collective-permute-done | bytes 262176 | tf_op jit(solution)/shard_map/ppermute | solution.py:300
  174.1 0.8 convert.1
  (74 shorter events, 15.5 us)
Async XLA Ops:
  7.2 1.4 copy-start
  10.0 26.3 %all-to-all-start = ((s32[64,2,128]{2,1,0:T(2,128)}), s32[64,2,128]{2,1,0:T(2,128)S(1)}, u32[]{:S(2)}, u32[]{:S(2)}) async-start(s32[64,2,128]{2,1,0:T(2,128)} %broadcast_select_fusion), calls=%async_computation | async-start | bytes 131072 | tf_op jit(solution)/shard_map/all_to_all | solution.py:262
  18.6 1.2 copy-start.1
  19.9 0.7 copy-start.4
  20.6 0.7 copy-start.6
  21.2 0.7 copy-start.8
  34.4 0.9 copy-start.10
  35.3 0.6 copy-start.15
  35.9 8.4 %copy-start.2 = (bf16[1024,512]{1,0:T(8,128)(2,1)S(1)}, bf16[1024,512]{1,0:T(8,128)(2,1)}, u32[]{:S(2)}) copy-start(bf16[1024,512]{1,0:T(8,128)(2,1)} %wup_ref.3) | copy-start | bytes 3145732
  35.9 25.7 %collective-permute-start = (bf16[64,5376]{1,0:T(8,128)(2,1)S(1)}, bf16[64,5376]{1,0:T(8,128)(2,1)S(1)}, u32[]{:S(2)}, u32[]{:S(2)}) collective-permute-start(bf16[64,5376]{1,0:T(8,128)(2,1)S(1)} %get-tuple-element.31), channel_id=1, source_target_pairs={{0,1},{1,0},{2,3},{3,2},{4,5},{5,4},{6,7},{7,6},{8,9},{9,8},{10,11... | collective-permute-start | bytes 2064392 | tf_op jit(solution)/shard_map/ppermute | solution.py:278
  36.2 0.6 copy-start.19
  36.9 24.3 %all-to-all-start.1 = ((bf16[64,64,128]{2,1,0:T(8,128)(2,1)}), bf16[64,64,128]{2,1,0:T(8,128)(2,1)S(1)}, u32[]{:S(2)}, u32[]{:S(2)}) async-start(bf16[64,64,128]{2,1,0:T(8,128)(2,1)} %get-tuple-element.34), calls=%async_computation.1 | async-start | bytes 2097152 | tf_op jit(solution)/shard_map/all_to_all | solution.py:270
  44.1 69.0 %reduce-scatter.5.cloned.1.call-start = ((), (), s32[]{:S(2)}) async-start(), calls=%async_computation.7 | async-start | bytes 3096576 | tf_op jit(solution)/shard_map/reduce_scatter | solution.py:281
  44.3 0.7 copy-start.5
  45.0 0.7 copy-start.7
  45.6 0.7 copy-start.9
  58.9 0.9 copy-start.3
  59.7 0.8 copy-start.12
  60.6 0.6 copy-start.17
  61.2 2.4 %collective-permute-start.1 = (bf16[64,5376]{1,0:T(8,128)(2,1)}, bf16[64,5376]{1,0:T(8,128)(2,1)S(1)}, u32[]{:S(2)}, u32[]{:S(2)}) collective-permute-start(bf16[64,5376]{1,0:T(8,128)(2,1)} %copy-done.3), channel_id=1, source_target_pairs={{0,1},{1,0},{2,3},{3,2},{4,5},{5,4},{6,7},{7,6},{8,9},{9,8},{10,11... | collective-permute-start | bytes 2064392 | tf_op jit(solution)/shard_map/ppermute | solution.py:278
  63.5 1.1 copy-start.11
  64.6 1.1 copy-start.13
  65.7 0.8 copy-start.16
  66.5 0.8 copy-start.18
  69.9 0.8 copy-start.20
  71.0 22.7 %all-to-all-start.2 = ((bf16[64,64,128]{2,1,0:T(8,128)(2,1)}), bf16[64,64,128]{2,1,0:T(8,128)(2,1)S(1)}, u32[]{:S(2)}, u32[]{:S(2)}) async-start(bf16[64,64,128]{2,1,0:T(8,128)(2,1)} %get-tuple-element.38), calls=%async_computation.2 | async-start | bytes 2097152 | tf_op jit(solution)/shard_map/all_to_all | solution.py:270
  78.4 79.6 %reduce-scatter.3.cloned.1.call-start = ((), (), s32[]{:S(2)}) async-start(), calls=%async_computation.6 | async-start | bytes 2359296 | tf_op jit(solution)/shard_map/reduce_scatter | solution.py:286
  89.7 2.0 %copy-start.14 = (f32[2,1024,512]{2,1,0:T(8,128)}, f32[2,1024,512]{2,1,0:T(8,128)S(1)}, u32[]{:S(2)}) copy-start(f32[2,1024,512]{2,1,0:T(8,128)S(1)} %table_first.1.refs_2_) | copy-start | bytes 12582916
  131.0 17.8 %collective-permute-start.4 = (f32[64,128]{1,0:T(8,128)S(1)}, f32[64,128]{1,0:T(8,128)S(1)}, u32[]{:S(2)}, u32[]{:S(2)}) collective-permute-start(f32[64,128]{1,0:T(8,128)S(1)} %bitcast.41), channel_id=1, source_target_pairs={{0,1},{1,0},{2,3},{3,2},{4,5},{5,4},{6,7},{7,6},{8,9},{9,8},{10,11... | collective-permute-start | bytes 98312 | tf_op jit(solution)/shard_map/ppermute | solution.py:297
  136.7 21.3 %collective-permute-start.2 = (f32[4,512]{1,0:T(4,128)S(1)}, f32[4,512]{1,0:T(4,128)S(1)}, u32[]{:S(2)}, u32[]{:S(2)}) collective-permute-start(f32[4,512]{1,0:T(4,128)S(1)} %slice.50), channel_id=1, source_target_pairs={{0,0},{1,2},{2,32},{3,34},{4,64},{5,66},{6,96},{7,98},{8,1},{9,3},... | collective-permute-start | bytes 24584 | tf_op jit(solution)/shard_map/ppermute | solution.py:294
  142.8 10.6 %collective-permute-start.3 = (f32[16,512]{1,0:T(8,128)S(1)}, f32[16,512]{1,0:T(8,128)S(1)}, u32[]{:S(2)}, u32[]{:S(2)}) collective-permute-start(f32[16,512]{1,0:T(8,128)S(1)} %get-tuple-element.51), channel_id=1, source_target_pairs={{0,0},{1,128},{2,16},{3,144},{4,32},{5,160},{6,48},{7,176},{8,1},{... | collective-permute-start | bytes 98312 | tf_op jit(solution)/shard_map/ppermute | solution.py:295
  158.0 16.1 %collective-permute-start.5 = (bf16[1024,128]{1,0:T(8,128)(2,1)}, bf16[1024,128]{1,0:T(8,128)(2,1)S(1)}, u32[]{:S(2)}, u32[]{:S(2)}) collective-permute-start(bf16[1024,128]{1,0:T(8,128)(2,1)} %reduce-scatter.3.cloned.1.call-done), channel_id=1, source_target_pairs={{0,0},{1,32},{32,1},{33,33},{2,2},{3,34},{34,3},{35,35},{4,4},{5,3... | collective-permute-start | bytes 786440 | tf_op jit(solution)/shard_map/ppermute | solution.py:300
Sparse Core Ops, SparseCore 0:
  70.1 42.9 reduce-scatter.4
  115.8 42.2 reduce-scatter.2

commit v4 on v3

--- a/solution.py
+++ b/solution.py
@@ -9,6 +9,7 @@
 from jax.sharding import PartitionSpec as P
 
 BF, F32 = jnp.bfloat16, jnp.float32
+VMEM_BYTES = 60 << 20
 
 
 def dot_nn(a, b):
@@ -38,20 +39,27 @@
     return jnp.sum(v.reshape(v.shape[0] // 8, 8, 128), axis=0)
 
 
-def layer_kernel(scale, b, fm_ref, core_ref, pooled_ref, cot_ref, proj_ref, wup_ref, wdown_ref, wc_ref, gain_ref,
-                 bags_ref, keep_ref, send_ref, tail_ref, inv_ref, ds1, ds2, wups, wupr):
+def layer_kernel(scale, b, part, with_ids, *refs):
+    fm_ref, core_ref, pooled_ref = refs[:3]
+    ids_ref = refs[3] if with_ids else None
+    (cot_hbm, projt_ref, wup_hbm, wdown_hbm, wc_ref, gain_ref, bags_ref, keep_ref, send_ref, tail_ref,
+     inv_ref, ds1, ds2, wups, wupr, cot_ref, wup_ref, wdown_ref, sems) = refs[3 + with_ids:]
+    copies = [pltpu.make_async_copy(source, target, sems.at[i]) for i, (source, target) in enumerate((
+        (wup_hbm, wup_ref), (wdown_hbm, wdown_ref), (cot_hbm.at[pl.ds(part * b, b)], cot_ref)))]
+    for copy in copies:
+        copy.start()
     for j in range(64):
         inv_ref[fm_ref[j]] = j
-    for q in range(4):
-        wups[...] = wup_ref[:, q * 128:(q + 1) * 128].astype(F32)
-        for k in range(16):
-            wupr[k * 64:(k + 1) * 64, q * 128:(q + 1) * 128] = wups[pl.ds(k, 64, stride=16), :].astype(BF)
+    if with_ids:
+        for n in range(64):
+            v = ids_ref[n]
+            rows = jnp.concatenate([jnp.bitwise_and(v, 255), lax.shift_right_logical(v, 8), jnp.zeros((12, 128), jnp.int32)], axis=0)
+            bags_ref[inv_ref[n], 64:80, :] = rows.astype(F32).astype(BF)
     x = pooled_ref[...]
     gain = gain_ref[...]
-    proj = proj_ref[...]
+    projt = projt_ref[...]
     wc = wc_ref[...]
-    projt = jnp.transpose(proj.astype(F32)).astype(BF)
-    consts = jnp.concatenate([jnp.transpose(wc.astype(F32)).astype(BF), proj], axis=1)
+    consts = jnp.transpose(jnp.concatenate([wc, projt], axis=0).astype(F32)).astype(BF)
     xcat = jnp.concatenate([x[s] for s in range(b)], axis=1)
     head = dot_nn(jnp.concatenate([projt, wc], axis=0), xcat)
     pts = [head[0:16, s * 128:(s + 1) * 128].astype(BF) for s in range(b)]
@@ -62,10 +70,17 @@
     inv_fm = lax.rsqrt(jnp.mean(cen * cen, axis=1, keepdims=True) + 1e-5)
     normed = cen * inv_fm
     nb = normed.astype(BF)
+    copies[0].wait()
+    for q in range(4):
+        wups[...] = wup_ref[:, q * 128:(q + 1) * 128].astype(F32)
+        for k in range(16):
+            wupr[k * 64:(k + 1) * 64, q * 128:(q + 1) * 128] = wups[pl.ds(k, 64, stride=16), :].astype(BF)
     preact = dot_nn(nb, wupr[...])
     sig = jax.nn.sigmoid(preact)
     hidden = (preact * sig).astype(BF)
+    copies[1].wait()
     fm_out = dot_nn(hidden, wdown_ref[...])
+    copies[2].wait()
     gg = jnp.zeros((8, 128), F32)
     dfms = []
     for m in range(32):
@@ -130,26 +145,33 @@
         jnp.broadcast_to(jnp.sum(gg, axis=0, keepdims=True), (16, 128))], axis=0) * scale
 
 
-def layer_call(part, batch, feature_map, core, pooled, cotangent, projection, w_up, w_down, w_compress, gain, scale):
+def layer_call(part, batch, feature_map, core, pooled, ids, cotangent, projt, w_up, w_down, w_compress, gain, scale):
     full = lambda *sh: pl.BlockSpec(sh, lambda i: (0,) * len(sh))
-    half = lambda: pl.BlockSpec((batch, 64, 128), lambda i: (part, 0, 0))
+    scalars = pl.BlockSpec(memory_space=pltpu.SMEM)
+    far = pl.BlockSpec(memory_space=pl.ANY)
+    with_ids = ids is not None
+    depth = batch + 16 if with_ids else batch
     return pl.pallas_call(
-        functools.partial(layer_kernel, scale, batch),
+        functools.partial(layer_kernel, scale, batch, part, int(with_ids)),
         grid=(1,),
-        in_specs=[pl.BlockSpec(memory_space=pltpu.SMEM), pl.BlockSpec(memory_space=pltpu.SMEM), half(), half(),
-                  full(64, 16), full(1024, 512), full(512, 4096), full(32, 64), full(1, 128)],
-        out_specs=[full(64, batch, 128), full(batch, 5376), full(batch, 5376), full(64, 128)],
-        out_shape=[jax.ShapeDtypeStruct((64, batch, 128), BF),
+        in_specs=[scalars, scalars, pl.BlockSpec((batch, 64, 128), lambda i: (part, 0, 0))]
+        + ([full(64, 2, 128)] if with_ids else [])
+        + [far, full(16, 64), far, far, full(32, 64), full(1, 128)],
+        out_specs=[full(64, depth, 128), full(batch, 5376), full(batch, 5376), full(64, 128)],
+        out_shape=[jax.ShapeDtypeStruct((64, depth, 128), BF),
                    jax.ShapeDtypeStruct((batch, 5376), BF),
                    jax.ShapeDtypeStruct((batch, 5376), BF),
                    jax.ShapeDtypeStruct((64, 128), F32)],
         scratch_shapes=[pltpu.SMEM((64,), jnp.int32),
                         pltpu.VMEM((32, batch, 128), F32), pltpu.VMEM((batch, 32, 128), F32),
-                        pltpu.VMEM((1024, 128), F32), pltpu.VMEM((1024, 512), BF)],
-        compiler_params=pltpu.CompilerParams(vmem_limit_bytes=50 << 20),
+                        pltpu.VMEM((1024, 128), F32), pltpu.VMEM((1024, 512), BF),
+                        pltpu.VMEM((batch, 64, 128), BF), pltpu.VMEM((1024, 512), BF), pltpu.VMEM((512, 4096), BF),
+                        pltpu.SemaphoreType.DMA((3,))],
+        compiler_params=pltpu.CompilerParams(vmem_limit_bytes=VMEM_BYTES),
         cost_estimate=pl.CostEstimate(flops=15 * 10**9, bytes_accessed=10 << 20, transcendentals=0),
-        name="layer",
-    )(feature_map, core, pooled, cotangent, projection, w_up, w_down, w_compress, gain)
+        name="layer_first" if with_ids else "layer_second",
+    )(*([feature_map, core, pooled] + ([ids] if with_ids else [])
+        + [cotangent, projt, w_up, w_down, w_compress, gain]))
 
 
 def weight_kernel(scale, a0_ref, b0_ref, a1_ref, b1_ref, tail0_ref, tail1_ref, w_ref, gus):
@@ -176,7 +198,7 @@
         functools.partial(weight_kernel, scale),
         out_shape=jax.ShapeDtypeStruct((8, 336, 512), BF),
         scratch_shapes=[pltpu.VMEM((512, 128), F32)],
-        compiler_params=pltpu.CompilerParams(vmem_limit_bytes=40 << 20),
+        compiler_params=pltpu.CompilerParams(vmem_limit_bytes=VMEM_BYTES),
         cost_estimate=pl.CostEstimate(flops=3 * 10**9, bytes_accessed=6 << 20, transcendentals=0),
         name="weight_grads",
     )(*acts, *tails)
@@ -189,7 +211,13 @@
         ids_ref, bags_ref, acc = refs
         acc = acc.at[0]
     step = pl.program_id(1)
-    ids = ids_ref[:, 0].reshape(pairs * 2, 128)
+    side = slice(64, 128) if last else slice(0, 64)
+    ids = []
+    for i in range(pairs):
+        codes = ids_ref[i, :, 0].astype(F32)
+        codes = codes[:, 0:2] + 256.0 * codes[:, 2:4]
+        ids.append(jnp.concatenate([codes[0][:, side], codes[1][:, side]], axis=1))
+    ids = jnp.concatenate(ids, axis=0).astype(jnp.int32)
     low = jnp.transpose(lax.shift_right_logical(ids, 10).astype(F32), (1, 0))
     high = jnp.bitwise_and(ids, 1023).astype(jnp.int16)
     iota = lax.broadcasted_iota(jnp.int16, (1024, 128), 0)
@@ -220,18 +248,18 @@
                     out_ref[h * 4 + q, 0] = acc[h * 512:(h + 1) * 512, q * 128:(q + 1) * 128].astype(BF)
 
 
-def table_call(ids, bags, start=None, pairs=8):
+def table_call(ids, bags, start=None, pairs=16):
     last = start is not None
     sums = pl.BlockSpec((1, 1024, 512), lambda j, i: (j, 0, 0))
     return pl.pallas_call(
         functools.partial(table_kernel, pairs, last),
         grid=(2, ids.shape[0] // pairs),
-        in_specs=[pl.BlockSpec((pairs, 1, 2, 128), lambda j, i: (i, j, 0, 0)),
+        in_specs=[pl.BlockSpec((pairs, 2, 1, 16, 128), lambda j, i: (i, 0, j, 4, 0)),
                   pl.BlockSpec((pairs, 2, 1, 64, 128), lambda j, i: (i, 0, j, 0, 0))] + ([sums] if last else []),
         out_specs=pl.BlockSpec((8, 1, 512, 128), lambda j, i: (0, j, 0, 0)) if last else sums,
         out_shape=jax.ShapeDtypeStruct((8, 2, 512, 128), BF) if last else jax.ShapeDtypeStruct((2, 1024, 512), F32),
         scratch_shapes=[pltpu.VMEM((1024, 512), F32)] if last else [],
-        compiler_params=pltpu.CompilerParams(vmem_limit_bytes=48 << 20),
+        compiler_params=pltpu.CompilerParams(vmem_limit_bytes=VMEM_BYTES),
         cost_estimate=pl.CostEstimate(flops=9 * 10**9, bytes_accessed=5 << 20, transcendentals=0),
         name="table_last" if last else "table_first",
     )(*([ids, bags] + ([start] if last else [])))
@@ -258,20 +286,17 @@
     batch = pooled.shape[0] // 2
     scale = float(batch * 512) ** (-0.5)
     core = lax.axis_index("c").astype(jnp.int32).reshape(1)
-    ids = jnp.take(jnp.transpose(bag_row_index, (1, 2, 0)), feature_map, axis=0)
-    ids = lax.all_to_all(ids, PLANE, 0, 0, tiled=True)
+    ids = jnp.transpose(bag_row_index, (1, 2, 0))
     swap = [(0, 1), (1, 0)]
 
     def layer(part):
-        return layer_call(part, batch, feature_map, core, pooled, cotangent, projection, w_up, w_down, w_compress,
-                          ln_gain.reshape(1, 128), scale)
+        return layer_call(part, batch, feature_map, core, pooled, ids if part == 0 else None, cotangent,
+                          projection.T, w_up, w_down, w_compress, ln_gain.reshape(1, 128), scale)
 
     def exchange(bag):
         return lax.all_to_all(bag, PLANE, 0, 0, tiled=True)
 
     bag0, keep0, send0, tail0 = layer(0)
-    bag0, ids = lax.optimization_barrier((bag0, ids))
-    ids = jnp.transpose(ids.reshape(16, 2, 2, 2, 2, batch), (4, 0, 2, 3, 1, 5)).reshape(2, 16, 2, 2, 128)
     first = exchange(bag0)
     bag1, keep1, send1, tail1 = layer(1)
     send1, first = lax.optimization_barrier((send1, first))
@@ -280,8 +305,9 @@
     bag1, weights = lax.optimization_barrier((bag1, weights))
     weights = lax.psum_scatter(weights.reshape(8 * 336, 512), ("zh", "zl"), scatter_dimension=0, tiled=True)
     second = exchange(bag1)
-    rows = table_call(ids[0], first.reshape(16, 2, 2, batch, 128))
-    rows = table_call(ids[1], second.reshape(16, 2, 2, batch, 128), rows)
+    first = first.reshape(16, 2, 2, batch + 16, 128)
+    rows = table_call(first, first)
+    rows = table_call(first, second.reshape(16, 2, 2, batch, 128), rows)
     weights, _ = lax.optimization_barrier((weights, rows))
     rows = lax.psum_scatter(rows.reshape(8192, 128), ("zh", "zl"), scatter_dimension=0, tiled=True)
     pieces = jnp.concatenate(

time: 184 us -> 166 us (0.902)
  local copies, waits for them, and re-layouts: 24.1 us -> 7.91 us
  waiting for transfers between devices: 22.7 us -> 31.6 us
  starting transfers between devices: 51 us -> 42.5 us
  other arithmetic: 3.14 us -> 1.01 us
    unnamed x46 -> x13, local copies, waits for them, and re-layouts: 18.2 us -> 3.1 us
    all_to_all x1 -> x0, starting transfers between devices: 7.88 us -> none  [shards(): ids = lax.all_to_all(ids, PLANE, 0, 0, tiled=True)]
    all_to_all x2, waiting for transfers between devices: 2.04 us -> 8.45 us  [exchange(): return lax.all_to_all(bag, PLANE, 0, 0, tiled=True)]
    reduce_scatter x1, waiting for transfers between devices: 5.35 us -> 7.45 us  [shards(): lax.psum_scatter(weights.reshape(8 * 336, 512), ('zh', 'zl'), scatter_dim...]
  transfers between devices with their start and end apart: 11 -> 10, of which waited for: 6 -> 7; matrix products, arithmetic and copies ran while one was open for 4% -> 3% of each run, Pallas kernels for 27% -> 22%
where the time goes in v4:
time: 166 us; the launch traced here: 164 us
  Pallas kernels  53 us (32%)
  starting transfers between devices  42.5 us (26%)
  waiting for transfers between devices  31.6 us (19%)
  between operations  14.2 us (9%)
  blocking collectives  14 us (8%)
  local copies, waits for them, and re-layouts  7.91 us (5%)
    pallas_call x2, Pallas kernels, table_call(): pl.pallas_call(functools.partial(table_kernel, pairs, last), grid=(2, ids...  24.3 us
    pallas_call x2, Pallas kernels, layer_call(): pl.pallas_call(functools.partial(layer_kernel, scale, batch, part, int(wi...  24.3 us
    all_to_all x1, blocking collectives, shards(): pieces = lax.all_to_all(pieces, ('y', 'x'), 0, 0, tiled=True)  14 us
    all_to_all x2, starting transfers between devices, exchange(): return lax.all_to_all(bag, PLANE, 0, 0, tiled=True)  14 us
    ppermute x1, starting transfers between devices, shards(): lax.ppermute(rows, ('zh', 'c'), [(0, 0), (1, 2), (2, 1), (3, 3)])  9.56 us
    all_to_all x2, waiting for transfers between devices, exchange(): return lax.all_to_all(bag, PLANE, 0, 0, tiled=True)  8.45 us
    reduce_scatter x1, waiting for transfers between devices, shards(): lax.psum_scatter(weights.reshape(8 * 336, 512), ('zh', 'zl'), scatter_dim...  7.45 us
    ppermute x1, waiting for transfers between devices, shards(): lax.ppermute(rows, ('zh', 'c'), [(0, 0), (1, 2), (2, 1), (3, 3)])  6.57 us
  transfers between devices with their start and end apart: 10, of which 7 were waited for; matrix products, arithmetic and copies ran while one was open for 3% of the time, Pallas kernels for 22%

profile of v4, /device:TPU:7, one launch (start us, length us, event | category | flops | bytes accessed | tf_op | source)
XLA Modules:
  0.0 164.3 jit_solution(345374082005359808)
XLA Ops:
  7.2 12.3 %layer_first.1 = (bf16[64,80,128]{2,1,0:T(8,128)(2,1)}, bf16[64,5376]{1,0:T(8,128)(2,1)}, bf16[64,5376]{1,0:T(8,128)(2,1)}, f32[64,128]{1,0:T(8,128)}) custom-call(s32[64]{0:T(128)} %refs_0_.3, s32[1]{0:T(128)} %bitcast.refs_1_, bf16[128,64,128]{2,1,0:T(8,128)(2,1)} %refs_2_.3, s32[64,2,128]{2,1,0:T(2,128)} %bitcast.43, bf16[128,64,128]{2,1,0:T(8,128)(2,1)} %refs_4_.1, ...), custom_call_target="tpu_custom_call" | custom-call | flops 15000000512 | bytes 10485760 | tf_op jit(solution)/shard_map/layer_first/pallas_call | solution.py:154
  19.5 8.0 %all-to-all-start = ((bf16[64,80,128]{2,1,0:T(8,128)(2,1)}), bf16[64,80,128]{2,1,0:T(8,128)(2,1)S(1)}, u32[]{:S(2)}, u32[]{:S(2)}) async-start(bf16[64,80,128]{2,1,0:T(8,128)(2,1)} %get-tuple-element.26), calls=%async_computation | async-start | bytes 2621440 | tf_op jit(solution)/shard_map/all_to_all | solution.py:297
  27.6 0.6 collective-permute-start
  28.2 12.0 %layer_second.1 = (bf16[64,64,128]{2,1,0:T(8,128)(2,1)}, bf16[64,5376]{1,0:T(8,128)(2,1)}, bf16[64,5376]{1,0:T(8,128)(2,1)}, f32[64,128]{1,0:T(8,128)}) custom-call(s32[64]{0:T(128)} %refs_0_.3, s32[1]{0:T(128)} %bitcast.refs_1_, bf16[128,64,128]{2,1,0:T(8,128)(2,1)} %refs_2_.3, bf16[128,64,128]{2,1,0:T(8,128)(2,1)} %refs_4_.1, bf16[16,64]{1,0:T(8,128)(2,1)} %bitcast.45, ...), custom_call_target="tpu_custom_call" | custom-call | flops 15000000512 | bytes 10485760 | tf_op jit(solution)/shard_map/layer_second/pallas_call | solution.py:154
  40.2 5.4 %all-to-all-done = bf16[64,80,128]{2,1,0:T(8,128)(2,1)S(1)} async-done(((bf16[64,80,128]{2,1,0:T(8,128)(2,1)}), bf16[64,80,128]{2,1,0:T(8,128)(2,1)S(1)}, u32[]{:S(2)}, u32[]{:S(2)}) %all-to-all-start) | async-done | bytes 1310752 | tf_op jit(solution)/shard_map/all_to_all | solution.py:297
  45.6 2.3 %collective-permute-done.1.b1_ref = bf16[64,5376]{1,0:T(8,128)(2,1)S(1)} collective-permute-done((bf16[64,5376]{1,0:T(8,128)(2,1)}, bf16[64,5376]{1,0:T(8,128)(2,1)S(1)}, u32[]{:S(2)}, u32[]{:S(2)}) %collective-permute-start.1) | collective-permute-done | bytes 688160 | tf_op jit(solution)/shard_map/ppermute | solution.py:303
  48.0 0.9 copy-done.4
  48.8 4.4 %weight_grads.1 = bf16[8,336,512]{2,1,0:T(8,128)(2,1)} custom-call(bf16[64,5376]{1,0:T(8,128)(2,1)} %get-tuple-element.29.a0_ref, bf16[64,5376]{1,0:T(8,128)(2,1)} %copy-done.3, bf16[64,5376]{1,0:T(8,128)(2,1)} %get-tuple-element.31.a1_ref, bf16[64,5376]{1,0:T(8,128)(2,1)} %copy-done.4, f32[64,128]{1,0:T(8,128)} %get-tuple-element.33.tail0_ref, ...), custom_call_target="tpu_custom_call" | custom-call | flops 3000000000 | bytes 6291456 | tf_op jit(solution)/shard_map/weight_grads/pallas_call | solution.py:197
  53.3 6.0 %all-to-all-start.1 = ((bf16[64,64,128]{2,1,0:T(8,128)(2,1)}), bf16[64,64,128]{2,1,0:T(8,128)(2,1)S(1)}, u32[]{:S(2)}, u32[]{:S(2)}) async-start(bf16[64,64,128]{2,1,0:T(8,128)(2,1)} %get-tuple-element.35), calls=%async_computation.1 | async-start | bytes 2097152 | tf_op jit(solution)/shard_map/all_to_all | solution.py:297
  59.5 11.9 %table_first.1.refs_2_ = f32[2,1024,512]{2,1,0:T(8,128)} custom-call(bf16[16,2,2,80,128]{4,3,2,1,0:T(8,128)(2,1)} %bitcast.32, bf16[16,2,2,80,128]{4,3,2,1,0:T(8,128)(2,1)} %bitcast.33), custom_call_target="tpu_custom_call" | custom-call | flops 8999999488 | bytes 5242880 | tf_op jit(solution)/shard_map/table_first/pallas_call | solution.py:254
  71.5 3.1 %all-to-all-done.1 = bf16[64,64,128]{2,1,0:T(8,128)(2,1)S(1)} async-done(((bf16[64,64,128]{2,1,0:T(8,128)(2,1)}), bf16[64,64,128]{2,1,0:T(8,128)(2,1)S(1)}, u32[]{:S(2)}, u32[]{:S(2)}) %all-to-all-start.1) | async-done | bytes 1048608 | tf_op jit(solution)/shard_map/all_to_all | solution.py:297
  74.5 1.0 copy-done.1
  75.5 12.4 %table_last.1 = bf16[8,2,512,128]{3,2,1,0:T(8,128)(2,1)} custom-call(bf16[16,2,2,80,128]{4,3,2,1,0:T(8,128)(2,1)} %bitcast.34, bf16[16,2,2,64,128]{4,3,2,1,0:T(8,128)(2,1)} %bitcast.35, f32[2,1024,512]{2,1,0:T(8,128)} %table_first.1.refs_2_), custom_call_target="tpu_custom_call" | custom-call | flops 8999999488 | bytes 5242880 | tf_op jit(solution)/shard_map/table_last/pallas_call | solution.py:254
  87.9 7.4 %reduce-scatter.5.cloned.1.call-done = bf16[336,512]{1,0:T(8,128)(2,1)} async-done(((bf16[2688,512]{1,0:T(8,128)(2,1)}), bf16[336,512]{1,0:T(8,128)(2,1)}) %reduce-scatter.5.cloned.1.call-update) | async-done | bytes 344080 | tf_op jit(solution)/shard_map/reduce_scatter | solution.py:306
  95.3 0.7 slice.29
  96.1 0.8 slice.27
  96.9 1.0 slice.28
  98.2 0.3 copy.25
  98.5 14.0 %all_to_all.15 = bf16[16,36,512]{2,1,0:T(8,128)(2,1)S(1)} all-to-all(bf16[16,36,512]{2,1,0:T(8,128)(2,1)S(1)} %copy.25), channel_id=1, replica_groups=mesh['y'=4,'zh'=2,'x'=4,'zl'=4,'c'=2] {'y','x'}, dimensions={0} | all-to-all | bytes 1179648 | tf_op jit(solution)/shard_map/all_to_all | solution.py:317
  112.7 6.0 %collective-permute-start.4 = (f32[64,128]{1,0:T(8,128)S(1)}, f32[64,128]{1,0:T(8,128)S(1)}, u32[]{:S(2)}, u32[]{:S(2)}) collective-permute-start(f32[64,128]{1,0:T(8,128)S(1)} %bitcast.39), channel_id=1, source_target_pairs={{0,1},{1,0},{2,3},{3,2},{4,5},{5,4},{6,7},{7,6},{8,9},{9,8},{10,11... | collective-permute-start | bytes 98312 | tf_op jit(solution)/shard_map/ppermute | solution.py:323
  118.7 6.0 %collective-permute-start.2 = (f32[4,512]{1,0:T(4,128)S(1)}, f32[4,512]{1,0:T(4,128)S(1)}, u32[]{:S(2)}, u32[]{:S(2)}) collective-permute-start(f32[4,512]{1,0:T(4,128)S(1)} %slice.36), channel_id=1, source_target_pairs={{0,0},{1,2},{2,32},{3,34},{4,64},{5,66},{6,96},{7,98},{8,1},{9,3},... | collective-permute-start | bytes 24584 | tf_op jit(solution)/shard_map/ppermute | solution.py:320
  124.7 6.0 %collective-permute-start.3 = (f32[16,512]{1,0:T(8,128)S(1)}, f32[16,512]{1,0:T(8,128)S(1)}, u32[]{:S(2)}, u32[]{:S(2)}) collective-permute-start(f32[16,512]{1,0:T(8,128)S(1)} %get-tuple-element.45), channel_id=1, source_target_pairs={{0,0},{1,128},{2,16},{3,144},{4,32},{5,160},{6,48},{7,176},{8,1},{... | collective-permute-start | bytes 98312 | tf_op jit(solution)/shard_map/ppermute | solution.py:321
  130.8 0.6 slice_bitcast_fusion.1
  131.4 0.5 slice_bitcast_fusion.2
  131.9 0.6 slice.40
  132.5 2.9 %collective-permute-done.3 = f32[16,512]{1,0:T(8,128)S(1)} collective-permute-done((f32[16,512]{1,0:T(8,128)S(1)}, f32[16,512]{1,0:T(8,128)S(1)}, u32[]{:S(2)}, u32[]{:S(2)}) %collective-permute-start.3) | collective-permute-done | bytes 32800 | tf_op jit(solution)/shard_map/ppermute | solution.py:321
  135.4 0.6 copy.29
  136.1 3.9 %reduce-scatter.3.cloned.1.call-done = bf16[1024,128]{1,0:T(8,128)(2,1)} async-done(((bf16[8192,128]{1,0:T(8,128)(2,1)}), bf16[1024,128]{1,0:T(8,128)(2,1)}) %reduce-scatter.3.cloned.1.call-update) | async-done | bytes 262160 | tf_op jit(solution)/shard_map/reduce_scatter | solution.py:312
  139.9 9.6 %collective-permute-start.5 = (bf16[1024,128]{1,0:T(8,128)(2,1)}, bf16[1024,128]{1,0:T(8,128)(2,1)S(1)}, u32[]{:S(2)}, u32[]{:S(2)}) collective-permute-start(bf16[1024,128]{1,0:T(8,128)(2,1)} %reduce-scatter.3.cloned.1.call-done), channel_id=1, source_target_pairs={{0,0},{1,32},{32,1},{33,33},{2,2},{3,34},{34,3},{35,35},{4,4},{5,3... | collective-permute-start | bytes 786440 | tf_op jit(solution)/shard_map/ppermute | solution.py:326
  149.5 6.6 %collective-permute-done.5 = bf16[1024,128]{1,0:T(8,128)(2,1)S(1)} collective-permute-done((bf16[1024,128]{1,0:T(8,128)(2,1)}, bf16[1024,128]{1,0:T(8,128)(2,1)S(1)}, u32[]{:S(2)}, u32[]{:S(2)}) %collective-permute-start.5) | collective-permute-done | bytes 262176 | tf_op jit(solution)/shard_map/ppermute | solution.py:326
  156.1 0.8 convert.1
  156.9 0.6 copy.35
  (29 shorter events, 0.8 us)
Async XLA Ops:
  19.5 8.1 %copy-start.2 = (bf16[64,5376]{1,0:T(8,128)(2,1)S(1)}, bf16[64,5376]{1,0:T(8,128)(2,1)}, u32[]{:S(2)}) copy-start(bf16[64,5376]{1,0:T(8,128)(2,1)} %get-tuple-element.30) | copy-start | bytes 2064388
  19.5 26.1 %all-to-all-start = ((bf16[64,80,128]{2,1,0:T(8,128)(2,1)}), bf16[64,80,128]{2,1,0:T(8,128)(2,1)S(1)}, u32[]{:S(2)}, u32[]{:S(2)}) async-start(bf16[64,80,128]{2,1,0:T(8,128)(2,1)} %get-tuple-element.26), calls=%async_computation | async-start | bytes 2621440 | tf_op jit(solution)/shard_map/all_to_all | solution.py:297
  27.5 67.8 %reduce-scatter.5.cloned.1.call-start = ((), (), s32[]{:S(2)}) async-start(), calls=%async_computation.6 | async-start | bytes 3096576 | tf_op jit(solution)/shard_map/reduce_scatter | solution.py:306
  27.6 18.0 %collective-permute-start = (bf16[64,5376]{1,0:T(8,128)(2,1)S(1)}, bf16[64,5376]{1,0:T(8,128)(2,1)S(1)}, u32[]{:S(2)}, u32[]{:S(2)}) collective-permute-start(bf16[64,5376]{1,0:T(8,128)(2,1)S(1)} %copy-done.2), channel_id=1, source_target_pairs={{0,1},{1,0},{2,3},{3,2},{4,5},{5,4},{6,7},{7,6},{8,9},{9,8},{10,11... | collective-permute-start | bytes 2064392 | tf_op jit(solution)/shard_map/ppermute | solution.py:303
  45.6 7.6 %copy-start = (bf16[64,80,128]{2,1,0:T(8,128)(2,1)}, bf16[64,80,128]{2,1,0:T(8,128)(2,1)S(1)}, u32[]{:S(2)}) copy-start(bf16[64,80,128]{2,1,0:T(8,128)(2,1)S(1)} %all-to-all-done) | copy-start | bytes 3932164
  45.6 2.4 %collective-permute-start.1 = (bf16[64,5376]{1,0:T(8,128)(2,1)}, bf16[64,5376]{1,0:T(8,128)(2,1)S(1)}, u32[]{:S(2)}, u32[]{:S(2)}) collective-permute-start(bf16[64,5376]{1,0:T(8,128)(2,1)} %get-tuple-element.32), channel_id=1, source_target_pairs={{0,1},{1,0},{2,3},{3,2},{4,5},{5,4},{6,7},{7,6},{8,9},{9,8},{10,11... | collective-permute-start | bytes 2064392 | tf_op jit(solution)/shard_map/ppermute | solution.py:303
  45.6 2.4 %copy-start.3 = (bf16[64,5376]{1,0:T(8,128)(2,1)}, bf16[64,5376]{1,0:T(8,128)(2,1)S(1)}, u32[]{:S(2)}) copy-start(bf16[64,5376]{1,0:T(8,128)(2,1)S(1)} %collective-permute-done.b0_ref) | copy-start | bytes 2064388
  48.0 0.9 copy-start.4
  53.3 21.3 %all-to-all-start.1 = ((bf16[64,64,128]{2,1,0:T(8,128)(2,1)}), bf16[64,64,128]{2,1,0:T(8,128)(2,1)S(1)}, u32[]{:S(2)}, u32[]{:S(2)}) async-start(bf16[64,64,128]{2,1,0:T(8,128)(2,1)} %get-tuple-element.35), calls=%async_computation.1 | async-start | bytes 2097152 | tf_op jit(solution)/shard_map/all_to_all | solution.py:297
  59.2 80.7 %reduce-scatter.3.cloned.1.call-start = ((), (), s32[]{:S(2)}) async-start(), calls=%async_computation.5 | async-start | bytes 2359296 | tf_op jit(solution)/shard_map/reduce_scatter | solution.py:312
  74.5 1.0 copy-start.1
  112.7 18.0 %collective-permute-start.4 = (f32[64,128]{1,0:T(8,128)S(1)}, f32[64,128]{1,0:T(8,128)S(1)}, u32[]{:S(2)}, u32[]{:S(2)}) collective-permute-start(f32[64,128]{1,0:T(8,128)S(1)} %bitcast.39), channel_id=1, source_target_pairs={{0,1},{1,0},{2,3},{3,2},{4,5},{5,4},{6,7},{7,6},{8,9},{9,8},{10,11... | collective-permute-start | bytes 98312 | tf_op jit(solution)/shard_map/ppermute | solution.py:323
  118.7 21.2 %collective-permute-start.2 = (f32[4,512]{1,0:T(4,128)S(1)}, f32[4,512]{1,0:T(4,128)S(1)}, u32[]{:S(2)}, u32[]{:S(2)}) collective-permute-start(f32[4,512]{1,0:T(4,128)S(1)} %slice.36), channel_id=1, source_target_pairs={{0,0},{1,2},{2,32},{3,34},{4,64},{5,66},{6,96},{7,98},{8,1},{9,3},... | collective-permute-start | bytes 24584 | tf_op jit(solution)/shard_map/ppermute | solution.py:320
  124.7 10.7 %collective-permute-start.3 = (f32[16,512]{1,0:T(8,128)S(1)}, f32[16,512]{1,0:T(8,128)S(1)}, u32[]{:S(2)}, u32[]{:S(2)}) collective-permute-start(f32[16,512]{1,0:T(8,128)S(1)} %get-tuple-element.45), channel_id=1, source_target_pairs={{0,0},{1,128},{2,16},{3,144},{4,32},{5,160},{6,48},{7,176},{8,1},{... | collective-permute-start | bytes 98312 | tf_op jit(solution)/shard_map/ppermute | solution.py:321
  139.9 16.1 %collective-permute-start.5 = (bf16[1024,128]{1,0:T(8,128)(2,1)}, bf16[1024,128]{1,0:T(8,128)(2,1)S(1)}, u32[]{:S(2)}, u32[]{:S(2)}) collective-permute-start(bf16[1024,128]{1,0:T(8,128)(2,1)} %reduce-scatter.3.cloned.1.call-done), channel_id=1, source_target_pairs={{0,0},{1,32},{32,1},{33,33},{2,2},{3,34},{34,3},{35,35},{4,4},{5,3... | collective-permute-start | bytes 786440 | tf_op jit(solution)/shard_map/ppermute | solution.py:326
Sparse Core Ops, SparseCore 0:
  53.4 41.9 reduce-scatter.4
  98.1 41.8 reduce-scatter.2

commit v5 on v4

--- a/solution.py
+++ b/solution.py
@@ -141,8 +141,8 @@
                 bags_ref[inv_ref[n * 8 + i], g * 16:(g + 1) * 16, :] = v.astype(BF)
     gsm = dot_nt(jnp.concatenate(tails, axis=1), xcat)
     tail_ref[...] = jnp.concatenate([
-        jnp.concatenate([gsm, jnp.zeros((48, 64), F32)], axis=1),
-        jnp.broadcast_to(jnp.sum(gg, axis=0, keepdims=True), (16, 128))], axis=0) * scale
+        jnp.concatenate([gsm[0:24], gsm[24:48]], axis=1),
+        jnp.broadcast_to(jnp.sum(gg, axis=0, keepdims=True), (8, 128))], axis=0) * scale
 
 
 def layer_call(part, batch, feature_map, core, pooled, ids, cotangent, projt, w_up, w_down, w_compress, gain, scale):
@@ -157,11 +157,11 @@
         in_specs=[scalars, scalars, pl.BlockSpec((batch, 64, 128), lambda i: (part, 0, 0))]
         + ([full(64, 2, 128)] if with_ids else [])
         + [far, full(16, 64), far, far, full(32, 64), full(1, 128)],
-        out_specs=[full(64, depth, 128), full(batch, 5376), full(batch, 5376), full(64, 128)],
+        out_specs=[full(64, depth, 128), full(batch, 5376), full(batch, 5376), full(32, 128)],
         out_shape=[jax.ShapeDtypeStruct((64, depth, 128), BF),
                    jax.ShapeDtypeStruct((batch, 5376), BF),
                    jax.ShapeDtypeStruct((batch, 5376), BF),
-                   jax.ShapeDtypeStruct((64, 128), F32)],
+                   jax.ShapeDtypeStruct((32, 128), F32)],
         scratch_shapes=[pltpu.SMEM((64,), jnp.int32),
                         pltpu.VMEM((32, batch, 128), F32), pltpu.VMEM((batch, 32, 128), F32),
                         pltpu.VMEM((1024, 128), F32), pltpu.VMEM((1024, 512), BF),
@@ -177,26 +177,27 @@
 def weight_kernel(scale, a0_ref, b0_ref, a1_ref, b1_ref, tail0_ref, tail1_ref, w_ref, gus):
     acts = jnp.concatenate([a0_ref[...], b0_ref[...], a1_ref[...], b1_ref[...]], axis=0)
     tail = tail0_ref[...] + tail1_ref[...]
-    tail = jnp.concatenate([tail[q * 16:(q + 1) * 16, :] for q in range(4)], axis=1).astype(BF)
+    tail = jnp.concatenate([tail[q * 8:(q + 1) * 8, :] for q in range(4)], axis=1)
+    tail = jnp.concatenate([tail, jnp.zeros((8, 512), F32)], axis=0).astype(BF)
     up = dot_tn(acts[:, 0:512], acts[:, 512:1024]) * scale
     for q in range(4):
         for k in range(8):
             gus[pl.ds(k, 64, stride=8), :] = up[k * 64:(k + 1) * 64, q * 128:(q + 1) * 128]
-        for z in range(8):
-            w_ref[z, 0:64, q * 128:(q + 1) * 128] = gus[z * 64:(z + 1) * 64, :].astype(BF)
+        for z in range(4):
+            w_ref[z, 0:128, q * 128:(q + 1) * 128] = gus[z * 128:(z + 1) * 128, :].astype(BF)
     hid = acts[:, 1024:1280]
     for q in range(8):
         down = (dot_tn(hid, acts[:, 1280 + q * 512:1792 + q * 512]) * scale).astype(BF)
-        for z in range(8):
-            w_ref[z, 64 + q * 32:96 + q * 32, :] = down[z * 32:(z + 1) * 32, :]
-    for z in range(8):
-        w_ref[z, 320:336, :] = tail
+        for z in range(4):
+            w_ref[z, 128 + q * 64:192 + q * 64, :] = down[z * 64:(z + 1) * 64, :]
+    for z in range(4):
+        w_ref[z, 640:656, :] = tail
 
 
 def weight_call(acts, tails, scale):
     return pl.pallas_call(
         functools.partial(weight_kernel, scale),
-        out_shape=jax.ShapeDtypeStruct((8, 336, 512), BF),
+        out_shape=jax.ShapeDtypeStruct((4, 656, 512), BF),
         scratch_shapes=[pltpu.VMEM((512, 128), F32)],
         compiler_params=pltpu.CompilerParams(vmem_limit_bytes=VMEM_BYTES),
         cost_estimate=pl.CostEstimate(flops=3 * 10**9, bytes_accessed=6 << 20, transcendentals=0),
@@ -204,13 +205,13 @@
     )(*acts, *tails)
 
 
-def table_kernel(pairs, last, *refs):
+def table_kernel(pairs, group, parts, last, *refs):
+    span = 4096 // parts
     if last:
         ids_ref, bags_ref, start_ref, out_ref, acc = refs
     else:
         ids_ref, bags_ref, acc = refs
         acc = acc.at[0]
-    step = pl.program_id(1)
     side = slice(64, 128) if last else slice(0, 64)
     ids = []
     for i in range(pairs):
@@ -218,47 +219,42 @@
         codes = codes[:, 0:2] + 256.0 * codes[:, 2:4]
         ids.append(jnp.concatenate([codes[0][:, side], codes[1][:, side]], axis=1))
     ids = jnp.concatenate(ids, axis=0).astype(jnp.int32)
-    low = jnp.transpose(lax.shift_right_logical(ids, 10).astype(F32), (1, 0))
-    high = jnp.bitwise_and(ids, 1023).astype(jnp.int16)
-    iota = lax.broadcasted_iota(jnp.int16, (1024, 128), 0)
-    left, right = [], []
-    for i in range(pairs):
-        values = bags_ref[i, :, 0].reshape(128, 128)
-        for t in range(2):
-            r = 2 * i + t
-            left.append(jnp.where(iota == high[r:r + 1, :], jnp.bfloat16(1), jnp.bfloat16(0)))
-            column = jnp.broadcast_to(low[:, r:r + 1], (128, 128)).astype(BF)
-            right.append(jnp.concatenate(
-                [jnp.where(column == jnp.bfloat16(q), values, jnp.bfloat16(0)) for q in range(4)], axis=1))
-    part = jnp.dot(jnp.concatenate(left, axis=1), jnp.concatenate(right, axis=0), preferred_element_type=F32)
-
-    @pl.when(step == 0)
-    def _():
-        acc[...] = start_ref[0] + part if last else part
-
-    @pl.when(step > 0)
-    def _():
-        acc[...] += part
+    low = jnp.transpose(lax.shift_right_logical(ids, span.bit_length() - 1).astype(F32), (1, 0))
+    high = jnp.bitwise_and(ids, span - 1).astype(jnp.int16)
+    iota = lax.broadcasted_iota(jnp.int16, (span, 128), 0)
+    for g in range(pairs // group):
+        left, right = [], []
+        for i in range(g * group, (g + 1) * group):
+            values = bags_ref[i, :, 0].reshape(128, 128)
+            for t in range(2):
+                r = 2 * i + t
+                left.append(jnp.where(iota == high[r:r + 1, :], jnp.bfloat16(1), jnp.bfloat16(0)))
+                column = jnp.broadcast_to(low[:, r:r + 1], (128, 128)).astype(BF)
+                right.append(jnp.concatenate(
+                    [jnp.where(column == jnp.bfloat16(q), values, jnp.bfloat16(0)) for q in range(parts)], axis=1))
+        part = jnp.dot(jnp.concatenate(left, axis=1), jnp.concatenate(right, axis=0), preferred_element_type=F32)
+        if g == 0:
+            acc[...] = start_ref[0] + part if last else part
+        else:
+            acc[...] += part
 
     if last:
-        @pl.when(step == pl.num_programs(1) - 1)
-        def _():
-            for q in range(4):
-                for h in range(2):
-                    out_ref[h * 4 + q, 0] = acc[h * 512:(h + 1) * 512, q * 128:(q + 1) * 128].astype(BF)
-
-
-def table_call(ids, bags, start=None, pairs=16):
+        for p in range(8):
+            q, h = p // (8 // parts), p % (8 // parts)
+            out_ref[(p % 2) * 4 + p // 2, 0] = acc[h * 512:(h + 1) * 512, q * 128:(q + 1) * 128].astype(BF)
+
+
+def table_call(ids, bags, start=None, pairs=16, group=4, parts=4):
     last = start is not None
-    sums = pl.BlockSpec((1, 1024, 512), lambda j, i: (j, 0, 0))
+    sums = pl.BlockSpec((1, 4096 // parts, 128 * parts), lambda j, i: (j, 0, 0))
     return pl.pallas_call(
-        functools.partial(table_kernel, pairs, last),
+        functools.partial(table_kernel, pairs, group, parts, last),
         grid=(2, ids.shape[0] // pairs),
         in_specs=[pl.BlockSpec((pairs, 2, 1, 16, 128), lambda j, i: (i, 0, j, 4, 0)),
                   pl.BlockSpec((pairs, 2, 1, 64, 128), lambda j, i: (i, 0, j, 0, 0))] + ([sums] if last else []),
         out_specs=pl.BlockSpec((8, 1, 512, 128), lambda j, i: (0, j, 0, 0)) if last else sums,
-        out_shape=jax.ShapeDtypeStruct((8, 2, 512, 128), BF) if last else jax.ShapeDtypeStruct((2, 1024, 512), F32),
-        scratch_shapes=[pltpu.VMEM((1024, 512), F32)] if last else [],
+        out_shape=jax.ShapeDtypeStruct((8, 2, 512, 128), BF) if last else jax.ShapeDtypeStruct((2, 4096 // parts, 128 * parts), F32),
+        scratch_shapes=[pltpu.VMEM((4096 // parts, 128 * parts), F32)] if last else [],
         compiler_params=pltpu.CompilerParams(vmem_limit_bytes=VMEM_BYTES),
         cost_estimate=pl.CostEstimate(flops=9 * 10**9, bytes_accessed=5 << 20, transcendentals=0),
         name="table_last" if last else "table_first",
@@ -276,9 +272,9 @@
     up, down = [], []
     for d in range(256):
         y, zh, x, zl, c = (d // 64, d // 32 % 2, d // 8 % 4, d // 2 % 4, d % 2)
-        z, sub = zh * 4 + zl, y * 4 + x
-        up.append((d, z * 32 + (sub // 2) * 4 + 2 * c + sub % 2))
-        down.append((d, c * 128 + z * 16 + sub))
+        unit = zl * 32 + (y * 2 + zh) * 4 + x
+        up.append((d, (unit // 2) * 4 + 2 * c + unit % 2))
+        down.append((d, c * 128 + unit))
     return up, down
 
 
@@ -299,11 +295,10 @@
     bag0, keep0, send0, tail0 = layer(0)
     first = exchange(bag0)
     bag1, keep1, send1, tail1 = layer(1)
-    send1, first = lax.optimization_barrier((send1, first))
     acts = (keep0, lax.ppermute(send0, "c", swap), keep1, lax.ppermute(send1, "c", swap))
     weights = weight_call(acts, (tail0, tail1), scale)
-    bag1, weights = lax.optimization_barrier((bag1, weights))
-    weights = lax.psum_scatter(weights.reshape(8 * 336, 512), ("zh", "zl"), scatter_dimension=0, tiled=True)
+    bag1, weights, first = lax.optimization_barrier((bag1, weights, first))
+    weights = lax.psum_scatter(weights.reshape(4 * 656, 512), "zl", scatter_dimension=0, tiled=True)
     second = exchange(bag1)
     first = first.reshape(16, 2, 2, batch + 16, 128)
     rows = table_call(first, first)
@@ -311,17 +306,18 @@
     weights, _ = lax.optimization_barrier((weights, rows))
     rows = lax.psum_scatter(rows.reshape(8192, 128), ("zh", "zl"), scatter_dimension=0, tiled=True)
     pieces = jnp.concatenate(
-        [weights[0:64].reshape(16, 4, 512),
-         weights[64:320].reshape(8, 16, 2, 512).transpose(1, 0, 2, 3).reshape(16, 16, 512),
-         jnp.broadcast_to(weights[320:336], (16, 16, 512))], axis=1)
-    pieces = lax.all_to_all(pieces, ("y", "x"), 0, 0, tiled=True)
+        [weights[0:128].reshape(32, 4, 512),
+         weights[128:640].reshape(8, 32, 2, 512).transpose(1, 0, 2, 3).reshape(32, 16, 512),
+         jnp.broadcast_to(weights[640:648], (32, 8, 512))], axis=1)
+    pieces = lax.all_to_all(pieces, HST, 0, 0, tiled=True)
     total = jnp.sum(pieces.astype(F32), axis=0)
     up_moves, down_moves = weight_moves()
     gu = lax.ppermute(total[0:4], AXES, up_moves)
     gd = lax.ppermute(total[4:20], AXES, down_moves).reshape(8, 2, 512).transpose(1, 0, 2).reshape(2, 4096)
-    tail = total[20:36].reshape(16, 4, 128).transpose(1, 0, 2).reshape(64, 128)
+    tail = total[20:28].reshape(8, 4, 128).transpose(1, 0, 2).reshape(32, 128)
     tail = tail + lax.ppermute(tail, "c", swap)
-    small = (tail[32:48, :64].T, tail[:32, :64], tail[48])
+    both = jnp.concatenate([tail[0:24, :64], tail[0:24, 64:]], axis=0)
+    small = (both[32:48].T, both[0:32], tail[24])
     rows, gu, gd, small = lax.optimization_barrier((rows, gu, gd, small))
     table_grad = lax.ppermute(rows, ("zh", "c"), [(0, 0), (1, 2), (2, 1), (3, 3)]).astype(F32)
     return (table_grad.reshape(2, 512, 128), gu, gd) + tuple(small)

time: 166 us -> 204 us (1.23)
  blocking collectives: 14 us -> 43.1 us
  waiting for transfers between devices: 31.6 us -> 41.6 us
    all_to_all x1, blocking collectives: 14 us -> 43.1 us  [shards(): pieces = lax.all_to_all(pieces, HST, 0, 0, tiled=True)]
    reduce_scatter x1, waiting for transfers between devices: 7.45 us -> 23.8 us  [shards(): lax.psum_scatter(weights.reshape(4 * 656, 512), 'zl', scatter_dimension=0...]
    all_to_all x2, waiting for transfers between devices: 8.45 us -> 3.05 us  [exchange(): return lax.all_to_all(bag, PLANE, 0, 0, tiled=True)]
    ppermute x1, starting transfers between devices: 6.04 us -> 1.92 us  [shards(): lax.ppermute(total[4:20], AXES, down_moves).reshape(8, 2, 512)]
    reduce_scatter x1, waiting for transfers between devices: 3.88 us -> 0.01 us  [shards(): lax.psum_scatter(rows.reshape(8192, 128), ('zh', 'zl'), scatter_dimension...]
    ppermute x1, starting transfers between devices: 5.99 us -> 8.21 us  [shards(): gu = lax.ppermute(total[0:4], AXES, up_moves)]
    ppermute x1, waiting for transfers between devices: 2.88 us -> 5.02 us  [shards(): lax.ppermute(total[4:20], AXES, down_moves).reshape(8, 2, 512)]
    unnamed x13 -> x12, local copies, waits for them, and re-layouts: 3.1 us -> 4.09 us
  transfers between devices with their start and end apart: 10 -> 10, of which waited for: 7 -> 6; matrix products, arithmetic and copies ran while one was open for 3% -> 2% of each run, Pallas kernels for 22% -> 20%
where the time goes in v5:
time: 204 us
  Pallas kernels  52.9 us (26%)
  blocking collectives  43.1 us (21%)
  starting transfers between devices  42.6 us (21%)
  waiting for transfers between devices  41.6 us (20%)
  between operations  14.2 us (7%)
  local copies, waits for them, and re-layouts  7.37 us (4%)
    all_to_all x1, blocking collectives, shards(): pieces = lax.all_to_all(pieces, HST, 0, 0, tiled=True)  43.1 us
    pallas_call x2, Pallas kernels, table_call(): pl.pallas_call(functools.partial(table_kernel, pairs, group, parts, last)...  24.3 us
    pallas_call x2, Pallas kernels, layer_call(): pl.pallas_call(functools.partial(layer_kernel, scale, batch, part, int(wi...  24.2 us
    reduce_scatter x1, waiting for transfers between devices, shards(): lax.psum_scatter(weights.reshape(4 * 656, 512), 'zl', scatter_dimension=0...  23.8 us
    all_to_all x2, starting transfers between devices, exchange(): return lax.all_to_all(bag, PLANE, 0, 0, tiled=True)  15.3 us
    ppermute x1, starting transfers between devices, shards(): lax.ppermute(rows, ('zh', 'c'), [(0, 0), (1, 2), (2, 1), (3, 3)])  10 us
    ppermute x1, starting transfers between devices, shards(): gu = lax.ppermute(total[0:4], AXES, up_moves)  8.21 us
    ppermute x1, waiting for transfers between devices, shards(): lax.ppermute(rows, ('zh', 'c'), [(0, 0), (1, 2), (2, 1), (3, 3)])  7.1 us
  transfers between devices with their start and end apart: 10, of which 6 were waited for; matrix products, arithmetic and copies ran while one was open for 2% of the time, Pallas kernels for 20%

profile of v5, /device:TPU:7, one launch (start us, length us, event | category | flops | bytes accessed | tf_op | source)
XLA Modules:
  0.0 203.6 jit_solution(4396004606978493689)
XLA Ops:
  7.2 12.2 %layer_first.1 = (bf16[64,80,128]{2,1,0:T(8,128)(2,1)}, bf16[64,5376]{1,0:T(8,128)(2,1)}, bf16[64,5376]{1,0:T(8,128)(2,1)}, f32[32,128]{1,0:T(8,128)}) custom-call(s32[64]{0:T(128)} %refs_0_.3, s32[1]{0:T(128)} %bitcast.refs_1_, bf16[128,64,128]{2,1,0:T(8,128)(2,1)} %refs_2_.3, s32[64,2,128]{2,1,0:T(2,128)} %bitcast.40, bf16[128,64,128]{2,1,0:T(8,128)(2,1)} %refs_4_.1, ...), custom_call_target="tpu_custom_call" | custom-call | flops 15000000512 | bytes 10485760 | tf_op jit(solution)/shard_map/layer_first/pallas_call | solution.py:154
  19.4 7.9 %all-to-all-start = ((bf16[64,80,128]{2,1,0:T(8,128)(2,1)}), bf16[64,80,128]{2,1,0:T(8,128)(2,1)S(1)}, u32[]{:S(2)}, u32[]{:S(2)}) async-start(bf16[64,80,128]{2,1,0:T(8,128)(2,1)} %get-tuple-element.31), calls=%async_computation | async-start | bytes 2621440 | tf_op jit(solution)/shard_map/all_to_all | solution.py:293
  27.3 0.2 reduce-scatter.5.cloned.1.call-start
  27.6 12.0 %layer_second.1 = (bf16[64,64,128]{2,1,0:T(8,128)(2,1)}, bf16[64,5376]{1,0:T(8,128)(2,1)}, bf16[64,5376]{1,0:T(8,128)(2,1)}, f32[32,128]{1,0:T(8,128)}) custom-call(s32[64]{0:T(128)} %refs_0_.3, s32[1]{0:T(128)} %bitcast.refs_1_, bf16[128,64,128]{2,1,0:T(8,128)(2,1)} %refs_2_.3, bf16[128,64,128]{2,1,0:T(8,128)(2,1)} %refs_4_.1, bf16[16,64]{1,0:T(8,128)(2,1)} %bitcast.42, ...), custom_call_target="tpu_custom_call" | custom-call | flops 15000000512 | bytes 10485760 | tf_op jit(solution)/shard_map/layer_second/pallas_call | solution.py:154
  39.5 0.4 collective-permute-start.1
  40.1 1.8 collective-permute-done.1.b1_ref
  42.0 0.8 collective-permute-done.b0_ref
  42.8 0.8 copy-done.4
  43.6 4.4 %weight_grads.1 = bf16[4,656,512]{2,1,0:T(8,128)(2,1)} custom-call(bf16[64,5376]{1,0:T(8,128)(2,1)} %get-tuple-element.25.a0_ref, bf16[64,5376]{1,0:T(8,128)(2,1)} %copy-done.4, bf16[64,5376]{1,0:T(8,128)(2,1)} %get-tuple-element.27.a1_ref, bf16[64,5376]{1,0:T(8,128)(2,1)} %copy-done.3, f32[32,128]{1,0:T(8,128)} %get-tuple-element.29.tail0_ref, ...), custom_call_target="tpu_custom_call" | custom-call | flops 3000000000 | bytes 6291456 | tf_op jit(solution)/shard_map/weight_grads/pallas_call | solution.py:198
  48.0 1.0 copy-done
  49.0 7.4 %all-to-all-start.1 = ((bf16[64,64,128]{2,1,0:T(8,128)(2,1)}), bf16[64,64,128]{2,1,0:T(8,128)(2,1)S(1)}, u32[]{:S(2)}, u32[]{:S(2)}) async-start(bf16[64,64,128]{2,1,0:T(8,128)(2,1)} %get-tuple-element.33), calls=%async_computation.1 | async-start | bytes 2097152 | tf_op jit(solution)/shard_map/all_to_all | solution.py:293
  56.4 0.3 reduce-scatter.3.cloned.1.call-start
  56.7 12.0 %table_first.1.refs_2_ = f32[2,1024,512]{2,1,0:T(8,128)} custom-call(bf16[16,2,2,80,128]{4,3,2,1,0:T(8,128)(2,1)} %bitcast.33, bf16[16,2,2,80,128]{4,3,2,1,0:T(8,128)(2,1)} %bitcast.34), custom_call_target="tpu_custom_call" | custom-call | flops 8999999488 | bytes 5242880 | tf_op jit(solution)/shard_map/table_first/pallas_call | solution.py:250
  68.6 3.0 %all-to-all-done.1 = bf16[64,64,128]{2,1,0:T(8,128)(2,1)S(1)} async-done(((bf16[64,64,128]{2,1,0:T(8,128)(2,1)}), bf16[64,64,128]{2,1,0:T(8,128)(2,1)S(1)}, u32[]{:S(2)}, u32[]{:S(2)}) %all-to-all-start.1) | async-done | bytes 1048608 | tf_op jit(solution)/shard_map/all_to_all | solution.py:293
  71.7 1.0 copy-done.1
  72.7 12.3 %table_last.1 = bf16[8,2,512,128]{3,2,1,0:T(8,128)(2,1)} custom-call(bf16[16,2,2,80,128]{4,3,2,1,0:T(8,128)(2,1)} %bitcast.35, bf16[16,2,2,64,128]{4,3,2,1,0:T(8,128)(2,1)} %bitcast.36, f32[2,1024,512]{2,1,0:T(8,128)} %table_first.1.refs_2_), custom_call_target="tpu_custom_call" | custom-call | flops 8999999488 | bytes 5242880 | tf_op jit(solution)/shard_map/table_last/pallas_call | solution.py:250
  85.0 23.8 %reduce-scatter.5.cloned.1.call-done = bf16[656,512]{1,0:T(8,128)(2,1)} async-done(((bf16[2624,512]{1,0:T(8,128)(2,1)}), bf16[656,512]{1,0:T(8,128)(2,1)}) %reduce-scatter.5.cloned.1.call-update) | async-done | bytes 671760 | tf_op jit(solution)/shard_map/reduce_scatter | solution.py:301
  108.8 1.1 slice.35
  110.5 0.5 copy.22
  111.0 43.1 %all_to_all.15 = bf16[32,28,512]{2,1,0:T(8,128)(2,1)S(1)} all-to-all(bf16[32,28,512]{2,1,0:T(8,128)(2,1)S(1)} %copy.22), channel_id=1, replica_groups=mesh['y'=4,'zh'=2,'x'=4,'zl'=4,'c'=2] {'y','zh','x'}, dimensions={0} | all-to-all | bytes 1835008 | tf_op jit(solution)/shard_map/all_to_all | solution.py:312
  154.2 6.1 %collective-permute-start.4 = (f32[32,128]{1,0:T(8,128)S(1)}, f32[32,128]{1,0:T(8,128)S(1)}, u32[]{:S(2)}, u32[]{:S(2)}) collective-permute-start(f32[32,128]{1,0:T(8,128)S(1)} %slice_bitcast_fusion), channel_id=1, source_target_pairs={{0,1},{1,0},{2,3},{3,2},{4,5},{5,4},{6,7},{7,6},{8,9},{9,8},{10,11... | collective-permute-start | bytes 49160 | tf_op jit(solution)/shard_map/ppermute | solution.py:318
  160.4 8.2 %collective-permute-start.2 = (f32[4,512]{1,0:T(4,128)S(1)}, f32[4,512]{1,0:T(4,128)S(1)}, u32[]{:S(2)}, u32[]{:S(2)}) collective-permute-start(f32[4,512]{1,0:T(4,128)S(1)} %slice.45), channel_id=1, source_target_pairs={{0,0},{1,2},{2,64},{3,66},{4,128},{5,130},{6,192},{7,194},{8,1},{9... | collective-permute-start | bytes 24584 | tf_op jit(solution)/shard_map/ppermute | solution.py:315
  168.6 1.9 collective-permute-start.3
  170.6 0.5 slice_bitcast_fusion.2
  171.1 0.7 slice_bitcast_fusion.1
  171.8 0.6 pad_maximum_fusion.1
  172.4 5.0 %collective-permute-done.3 = f32[16,512]{1,0:T(8,128)S(1)} collective-permute-done((f32[16,512]{1,0:T(8,128)S(1)}, f32[16,512]{1,0:T(8,128)S(1)}, u32[]{:S(2)}, u32[]{:S(2)}) %collective-permute-start.3) | collective-permute-done | bytes 32800 | tf_op jit(solution)/shard_map/ppermute | solution.py:316
  177.5 0.6 copy.24
  178.1 10.0 %collective-permute-start.5 = (bf16[1024,128]{1,0:T(8,128)(2,1)}, bf16[1024,128]{1,0:T(8,128)(2,1)S(1)}, u32[]{:S(2)}, u32[]{:S(2)}) collective-permute-start(bf16[1024,128]{1,0:T(8,128)(2,1)} %reduce-scatter.3.cloned.1.call-done), channel_id=1, source_target_pairs={{0,0},{1,32},{32,1},{33,33},{2,2},{3,34},{34,3},{35,35},{4,4},{5,3... | collective-permute-start | bytes 786440 | tf_op jit(solution)/shard_map/ppermute | solution.py:322
  188.2 7.1 %collective-permute-done.5 = bf16[1024,128]{1,0:T(8,128)(2,1)S(1)} collective-permute-done((bf16[1024,128]{1,0:T(8,128)(2,1)}, bf16[1024,128]{1,0:T(8,128)(2,1)S(1)}, u32[]{:S(2)}, u32[]{:S(2)}) %collective-permute-start.5) | collective-permute-done | bytes 262176 | tf_op jit(solution)/shard_map/ppermute | solution.py:322
  195.3 0.8 convert.1
  196.1 0.6 copy.28
  (32 shorter events, 1.0 us)
Async XLA Ops:
  19.4 28.6 %all-to-all-start = ((bf16[64,80,128]{2,1,0:T(8,128)(2,1)}), bf16[64,80,128]{2,1,0:T(8,128)(2,1)S(1)}, u32[]{:S(2)}, u32[]{:S(2)}) async-start(bf16[64,80,128]{2,1,0:T(8,128)(2,1)} %get-tuple-element.31), calls=%async_computation | async-start | bytes 2621440 | tf_op jit(solution)/shard_map/all_to_all | solution.py:293
  27.3 12.7 %copy-start.2 = (bf16[64,5376]{1,0:T(8,128)(2,1)S(1)}, bf16[64,5376]{1,0:T(8,128)(2,1)}, u32[]{:S(2)}) copy-start(bf16[64,5376]{1,0:T(8,128)(2,1)} %get-tuple-element.26) | copy-start | bytes 2064388
  27.3 81.5 %reduce-scatter.5.cloned.1.call-start = ((), (), s32[]{:S(2)}) async-start(), calls=%async_computation.6 | async-start | bytes 3358720 | tf_op jit(solution)/shard_map/reduce_scatter | solution.py:301
  39.5 2.4 %collective-permute-start.1 = (bf16[64,5376]{1,0:T(8,128)(2,1)}, bf16[64,5376]{1,0:T(8,128)(2,1)S(1)}, u32[]{:S(2)}, u32[]{:S(2)}) collective-permute-start(bf16[64,5376]{1,0:T(8,128)(2,1)} %get-tuple-element.28), channel_id=1, source_target_pairs={{0,1},{1,0},{2,3},{3,2},{4,5},{5,4},{6,7},{7,6},{8,9},{9,8},{10,11... | collective-permute-start | bytes 2064392 | tf_op jit(solution)/shard_map/ppermute | solution.py:298
  40.0 2.8 %collective-permute-start = (bf16[64,5376]{1,0:T(8,128)(2,1)S(1)}, bf16[64,5376]{1,0:T(8,128)(2,1)S(1)}, u32[]{:S(2)}, u32[]{:S(2)}) collective-permute-start(bf16[64,5376]{1,0:T(8,128)(2,1)S(1)} %copy-done.2), channel_id=1, source_target_pairs={{0,1},{1,0},{2,3},{3,2},{4,5},{5,4},{6,7},{7,6},{8,9},{9,8},{10,11... | collective-permute-start | bytes 2064392 | tf_op jit(solution)/shard_map/ppermute | solution.py:298
  42.0 0.9 copy-start.3
  42.8 0.8 copy-start.4
  48.0 1.0 copy-start
  49.0 22.7 %all-to-all-start.1 = ((bf16[64,64,128]{2,1,0:T(8,128)(2,1)}), bf16[64,64,128]{2,1,0:T(8,128)(2,1)S(1)}, u32[]{:S(2)}, u32[]{:S(2)}) async-start(bf16[64,64,128]{2,1,0:T(8,128)(2,1)} %get-tuple-element.33), calls=%async_computation.1 | async-start | bytes 2097152 | tf_op jit(solution)/shard_map/all_to_all | solution.py:293
  56.4 121.7 %reduce-scatter.3.cloned.1.call-start = ((), (), s32[]{:S(2)}) async-start(), calls=%async_computation.5 | async-start | bytes 2359296 | tf_op jit(solution)/shard_map/reduce_scatter | solution.py:307
  71.7 1.0 copy-start.1
  108.8 1.4 slice-start.1
  108.8 1.5 slice-start
  154.2 16.3 %collective-permute-start.4 = (f32[32,128]{1,0:T(8,128)S(1)}, f32[32,128]{1,0:T(8,128)S(1)}, u32[]{:S(2)}, u32[]{:S(2)}) collective-permute-start(f32[32,128]{1,0:T(8,128)S(1)} %slice_bitcast_fusion), channel_id=1, source_target_pairs={{0,1},{1,0},{2,3},{3,2},{4,5},{5,4},{6,7},{7,6},{8,9},{9,8},{10,11... | collective-permute-start | bytes 49160 | tf_op jit(solution)/shard_map/ppermute | solution.py:318
  160.4 17.8 %collective-permute-start.2 = (f32[4,512]{1,0:T(4,128)S(1)}, f32[4,512]{1,0:T(4,128)S(1)}, u32[]{:S(2)}, u32[]{:S(2)}) collective-permute-start(f32[4,512]{1,0:T(4,128)S(1)} %slice.45), channel_id=1, source_target_pairs={{0,0},{1,2},{2,64},{3,66},{4,128},{5,130},{6,192},{7,194},{8,1},{9... | collective-permute-start | bytes 24584 | tf_op jit(solution)/shard_map/ppermute | solution.py:315
  168.6 8.8 %collective-permute-start.3 = (f32[16,512]{1,0:T(8,128)S(1)}, f32[16,512]{1,0:T(8,128)S(1)}, u32[]{:S(2)}, u32[]{:S(2)}) collective-permute-start(f32[16,512]{1,0:T(8,128)S(1)} %slice.46), channel_id=1, source_target_pairs={{0,0},{1,128},{2,32},{3,160},{4,64},{5,192},{6,96},{7,224},{8,1},{... | collective-permute-start | bytes 98312 | tf_op jit(solution)/shard_map/ppermute | solution.py:316
  178.1 17.1 %collective-permute-start.5 = (bf16[1024,128]{1,0:T(8,128)(2,1)}, bf16[1024,128]{1,0:T(8,128)(2,1)S(1)}, u32[]{:S(2)}, u32[]{:S(2)}) collective-permute-start(bf16[1024,128]{1,0:T(8,128)(2,1)} %reduce-scatter.3.cloned.1.call-done), channel_id=1, source_target_pairs={{0,0},{1,32},{32,1},{33,33},{2,2},{3,34},{34,3},{35,35},{4,4},{5,3... | collective-permute-start | bytes 786440 | tf_op jit(solution)/shard_map/ppermute | solution.py:322
Sparse Core Ops, SparseCore 0:
  48.1 60.6 reduce-scatter.4
  111.5 59.0 reduce-scatter.2

commit v6 on v5

--- a/solution.py
+++ b/solution.py
@@ -183,21 +183,21 @@
     for q in range(4):
         for k in range(8):
             gus[pl.ds(k, 64, stride=8), :] = up[k * 64:(k + 1) * 64, q * 128:(q + 1) * 128]
-        for z in range(4):
-            w_ref[z, 0:128, q * 128:(q + 1) * 128] = gus[z * 128:(z + 1) * 128, :].astype(BF)
+        for z in range(8):
+            w_ref[z, 0:64, q * 128:(q + 1) * 128] = gus[z * 64:(z + 1) * 64, :].astype(BF)
     hid = acts[:, 1024:1280]
     for q in range(8):
         down = (dot_tn(hid, acts[:, 1280 + q * 512:1792 + q * 512]) * scale).astype(BF)
-        for z in range(4):
-            w_ref[z, 128 + q * 64:192 + q * 64, :] = down[z * 64:(z + 1) * 64, :]
-    for z in range(4):
-        w_ref[z, 640:656, :] = tail
+        for z in range(8):
+            w_ref[z, 64 + q * 32:96 + q * 32, :] = down[z * 32:(z + 1) * 32, :]
+    for z in range(8):
+        w_ref[z, 320:336, :] = tail
 
 
 def weight_call(acts, tails, scale):
     return pl.pallas_call(
         functools.partial(weight_kernel, scale),
-        out_shape=jax.ShapeDtypeStruct((4, 656, 512), BF),
+        out_shape=jax.ShapeDtypeStruct((8, 336, 512), BF),
         scratch_shapes=[pltpu.VMEM((512, 128), F32)],
         compiler_params=pltpu.CompilerParams(vmem_limit_bytes=VMEM_BYTES),
         cost_estimate=pl.CostEstimate(flops=3 * 10**9, bytes_accessed=6 << 20, transcendentals=0),
@@ -272,7 +272,7 @@
     up, down = [], []
     for d in range(256):
         y, zh, x, zl, c = (d // 64, d // 32 % 2, d // 8 % 4, d // 2 % 4, d % 2)
-        unit = zl * 32 + (y * 2 + zh) * 4 + x
+        unit = (zh * 4 + zl) * 16 + y * 4 + x
         up.append((d, (unit // 2) * 4 + 2 * c + unit % 2))
         down.append((d, c * 128 + unit))
     return up, down
@@ -298,7 +298,7 @@
     acts = (keep0, lax.ppermute(send0, "c", swap), keep1, lax.ppermute(send1, "c", swap))
     weights = weight_call(acts, (tail0, tail1), scale)
     bag1, weights, first = lax.optimization_barrier((bag1, weights, first))
-    weights = lax.psum_scatter(weights.reshape(4 * 656, 512), "zl", scatter_dimension=0, tiled=True)
+    weights = lax.psum_scatter(weights.reshape(8 * 336, 512), ("zh", "zl"), scatter_dimension=0, tiled=True)
     second = exchange(bag1)
     first = first.reshape(16, 2, 2, batch + 16, 128)
     rows = table_call(first, first)
@@ -306,10 +306,10 @@
     weights, _ = lax.optimization_barrier((weights, rows))
     rows = lax.psum_scatter(rows.reshape(8192, 128), ("zh", "zl"), scatter_dimension=0, tiled=True)
     pieces = jnp.concatenate(
-        [weights[0:128].reshape(32, 4, 512),
-         weights[128:640].reshape(8, 32, 2, 512).transpose(1, 0, 2, 3).reshape(32, 16, 512),
-         jnp.broadcast_to(weights[640:648], (32, 8, 512))], axis=1)
-    pieces = lax.all_to_all(pieces, HST, 0, 0, tiled=True)
+        [weights[0:64].reshape(16, 4, 512),
+         weights[64:320].reshape(8, 16, 2, 512).transpose(1, 0, 2, 3).reshape(16, 16, 512),
+         jnp.broadcast_to(weights[320:328], (16, 8, 512))], axis=1)
+    pieces = lax.all_to_all(pieces, ("y", "x"), 0, 0, tiled=True)
     total = jnp.sum(pieces.astype(F32), axis=0)
     up_moves, down_moves = weight_moves()
     gu = lax.ppermute(total[0:4], AXES, up_moves)

time: 204 us -> 162 us (0.79)
  blocking collectives: 43.1 us -> 13.3 us
  waiting for transfers between devices: 41.6 us -> 26.2 us
    all_to_all x1, blocking collectives: 43.1 us -> 13.3 us  [shards(): pieces = lax.all_to_all(pieces, ('y', 'x'), 0, 0, tiled=True)]
    reduce_scatter x1, waiting for transfers between devices: 23.8 us -> 6.3 us  [shards(): lax.psum_scatter(weights.reshape(8 * 336, 512), ('zh', 'zl'), scatter_dim...]
    reduce_scatter x1, waiting for transfers between devices: 0.01 us -> 4.63 us  [shards(): lax.psum_scatter(rows.reshape(8192, 128), ('zh', 'zl'), scatter_dimension...]
    ppermute x1, starting transfers between devices: 1.92 us -> 5.64 us  [shards(): lax.ppermute(total[4:20], AXES, down_moves).reshape(8, 2, 512)]
  transfers between devices with their start and end apart: 10 -> 10, of which waited for: 6 -> 7; matrix products, arithmetic and copies ran while one was open for 2% -> 4% of each run, Pallas kernels for 20% -> 25%
where the time goes in v6:
time: 162 us; the launch traced here: 160 us
  Pallas kernels  52.9 us (33%)
  starting transfers between devices  43.8 us (27%)
  waiting for transfers between devices  26.2 us (16%)
  between operations  14.2 us (9%)
  blocking collectives  13.3 us (8%)
  local copies, waits for them, and re-layouts  8.35 us (5%)
    pallas_call x2, Pallas kernels, table_call(): pl.pallas_call(functools.partial(table_kernel, pairs, group, parts, last)...  24.3 us
    pallas_call x2, Pallas kernels, layer_call(): pl.pallas_call(functools.partial(layer_kernel, scale, batch, part, int(wi...  24.2 us
    all_to_all x2, starting transfers between devices, exchange(): return lax.all_to_all(bag, PLANE, 0, 0, tiled=True)  15.3 us
    all_to_all x1, blocking collectives, shards(): pieces = lax.all_to_all(pieces, ('y', 'x'), 0, 0, tiled=True)  13.3 us
    ppermute x1, starting transfers between devices, shards(): lax.ppermute(rows, ('zh', 'c'), [(0, 0), (1, 2), (2, 1), (3, 3)])  9.45 us
    ppermute x1, waiting for transfers between devices, shards(): lax.ppermute(rows, ('zh', 'c'), [(0, 0), (1, 2), (2, 1), (3, 3)])  6.53 us
    ppermute x1, starting transfers between devices, shards(): gu = lax.ppermute(total[0:4], AXES, up_moves)  6.51 us
    reduce_scatter x1, waiting for transfers between devices, shards(): lax.psum_scatter(weights.reshape(8 * 336, 512), ('zh', 'zl'), scatter_dim...  6.3 us
  transfers between devices with their start and end apart: 10, of which 7 were waited for; matrix products, arithmetic and copies ran while one was open for 4% of the time, Pallas kernels for 25%

profile of v6, /device:TPU:7, one launch (start us, length us, event | category | flops | bytes accessed | tf_op | source)
XLA Modules:
  0.0 160.3 jit_solution(10421075166254973091)
XLA Ops:
  7.2 12.2 %layer_first.1 = (bf16[64,80,128]{2,1,0:T(8,128)(2,1)}, bf16[64,5376]{1,0:T(8,128)(2,1)}, bf16[64,5376]{1,0:T(8,128)(2,1)}, f32[32,128]{1,0:T(8,128)}) custom-call(s32[64]{0:T(128)} %refs_0_.3, s32[1]{0:T(128)} %bitcast.refs_1_, bf16[128,64,128]{2,1,0:T(8,128)(2,1)} %refs_2_.3, s32[64,2,128]{2,1,0:T(2,128)} %bitcast.40, bf16[128,64,128]{2,1,0:T(8,128)(2,1)} %refs_4_.1, ...), custom_call_target="tpu_custom_call" | custom-call | flops 15000000512 | bytes 10485760 | tf_op jit(solution)/shard_map/layer_first/pallas_call | solution.py:154
  19.4 7.9 %all-to-all-start = ((bf16[64,80,128]{2,1,0:T(8,128)(2,1)}), bf16[64,80,128]{2,1,0:T(8,128)(2,1)S(1)}, u32[]{:S(2)}, u32[]{:S(2)}) async-start(bf16[64,80,128]{2,1,0:T(8,128)(2,1)} %get-tuple-element.31), calls=%async_computation | async-start | bytes 2621440 | tf_op jit(solution)/shard_map/all_to_all | solution.py:293
  27.6 12.0 %layer_second.1 = (bf16[64,64,128]{2,1,0:T(8,128)(2,1)}, bf16[64,5376]{1,0:T(8,128)(2,1)}, bf16[64,5376]{1,0:T(8,128)(2,1)}, f32[32,128]{1,0:T(8,128)}) custom-call(s32[64]{0:T(128)} %refs_0_.3, s32[1]{0:T(128)} %bitcast.refs_1_, bf16[128,64,128]{2,1,0:T(8,128)(2,1)} %refs_2_.3, bf16[128,64,128]{2,1,0:T(8,128)(2,1)} %refs_4_.1, bf16[16,64]{1,0:T(8,128)(2,1)} %bitcast.42, ...), custom_call_target="tpu_custom_call" | custom-call | flops 15000000512 | bytes 10485760 | tf_op jit(solution)/shard_map/layer_second/pallas_call | solution.py:154
  39.5 0.4 collective-permute-start.1
  40.1 1.8 %collective-permute-done.1.b1_ref = bf16[64,5376]{1,0:T(8,128)(2,1)S(1)} collective-permute-done((bf16[64,5376]{1,0:T(8,128)(2,1)}, bf16[64,5376]{1,0:T(8,128)(2,1)S(1)}, u32[]{:S(2)}, u32[]{:S(2)}) %collective-permute-start.1) | collective-permute-done | bytes 688160 | tf_op jit(solution)/shard_map/ppermute | solution.py:298
  42.0 0.8 collective-permute-done.b0_ref
  42.8 0.8 copy-done.4
  43.6 4.4 %weight_grads.1 = bf16[8,336,512]{2,1,0:T(8,128)(2,1)} custom-call(bf16[64,5376]{1,0:T(8,128)(2,1)} %get-tuple-element.25.a0_ref, bf16[64,5376]{1,0:T(8,128)(2,1)} %copy-done.4, bf16[64,5376]{1,0:T(8,128)(2,1)} %get-tuple-element.27.a1_ref, bf16[64,5376]{1,0:T(8,128)(2,1)} %copy-done.3, f32[32,128]{1,0:T(8,128)} %get-tuple-element.29.tail0_ref, ...), custom_call_target="tpu_custom_call" | custom-call | flops 3000000000 | bytes 6291456 | tf_op jit(solution)/shard_map/weight_grads/pallas_call | solution.py:198
  48.0 1.0 copy-done
  49.1 7.4 %all-to-all-start.1 = ((bf16[64,64,128]{2,1,0:T(8,128)(2,1)}), bf16[64,64,128]{2,1,0:T(8,128)(2,1)S(1)}, u32[]{:S(2)}, u32[]{:S(2)}) async-start(bf16[64,64,128]{2,1,0:T(8,128)(2,1)} %get-tuple-element.33), calls=%async_computation.1 | async-start | bytes 2097152 | tf_op jit(solution)/shard_map/all_to_all | solution.py:293
  56.7 12.0 %table_first.1.refs_2_ = f32[2,1024,512]{2,1,0:T(8,128)} custom-call(bf16[16,2,2,80,128]{4,3,2,1,0:T(8,128)(2,1)} %bitcast.31, bf16[16,2,2,80,128]{4,3,2,1,0:T(8,128)(2,1)} %bitcast.32), custom_call_target="tpu_custom_call" | custom-call | flops 8999999488 | bytes 5242880 | tf_op jit(solution)/shard_map/table_first/pallas_call | solution.py:250
  68.7 3.0 %all-to-all-done.1 = bf16[64,64,128]{2,1,0:T(8,128)(2,1)S(1)} async-done(((bf16[64,64,128]{2,1,0:T(8,128)(2,1)}), bf16[64,64,128]{2,1,0:T(8,128)(2,1)S(1)}, u32[]{:S(2)}, u32[]{:S(2)}) %all-to-all-start.1) | async-done | bytes 1048608 | tf_op jit(solution)/shard_map/all_to_all | solution.py:293
  71.7 1.0 copy-done.1
  72.7 12.4 %table_last.1 = bf16[8,2,512,128]{3,2,1,0:T(8,128)(2,1)} custom-call(bf16[16,2,2,80,128]{4,3,2,1,0:T(8,128)(2,1)} %bitcast.33, bf16[16,2,2,64,128]{4,3,2,1,0:T(8,128)(2,1)} %bitcast.35, f32[2,1024,512]{2,1,0:T(8,128)} %table_first.1.refs_2_), custom_call_target="tpu_custom_call" | custom-call | flops 8999999488 | bytes 5242880 | tf_op jit(solution)/shard_map/table_last/pallas_call | solution.py:250
  85.1 6.3 %reduce-scatter.5.cloned.1.call-done = bf16[336,512]{1,0:T(8,128)(2,1)} async-done(((bf16[2688,512]{1,0:T(8,128)(2,1)}), bf16[336,512]{1,0:T(8,128)(2,1)}) %reduce-scatter.5.cloned.1.call-update) | async-done | bytes 344080 | tf_op jit(solution)/shard_map/reduce_scatter | solution.py:301
  91.4 0.7 slice.36
  92.1 0.8 slice.34
  92.9 1.0 slice.35
  94.4 13.3 %all_to_all.15 = bf16[16,28,512]{2,1,0:T(8,128)(2,1)S(1)} all-to-all(bf16[16,28,512]{2,1,0:T(8,128)(2,1)S(1)} %copy.22), channel_id=1, replica_groups=mesh['y'=4,'zh'=2,'x'=4,'zl'=4,'c'=2] {'y','x'}, dimensions={0} | all-to-all | bytes 917504 | tf_op jit(solution)/shard_map/all_to_all | solution.py:312
  107.8 5.8 %collective-permute-start.4 = (f32[32,128]{1,0:T(8,128)S(1)}, f32[32,128]{1,0:T(8,128)S(1)}, u32[]{:S(2)}, u32[]{:S(2)}) collective-permute-start(f32[32,128]{1,0:T(8,128)S(1)} %slice_bitcast_fusion), channel_id=1, source_target_pairs={{0,1},{1,0},{2,3},{3,2},{4,5},{5,4},{6,7},{7,6},{8,9},{9,8},{10,11... | collective-permute-start | bytes 49160 | tf_op jit(solution)/shard_map/ppermute | solution.py:318
  113.6 6.5 %collective-permute-start.2 = (f32[4,512]{1,0:T(4,128)S(1)}, f32[4,512]{1,0:T(4,128)S(1)}, u32[]{:S(2)}, u32[]{:S(2)}) collective-permute-start(f32[4,512]{1,0:T(4,128)S(1)} %slice.45), channel_id=1, source_target_pairs={{0,0},{1,2},{2,32},{3,34},{4,64},{5,66},{6,96},{7,98},{8,1},{9,3},... | collective-permute-start | bytes 24584 | tf_op jit(solution)/shard_map/ppermute | solution.py:315
  120.2 5.6 %collective-permute-start.3 = (f32[16,512]{1,0:T(8,128)S(1)}, f32[16,512]{1,0:T(8,128)S(1)}, u32[]{:S(2)}, u32[]{:S(2)}) collective-permute-start(f32[16,512]{1,0:T(8,128)S(1)} %slice.46), channel_id=1, source_target_pairs={{0,0},{1,128},{2,16},{3,144},{4,32},{5,160},{6,48},{7,176},{8,1},{... | collective-permute-start | bytes 98312 | tf_op jit(solution)/shard_map/ppermute | solution.py:316
  125.8 0.5 slice_bitcast_fusion.2
  126.3 0.7 slice_bitcast_fusion.1
  127.1 0.6 pad_maximum_fusion.1
  127.7 3.0 %collective-permute-done.3 = f32[16,512]{1,0:T(8,128)S(1)} collective-permute-done((f32[16,512]{1,0:T(8,128)S(1)}, f32[16,512]{1,0:T(8,128)S(1)}, u32[]{:S(2)}, u32[]{:S(2)}) %collective-permute-start.3) | collective-permute-done | bytes 32800 | tf_op jit(solution)/shard_map/ppermute | solution.py:316
  130.8 0.6 copy.24
  131.4 4.6 %reduce-scatter.3.cloned.1.call-done = bf16[1024,128]{1,0:T(8,128)(2,1)} async-done(((bf16[8192,128]{1,0:T(8,128)(2,1)}), bf16[1024,128]{1,0:T(8,128)(2,1)}) %reduce-scatter.3.cloned.1.call-update) | async-done | bytes 262160 | tf_op jit(solution)/shard_map/reduce_scatter | solution.py:307
  136.0 9.5 %collective-permute-start.5 = (bf16[1024,128]{1,0:T(8,128)(2,1)}, bf16[1024,128]{1,0:T(8,128)(2,1)S(1)}, u32[]{:S(2)}, u32[]{:S(2)}) collective-permute-start(bf16[1024,128]{1,0:T(8,128)(2,1)} %reduce-scatter.3.cloned.1.call-done), channel_id=1, source_target_pairs={{0,0},{1,32},{32,1},{33,33},{2,2},{3,34},{34,3},{35,35},{4,4},{5,3... | collective-permute-start | bytes 786440 | tf_op jit(solution)/shard_map/ppermute | solution.py:322
  145.5 6.5 %collective-permute-done.5 = bf16[1024,128]{1,0:T(8,128)(2,1)S(1)} collective-permute-done((bf16[1024,128]{1,0:T(8,128)(2,1)}, bf16[1024,128]{1,0:T(8,128)(2,1)S(1)}, u32[]{:S(2)}, u32[]{:S(2)}) %collective-permute-start.5) | collective-permute-done | bytes 262176 | tf_op jit(solution)/shard_map/ppermute | solution.py:322
  152.0 0.8 convert.1
  152.9 0.6 copy.28
  (30 shorter events, 1.5 us)
Async XLA Ops:
  19.4 28.6 %all-to-all-start = ((bf16[64,80,128]{2,1,0:T(8,128)(2,1)}), bf16[64,80,128]{2,1,0:T(8,128)(2,1)S(1)}, u32[]{:S(2)}, u32[]{:S(2)}) async-start(bf16[64,80,128]{2,1,0:T(8,128)(2,1)} %get-tuple-element.31), calls=%async_computation | async-start | bytes 2621440 | tf_op jit(solution)/shard_map/all_to_all | solution.py:293
  27.3 12.7 %copy-start.2 = (bf16[64,5376]{1,0:T(8,128)(2,1)S(1)}, bf16[64,5376]{1,0:T(8,128)(2,1)}, u32[]{:S(2)}) copy-start(bf16[64,5376]{1,0:T(8,128)(2,1)} %get-tuple-element.26) | copy-start | bytes 2064388
  27.3 64.1 %reduce-scatter.5.cloned.1.call-start = ((), (), s32[]{:S(2)}) async-start(), calls=%async_computation.6 | async-start | bytes 3096576 | tf_op jit(solution)/shard_map/reduce_scatter | solution.py:301
  39.5 2.4 %collective-permute-start.1 = (bf16[64,5376]{1,0:T(8,128)(2,1)}, bf16[64,5376]{1,0:T(8,128)(2,1)S(1)}, u32[]{:S(2)}, u32[]{:S(2)}) collective-permute-start(bf16[64,5376]{1,0:T(8,128)(2,1)} %get-tuple-element.28), channel_id=1, source_target_pairs={{0,1},{1,0},{2,3},{3,2},{4,5},{5,4},{6,7},{7,6},{8,9},{9,8},{10,11... | collective-permute-start | bytes 2064392 | tf_op jit(solution)/shard_map/ppermute | solution.py:298
  40.0 2.8 %collective-permute-start = (bf16[64,5376]{1,0:T(8,128)(2,1)S(1)}, bf16[64,5376]{1,0:T(8,128)(2,1)S(1)}, u32[]{:S(2)}, u32[]{:S(2)}) collective-permute-start(bf16[64,5376]{1,0:T(8,128)(2,1)S(1)} %copy-done.2), channel_id=1, source_target_pairs={{0,1},{1,0},{2,3},{3,2},{4,5},{5,4},{6,7},{7,6},{8,9},{9,8},{10,11... | collective-permute-start | bytes 2064392 | tf_op jit(solution)/shard_map/ppermute | solution.py:298
  42.0 0.8 copy-start.3
  42.8 0.8 copy-start.4
  48.0 1.0 copy-start
  49.1 22.7 %all-to-all-start.1 = ((bf16[64,64,128]{2,1,0:T(8,128)(2,1)}), bf16[64,64,128]{2,1,0:T(8,128)(2,1)S(1)}, u32[]{:S(2)}, u32[]{:S(2)}) async-start(bf16[64,64,128]{2,1,0:T(8,128)(2,1)} %get-tuple-element.33), calls=%async_computation.1 | async-start | bytes 2097152 | tf_op jit(solution)/shard_map/all_to_all | solution.py:293
  56.4 79.6 %reduce-scatter.3.cloned.1.call-start = ((), (), s32[]{:S(2)}) async-start(), calls=%async_computation.5 | async-start | bytes 2359296 | tf_op jit(solution)/shard_map/reduce_scatter | solution.py:307
  71.7 1.0 copy-start.1
  107.8 18.0 %collective-permute-start.4 = (f32[32,128]{1,0:T(8,128)S(1)}, f32[32,128]{1,0:T(8,128)S(1)}, u32[]{:S(2)}, u32[]{:S(2)}) collective-permute-start(f32[32,128]{1,0:T(8,128)S(1)} %slice_bitcast_fusion), channel_id=1, source_target_pairs={{0,1},{1,0},{2,3},{3,2},{4,5},{5,4},{6,7},{7,6},{8,9},{9,8},{10,11... | collective-permute-start | bytes 49160 | tf_op jit(solution)/shard_map/ppermute | solution.py:318
  113.6 22.4 %collective-permute-start.2 = (f32[4,512]{1,0:T(4,128)S(1)}, f32[4,512]{1,0:T(4,128)S(1)}, u32[]{:S(2)}, u32[]{:S(2)}) collective-permute-start(f32[4,512]{1,0:T(4,128)S(1)} %slice.45), channel_id=1, source_target_pairs={{0,0},{1,2},{2,32},{3,34},{4,64},{5,66},{6,96},{7,98},{8,1},{9,3},... | collective-permute-start | bytes 24584 | tf_op jit(solution)/shard_map/ppermute | solution.py:315
  120.2 10.6 %collective-permute-start.3 = (f32[16,512]{1,0:T(8,128)S(1)}, f32[16,512]{1,0:T(8,128)S(1)}, u32[]{:S(2)}, u32[]{:S(2)}) collective-permute-start(f32[16,512]{1,0:T(8,128)S(1)} %slice.46), channel_id=1, source_target_pairs={{0,0},{1,128},{2,16},{3,144},{4,32},{5,160},{6,48},{7,176},{8,1},{... | collective-permute-start | bytes 98312 | tf_op jit(solution)/shard_map/ppermute | solution.py:316
  136.0 16.0 %collective-permute-start.5 = (bf16[1024,128]{1,0:T(8,128)(2,1)}, bf16[1024,128]{1,0:T(8,128)(2,1)S(1)}, u32[]{:S(2)}, u32[]{:S(2)}) collective-permute-start(bf16[1024,128]{1,0:T(8,128)(2,1)} %reduce-scatter.3.cloned.1.call-done), channel_id=1, source_target_pairs={{0,0},{1,32},{32,1},{33,33},{2,2},{3,34},{34,3},{35,35},{4,4},{5,3... | collective-permute-start | bytes 786440 | tf_op jit(solution)/shard_map/ppermute | solution.py:322
Sparse Core Ops, SparseCore 0:
  48.2 43.1 reduce-scatter.4
  94.1 41.8 reduce-scatter.2

commit v7 on v6

--- a/solution.py
+++ b/solution.py
@@ -49,7 +49,7 @@
     for copy in copies:
         copy.start()
     for j in range(64):
-        inv_ref[fm_ref[j]] = j
+        inv_ref[fm_ref[j]] = ((j // 16 * 4 + j // 2 % 4) * 2 + j // 8 % 2) * 2 + j % 2
     if with_ids:
         for n in range(64):
             v = ids_ref[n]
@@ -205,67 +205,68 @@
     )(*acts, *tails)
 
 
-def table_kernel(pairs, group, parts, last, *refs):
-    span = 4096 // parts
+def table_kernel(last, *refs):
     if last:
-        ids_ref, bags_ref, start_ref, out_ref, acc = refs
+        core_ref, own_ids, other_ids, own_bags, other_bags, start_ref, out_ref, acc = refs
     else:
-        ids_ref, bags_ref, acc = refs
+        core_ref, own_ids, other_ids, own_bags, other_bags, acc = refs
         acc = acc.at[0]
     side = slice(64, 128) if last else slice(0, 64)
     ids = []
-    for i in range(pairs):
-        codes = ids_ref[i, :, 0].astype(F32)
-        codes = codes[:, 0:2] + 256.0 * codes[:, 2:4]
-        ids.append(jnp.concatenate([codes[0][:, side], codes[1][:, side]], axis=1))
+    for ids_ref in (own_ids, other_ids):
+        for i in range(8):
+            codes = ids_ref[i, :, 0].astype(F32)
+            codes = codes[:, 0:2] + 256.0 * codes[:, 2:4]
+            ids.append(jnp.concatenate([codes[0][:, side], codes[1][:, side]], axis=1))
     ids = jnp.concatenate(ids, axis=0).astype(jnp.int32)
-    low = jnp.transpose(lax.shift_right_logical(ids, span.bit_length() - 1).astype(F32), (1, 0))
-    high = jnp.bitwise_and(ids, span - 1).astype(jnp.int16)
-    iota = lax.broadcasted_iota(jnp.int16, (span, 128), 0)
-    for g in range(pairs // group):
+    low = jnp.transpose(lax.shift_right_logical(ids, 11).astype(F32), (1, 0))
+    high = jnp.bitwise_and(lax.shift_right_logical(ids, 1), 512) + jnp.bitwise_and(ids, 511)
+    mine = jnp.bitwise_and(lax.shift_right_logical(ids, 9), 1) == core_ref[0]
+    high = jnp.where(mine, high, -1).astype(jnp.int16)
+    iota = lax.broadcasted_iota(jnp.int16, (1024, 128), 0)
+    for g in range(4):
         left, right = [], []
-        for i in range(g * group, (g + 1) * group):
-            values = bags_ref[i, :, 0].reshape(128, 128)
+        for i in range(g * 4, (g + 1) * 4):
+            values = (own_bags if i < 8 else other_bags)[i % 8, :, 0].reshape(128, 128)
             for t in range(2):
                 r = 2 * i + t
                 left.append(jnp.where(iota == high[r:r + 1, :], jnp.bfloat16(1), jnp.bfloat16(0)))
                 column = jnp.broadcast_to(low[:, r:r + 1], (128, 128)).astype(BF)
                 right.append(jnp.concatenate(
-                    [jnp.where(column == jnp.bfloat16(q), values, jnp.bfloat16(0)) for q in range(parts)], axis=1))
+                    [jnp.where(column == jnp.bfloat16(q), values, jnp.bfloat16(0)) for q in range(2)], axis=1))
         part = jnp.dot(jnp.concatenate(left, axis=1), jnp.concatenate(right, axis=0), preferred_element_type=F32)
         if g == 0:
             acc[...] = start_ref[0] + part if last else part
         else:
             acc[...] += part
-
     if last:
-        for p in range(8):
-            q, h = p // (8 // parts), p % (8 // parts)
-            out_ref[(p % 2) * 4 + p // 2, 0] = acc[h * 512:(h + 1) * 512, q * 128:(q + 1) * 128].astype(BF)
-
-
-def table_call(ids, bags, start=None, pairs=16, group=4, parts=4):
+        for block in range(4):
+            h, q = block % 2, block // 2
+            out_ref[0, block, 0] = acc[h * 512:(h + 1) * 512, q * 128:(q + 1) * 128].astype(BF)
+
+
+def table_call(core, own_ids, other_ids, own, other, start=None):
     last = start is not None
-    sums = pl.BlockSpec((1, 4096 // parts, 128 * parts), lambda j, i: (j, 0, 0))
+    sums = pl.BlockSpec((1, 1024, 256), lambda j: (j, 0, 0))
+    codes = pl.BlockSpec((8, 2, 1, 16, 128), lambda j: (0, 0, j, 4, 0))
+    bags = pl.BlockSpec((8, 2, 1, 64, 128), lambda j: (0, 0, j, 0, 0))
     return pl.pallas_call(
-        functools.partial(table_kernel, pairs, group, parts, last),
-        grid=(2, ids.shape[0] // pairs),
-        in_specs=[pl.BlockSpec((pairs, 2, 1, 16, 128), lambda j, i: (i, 0, j, 4, 0)),
-                  pl.BlockSpec((pairs, 2, 1, 64, 128), lambda j, i: (i, 0, j, 0, 0))] + ([sums] if last else []),
-        out_specs=pl.BlockSpec((8, 1, 512, 128), lambda j, i: (0, j, 0, 0)) if last else sums,
-        out_shape=jax.ShapeDtypeStruct((8, 2, 512, 128), BF) if last else jax.ShapeDtypeStruct((2, 4096 // parts, 128 * parts), F32),
-        scratch_shapes=[pltpu.VMEM((4096 // parts, 128 * parts), F32)] if last else [],
+        functools.partial(table_kernel, last),
+        grid=(4,),
+        in_specs=[pl.BlockSpec(memory_space=pltpu.SMEM), codes, codes, bags, bags] + ([sums] if last else []),
+        out_specs=pl.BlockSpec((1, 4, 1, 512, 128), lambda j: (j // 2, 0, j % 2, 0, 0)) if last else sums,
+        out_shape=jax.ShapeDtypeStruct((2, 4, 2, 512, 128), BF) if last else jax.ShapeDtypeStruct((4, 1024, 256), F32),
+        scratch_shapes=[pltpu.VMEM((1024, 256), F32)] if last else [],
         compiler_params=pltpu.CompilerParams(vmem_limit_bytes=VMEM_BYTES),
         cost_estimate=pl.CostEstimate(flops=9 * 10**9, bytes_accessed=5 << 20, transcendentals=0),
         name="table_last" if last else "table_first",
-    )(*([ids, bags] + ([start] if last else [])))
+    )(*([core, own_ids, other_ids, own, other] + ([start] if last else [])))
 
 
 AXES = ("y", "zh", "x", "zl", "c")
 HST = ("y", "zh", "x")
 LOCAL = ("zl", "c")
 SIZES = (4, 2, 4, 4, 2)
-PLANE = ("y", "c", "x")
 
 
 def weight_moves():
@@ -290,7 +291,7 @@
                           projection.T, w_up, w_down, w_compress, ln_gain.reshape(1, 128), scale)
 
     def exchange(bag):
-        return lax.all_to_all(bag, PLANE, 0, 0, tiled=True)
+        return lax.all_to_all(bag, ("y", "x"), 0, 0, tiled=True)
 
     bag0, keep0, send0, tail0 = layer(0)
     first = exchange(bag0)
@@ -300,9 +301,12 @@
     bag1, weights, first = lax.optimization_barrier((bag1, weights, first))
     weights = lax.psum_scatter(weights.reshape(8 * 336, 512), ("zh", "zl"), scatter_dimension=0, tiled=True)
     second = exchange(bag1)
-    first = first.reshape(16, 2, 2, batch + 16, 128)
-    rows = table_call(first, first)
-    rows = table_call(first, second.reshape(16, 2, 2, batch, 128), rows)
+    first = first.reshape(8, 2, 4, batch + 16, 128)
+    other = lax.ppermute(first, "c", swap)
+    rows = table_call(core, first, other, first, other)
+    second, rows = lax.optimization_barrier((second, rows))
+    second = second.reshape(8, 2, 4, batch, 128)
+    rows = table_call(core, first, other, second, lax.ppermute(second, "c", swap), rows)
     weights, _ = lax.optimization_barrier((weights, rows))
     rows = lax.psum_scatter(rows.reshape(8192, 128), ("zh", "zl"), scatter_dimension=0, tiled=True)
     pieces = jnp.concatenate(
@@ -319,8 +323,7 @@
     both = jnp.concatenate([tail[0:24, :64], tail[0:24, 64:]], axis=0)
     small = (both[32:48].T, both[0:32], tail[24])
     rows, gu, gd, small = lax.optimization_barrier((rows, gu, gd, small))
-    table_grad = lax.ppermute(rows, ("zh", "c"), [(0, 0), (1, 2), (2, 1), (3, 3)]).astype(F32)
-    return (table_grad.reshape(2, 512, 128), gu, gd) + tuple(small)
+    return (rows.astype(F32).reshape(2, 512, 128), gu, gd) + tuple(small)
 
 
 def solution(mesh):

time: 162 us -> 150 us (0.926)
  the two profiles are of different devices: /device:TPU:7 before, /device:TPU:2 now
where the time goes in v7:
time: 150 us; the launch traced here: 149 us
  Pallas kernels  54.2 us (36%)
  waiting for transfers between devices  32.1 us (21%)
  starting transfers between devices  22.1 us (15%)
  blocking collectives  15.9 us (11%)
  between operations  14.2 us (9%)
  local copies, waits for them, and re-layouts  8.18 us (5%)
  other arithmetic  2.53 us (2%)
    pallas_call x2, Pallas kernels, table_call(): pl.pallas_call(functools.partial(table_kernel, last), grid=(4,), in_specs...  25.6 us
    pallas_call x2, Pallas kernels, layer_call(): pl.pallas_call(functools.partial(layer_kernel, scale, batch, part, int(wi...  24.2 us
    all_to_all x1, blocking collectives, shards(): pieces = lax.all_to_all(pieces, ('y', 'x'), 0, 0, tiled=True)  15.9 us
    all_to_all x2, starting transfers between devices, exchange(): return lax.all_to_all(bag, ('y', 'x'), 0, 0, tiled=True)  14.7 us
    reduce_scatter x1, waiting for transfers between devices, shards(): lax.psum_scatter(rows.reshape(8192, 128), ('zh', 'zl'), scatter_dimension...  13.4 us
    reduce_scatter x1, waiting for transfers between devices, shards(): lax.psum_scatter(weights.reshape(8 * 336, 512), ('zh', 'zl'), scatter_dim...  6.32 us
    pallas_call x1, Pallas kernels, weight_call(): pl.pallas_call(functools.partial(weight_kernel, scale), out_shape=jax.Sha...  4.39 us
    unnamed x14, local copies, waits for them, and re-layouts  3.92 us
  transfers between devices with their start and end apart: 11, of which 7 were waited for; matrix products, arithmetic and copies ran while one was open for 4% of the time, Pallas kernels for 28%

profile of v7, /device:TPU:2, one launch (start us, length us, event | category | flops | bytes accessed | tf_op | source)
XLA Modules:
  0.0 149.2 jit_solution(9060816335450575337)
XLA Ops:
  7.2 12.2 %layer_first.1 = (bf16[64,80,128]{2,1,0:T(8,128)(2,1)}, bf16[64,5376]{1,0:T(8,128)(2,1)}, bf16[64,5376]{1,0:T(8,128)(2,1)}, f32[32,128]{1,0:T(8,128)}) custom-call(s32[64]{0:T(128)} %refs_0_.3, s32[1]{0:T(128)} %bitcast.refs_1_.refs_0_, bf16[128,64,128]{2,1,0:T(8,128)(2,1)} %refs_2_.3, s32[64,2,128]{2,1,0:T(2,128)} %bitcast.42, ...), custom_call_target="tpu_custom_call" | custom-call | flops 15000000512 | bytes 10485760 | tf_op jit(solution)/shard_map/layer_first/pallas_call | solution.py:154
  19.4 7.5 %all-to-all-start = ((bf16[64,80,128]{2,1,0:T(8,128)(2,1)}), bf16[64,80,128]{2,1,0:T(8,128)(2,1)S(1)}, u32[]{:S(2)}, u32[]{:S(2)}) async-start(bf16[64,80,128]{2,1,0:T(8,128)(2,1)} %get-tuple-element.33), calls=%async_computation | async-start | bytes 2621440 | tf_op jit(solution)/shard_map/all_to_all | solution.py:294
  27.1 12.0 %layer_second.1 = (bf16[64,64,128]{2,1,0:T(8,128)(2,1)}, bf16[64,5376]{1,0:T(8,128)(2,1)}, bf16[64,5376]{1,0:T(8,128)(2,1)}, f32[32,128]{1,0:T(8,128)}) custom-call(s32[64]{0:T(128)} %refs_0_.3, s32[1]{0:T(128)} %bitcast.refs_1_.refs_0_, bf16[128,64,128]{2,1,0:T(8,128)(2,1)} %refs_2_.3, bf16[128,64,128]{2,1,0:T(8,128)(2,1)} %refs_4_.1, ...), custom_call_target="tpu_custom_call" | custom-call | flops 15000000512 | bytes 10485760 | tf_op jit(solution)/shard_map/layer_second/pallas_call | solution.py:154
  39.2 0.5 collective-permute-start
  39.7 1.8 %collective-permute-done.1.b1_ref = bf16[64,5376]{1,0:T(8,128)(2,1)S(1)} collective-permute-done((bf16[64,5376]{1,0:T(8,128)(2,1)}, bf16[64,5376]{1,0:T(8,128)(2,1)S(1)}, u32[]{:S(2)}, u32[]{:S(2)}) %collective-permute-start.1) | collective-permute-done | bytes 688160 | tf_op jit(solution)/shard_map/ppermute | solution.py:299
  41.5 0.8 collective-permute-done.b0_ref
  42.4 0.8 copy-done.5
  43.2 4.4 %weight_grads.1 = bf16[8,336,512]{2,1,0:T(8,128)(2,1)} custom-call(bf16[64,5376]{1,0:T(8,128)(2,1)} %get-tuple-element.27.a0_ref, bf16[64,5376]{1,0:T(8,128)(2,1)} %copy-done.5, bf16[64,5376]{1,0:T(8,128)(2,1)} %get-tuple-element.29.a1_ref, bf16[64,5376]{1,0:T(8,128)(2,1)} %copy-done.4, f32[32,128]{1,0:T(8,128)} %get-tuple-element.31.tail0_ref, ...), custom_call_target="tpu_custom_call" | custom-call | flops 3000000000 | bytes 6291456 | tf_op jit(solution)/shard_map/weight_grads/pallas_call | solution.py:198
  47.8 0.8 copy-done
  48.6 7.2 %all-to-all-start.1 = ((bf16[64,64,128]{2,1,0:T(8,128)(2,1)}), bf16[64,64,128]{2,1,0:T(8,128)(2,1)S(1)}, u32[]{:S(2)}, u32[]{:S(2)}) async-start(bf16[64,64,128]{2,1,0:T(8,128)(2,1)} %get-tuple-element.35), calls=%async_computation.1 | async-start | bytes 2097152 | tf_op jit(solution)/shard_map/all_to_all | solution.py:294
  55.8 0.3 reduce-scatter.3.cloned.1.call-start
  56.1 12.7 %table_first.1.refs_5_ = f32[4,1024,256]{2,1,0:T(8,128)} custom-call(s32[1]{0:T(128)} %bitcast.refs_1_.refs_0_, bf16[8,2,4,80,128]{4,3,2,1,0:T(8,128)(2,1)} %bitcast.32, bf16[8,2,4,80,128]{4,3,2,1,0:T(8,128)(2,1)} %collective-permute-done.2.refs_2_.refs_4_, bf16[8,2,4,80,128]{4,3,2,1,0:T(8,128)(2,1)} %bitcast.33, ...), custom_call_target="tpu_custom_call" | custom-call | flops 8999999488 | bytes 5242880 | tf_op jit(solution)/shard_map/table_first/pallas_call | solution.py:253
  68.8 3.1 %all-to-all-done.1 = bf16[64,64,128]{2,1,0:T(8,128)(2,1)S(1)} async-done(((bf16[64,64,128]{2,1,0:T(8,128)(2,1)}), bf16[64,64,128]{2,1,0:T(8,128)(2,1)S(1)}, u32[]{:S(2)}, u32[]{:S(2)}) %all-to-all-start.1) | async-done | bytes 1048608 | tf_op jit(solution)/shard_map/all_to_all | solution.py:294
  71.9 2.7 %collective-permute-done.3.refs_4_ = bf16[8,2,4,64,128]{4,3,2,1,0:T(8,128)(2,1)S(1)} collective-permute-done((bf16[8,2,4,64,128]{4,3,2,1,0:T(8,128)(2,1)S(1)}, bf16[8,2,4,64,128]{4,3,2,1,0:T(8,128)(2,1)S(1)}, u32[]{:S(2)}, u32[]{:S(2)}) %collective-permute-start.3) | collective-permute-done | bytes 1048608 | tf_op jit(solution)/shard_map/ppermute | solution.py:309
  74.6 1.0 copy-done.2
  75.6 13.0 %table_last.1 = bf16[2,4,2,512,128]{4,3,2,1,0:T(8,128)(2,1)} custom-call(s32[1]{0:T(128)} %bitcast.refs_1_.refs_0_, bf16[8,2,4,80,128]{4,3,2,1,0:T(8,128)(2,1)} %bitcast.34, bf16[8,2,4,80,128]{4,3,2,1,0:T(8,128)(2,1)} %collective-permute-done.2.refs_2_.refs_4_, bf16[8,2,4,64,128]{4,3,2,1,0:T(8,128)(2,1)} %bitcast.37, bf16[8,2,4,64,128]{4,3,2,1,0:T(8,128)(2,1)} %copy-done.2, ...), custom_call_target="tpu_custom_call" | custom-call | flops 8999999488 | bytes 5242880 | tf_op jit(solution)/shard_map/table_last/pallas_call | solution.py:253
  88.6 6.3 %reduce-scatter.5.cloned.1.call-done = bf16[336,512]{1,0:T(8,128)(2,1)} async-done(((bf16[2688,512]{1,0:T(8,128)(2,1)}), bf16[336,512]{1,0:T(8,128)(2,1)}) %reduce-scatter.5.cloned.1.call-update) | async-done | bytes 344080 | tf_op jit(solution)/shard_map/reduce_scatter | solution.py:302
  94.9 0.7 slice.36
  95.6 0.8 slice.34
  96.5 1.0 slice.35
  97.7 0.3 copy.22
  98.0 15.9 %all_to_all.15 = bf16[16,28,512]{2,1,0:T(8,128)(2,1)S(1)} all-to-all(bf16[16,28,512]{2,1,0:T(8,128)(2,1)S(1)} %copy.22), channel_id=1, replica_groups=mesh['y'=4,'zh'=2,'x'=4,'zl'=4,'c'=2] {'y','x'}, dimensions={0} | all-to-all | bytes 917504 | tf_op jit(solution)/shard_map/all_to_all | solution.py:316
  114.1 3.5 %collective-permute-start.4 = (f32[4,512]{1,0:T(4,128)S(1)}, f32[4,512]{1,0:T(4,128)S(1)}, u32[]{:S(2)}, u32[]{:S(2)}) collective-permute-start(f32[4,512]{1,0:T(4,128)S(1)} %slice.45), channel_id=1, source_target_pairs={{0,0},{1,2},{2,32},{3,34},{4,64},{5,66},{6,96},{7,98},{8,1},{9,3},... | collective-permute-start | bytes 24584 | tf_op jit(solution)/shard_map/ppermute | solution.py:319
  117.6 2.5 %collective-permute-start.5 = (f32[16,512]{1,0:T(8,128)S(1)}, f32[16,512]{1,0:T(8,128)S(1)}, u32[]{:S(2)}, u32[]{:S(2)}) collective-permute-start(f32[16,512]{1,0:T(8,128)S(1)} %slice.46), channel_id=1, source_target_pairs={{0,0},{1,128},{2,16},{3,144},{4,32},{5,160},{6,48},{7,176},{8,1},{... | collective-permute-start | bytes 98312 | tf_op jit(solution)/shard_map/ppermute | solution.py:320
  120.1 0.5 slice_bitcast_fusion.2
  120.6 0.7 slice_bitcast_fusion.1
  121.4 0.6 pad_maximum_fusion.1
  122.0 3.9 %collective-permute-done.5 = f32[16,512]{1,0:T(8,128)S(1)} collective-permute-done((f32[16,512]{1,0:T(8,128)S(1)}, f32[16,512]{1,0:T(8,128)S(1)}, u32[]{:S(2)}, u32[]{:S(2)}) %collective-permute-start.5) | collective-permute-done | bytes 32800 | tf_op jit(solution)/shard_map/ppermute | solution.py:320
  125.9 0.6 copy.24
  126.6 13.4 %reduce-scatter.3.cloned.1.call-done = bf16[1024,128]{1,0:T(8,128)(2,1)} async-done(((bf16[8192,128]{1,0:T(8,128)(2,1)}), bf16[1024,128]{1,0:T(8,128)(2,1)}) %reduce-scatter.3.cloned.1.call-update) | async-done | bytes 262160 | tf_op jit(solution)/shard_map/reduce_scatter | solution.py:311
  140.0 1.8 %convert.1 = f32[2,512,128]{2,1,0:T(8,128)} convert(bf16[2,512,128]{2,1,0:T(8,128)(2,1)} %bitcast.39) | non-fusion elementwise | flops 131072 | bytes 786432 | tf_op jit(solution)/shard_map/reshape | solution.py:326
  141.8 0.6 copy.28
  (34 shorter events, 1.2 us)
Async XLA Ops:
  19.4 28.2 %all-to-all-start = ((bf16[64,80,128]{2,1,0:T(8,128)(2,1)}), bf16[64,80,128]{2,1,0:T(8,128)(2,1)S(1)}, u32[]{:S(2)}, u32[]{:S(2)}) async-start(bf16[64,80,128]{2,1,0:T(8,128)(2,1)} %get-tuple-element.33), calls=%async_computation | async-start | bytes 2621440 | tf_op jit(solution)/shard_map/all_to_all | solution.py:294
  26.9 12.3 %copy-start.3 = (bf16[64,5376]{1,0:T(8,128)(2,1)S(1)}, bf16[64,5376]{1,0:T(8,128)(2,1)}, u32[]{:S(2)}) copy-start(bf16[64,5376]{1,0:T(8,128)(2,1)} %get-tuple-element.28) | copy-start | bytes 2064388
  26.9 68.0 %reduce-scatter.5.cloned.1.call-start = ((), (), s32[]{:S(2)}) async-start(), calls=%async_computation.6 | async-start | bytes 3096576 | tf_op jit(solution)/shard_map/reduce_scatter | solution.py:302
  39.1 2.4 %collective-permute-start.1 = (bf16[64,5376]{1,0:T(8,128)(2,1)}, bf16[64,5376]{1,0:T(8,128)(2,1)S(1)}, u32[]{:S(2)}, u32[]{:S(2)}) collective-permute-start(bf16[64,5376]{1,0:T(8,128)(2,1)} %get-tuple-element.30), channel_id=1, source_target_pairs={{0,1},{1,0},{2,3},{3,2},{4,5},{5,4},{6,7},{7,6},{8,9},{9,8},{10,11... | collective-permute-start | bytes 2064392 | tf_op jit(solution)/shard_map/ppermute | solution.py:299
  39.2 3.1 %collective-permute-start = (bf16[64,5376]{1,0:T(8,128)(2,1)S(1)}, bf16[64,5376]{1,0:T(8,128)(2,1)S(1)}, u32[]{:S(2)}, u32[]{:S(2)}) collective-permute-start(bf16[64,5376]{1,0:T(8,128)(2,1)S(1)} %copy-done.3), channel_id=1, source_target_pairs={{0,1},{1,0},{2,3},{3,2},{4,5},{5,4},{6,7},{7,6},{8,9},{9,8},{10,11... | collective-permute-start | bytes 2064392 | tf_op jit(solution)/shard_map/ppermute | solution.py:299
  41.5 0.9 copy-start.4
  42.3 0.8 copy-start.5
  47.6 1.0 copy-start
  47.6 8.5 %collective-permute-start.2 = (bf16[8,2,4,80,128]{4,3,2,1,0:T(8,128)(2,1)S(1)}, bf16[8,2,4,80,128]{4,3,2,1,0:T(8,128)(2,1)}, u32[]{:S(2)}, u32[]{:S(2)}) collective-permute-start(bf16[8,2,4,80,128]{4,3,2,1,0:T(8,128)(2,1)S(1)} %bitcast.31), channel_id=1, source_target_pairs={{0,1},{1,0},{2,3},{3,2},{4,5},{5,4},{6,7},{7,6},{8,9},{9,8},{10,11... | collective-permute-start | bytes 3932168 | tf_op jit(solution)/shard_map/ppermute | solution.py:305
  48.6 23.3 %all-to-all-start.1 = ((bf16[64,64,128]{2,1,0:T(8,128)(2,1)}), bf16[64,64,128]{2,1,0:T(8,128)(2,1)S(1)}, u32[]{:S(2)}, u32[]{:S(2)}) async-start(bf16[64,64,128]{2,1,0:T(8,128)(2,1)} %get-tuple-element.35), calls=%async_computation.1 | async-start | bytes 2097152 | tf_op jit(solution)/shard_map/all_to_all | solution.py:294
  55.8 84.1 %reduce-scatter.3.cloned.1.call-start = ((), (), s32[]{:S(2)}) async-start(), calls=%async_computation.5 | async-start | bytes 2359296 | tf_op jit(solution)/shard_map/reduce_scatter | solution.py:311
  71.9 2.7 %copy-start.1 = (bf16[64,64,128]{2,1,0:T(8,128)(2,1)}, bf16[64,64,128]{2,1,0:T(8,128)(2,1)S(1)}, u32[]{:S(2)}) copy-start(bf16[64,64,128]{2,1,0:T(8,128)(2,1)S(1)} %all-to-all-done.1) | copy-start | bytes 3145732
  71.9 2.7 %collective-permute-start.3 = (bf16[8,2,4,64,128]{4,3,2,1,0:T(8,128)(2,1)S(1)}, bf16[8,2,4,64,128]{4,3,2,1,0:T(8,128)(2,1)S(1)}, u32[]{:S(2)}, u32[]{:S(2)}) collective-permute-start(bf16[8,2,4,64,128]{4,3,2,1,0:T(8,128)(2,1)S(1)} %bitcast.36), channel_id=1, source_target_pairs={{0,1},{1,0},{2,3},{3,2},{4,5},{5,4},{6,7},{7,6},{8,9},{9,8},{10,11... | collective-permute-start | bytes 3145736 | tf_op jit(solution)/shard_map/ppermute | solution.py:309
  74.6 1.0 copy-start.2
  114.0 6.1 %collective-permute-start.6 = (f32[32,128]{1,0:T(8,128)S(1)}, f32[32,128]{1,0:T(8,128)S(1)}, u32[]{:S(2)}, u32[]{:S(2)}) collective-permute-start(f32[32,128]{1,0:T(8,128)S(1)} %slice_bitcast_fusion), channel_id=1, source_target_pairs={{0,1},{1,0},{2,3},{3,2},{4,5},{5,4},{6,7},{7,6},{8,9},{9,8},{10,11... | collective-permute-start | bytes 49160 | tf_op jit(solution)/shard_map/ppermute | solution.py:322
  114.1 12.5 %collective-permute-start.4 = (f32[4,512]{1,0:T(4,128)S(1)}, f32[4,512]{1,0:T(4,128)S(1)}, u32[]{:S(2)}, u32[]{:S(2)}) collective-permute-start(f32[4,512]{1,0:T(4,128)S(1)} %slice.45), channel_id=1, source_target_pairs={{0,0},{1,2},{2,32},{3,34},{4,64},{5,66},{6,96},{7,98},{8,1},{9,3},... | collective-permute-start | bytes 24584 | tf_op jit(solution)/shard_map/ppermute | solution.py:319
  117.6 8.3 %collective-permute-start.5 = (f32[16,512]{1,0:T(8,128)S(1)}, f32[16,512]{1,0:T(8,128)S(1)}, u32[]{:S(2)}, u32[]{:S(2)}) collective-permute-start(f32[16,512]{1,0:T(8,128)S(1)} %slice.46), channel_id=1, source_target_pairs={{0,0},{1,128},{2,16},{3,144},{4,32},{5,160},{6,48},{7,176},{8,1},{... | collective-permute-start | bytes 98312 | tf_op jit(solution)/shard_map/ppermute | solution.py:320
Sparse Core Ops, SparseCore 0:
  47.7 47.1 reduce-scatter.4
  97.6 42.2 reduce-scatter.2

commit v8 on v7

--- a/solution.py
+++ b/solution.py
@@ -43,7 +43,7 @@
     fm_ref, core_ref, pooled_ref = refs[:3]
     ids_ref = refs[3] if with_ids else None
     (cot_hbm, projt_ref, wup_hbm, wdown_hbm, wc_ref, gain_ref, bags_ref, keep_ref, send_ref, tail_ref,
-     inv_ref, ds1, ds2, wups, wupr, cot_ref, wup_ref, wdown_ref, sems) = refs[3 + with_ids:]
+     inv_ref, ds1, ds2, wupr, cot_ref, wup_ref, wdown_ref, sems) = refs[3 + with_ids:]
     copies = [pltpu.make_async_copy(source, target, sems.at[i]) for i, (source, target) in enumerate((
         (wup_hbm, wup_ref), (wdown_hbm, wdown_ref), (cot_hbm.at[pl.ds(part * b, b)], cot_ref)))]
     for copy in copies:
@@ -72,9 +72,10 @@
     nb = normed.astype(BF)
     copies[0].wait()
     for q in range(4):
-        wups[...] = wup_ref[:, q * 128:(q + 1) * 128].astype(F32)
-        for k in range(16):
-            wupr[k * 64:(k + 1) * 64, q * 128:(q + 1) * 128] = wups[pl.ds(k, 64, stride=16), :].astype(BF)
+        for n in range(4):
+            turned = jnp.swapaxes(wup_ref[n * 256:(n + 1) * 256, q * 128:(q + 1) * 128].reshape(16, 16, 128), 0, 1)
+            for k in range(16):
+                wupr[k * 64 + n * 16:k * 64 + n * 16 + 16, q * 128:(q + 1) * 128] = turned[k]
     preact = dot_nn(nb, wupr[...])
     sig = jax.nn.sigmoid(preact)
     hidden = (preact * sig).astype(BF)
@@ -164,7 +165,7 @@
                    jax.ShapeDtypeStruct((32, 128), F32)],
         scratch_shapes=[pltpu.SMEM((64,), jnp.int32),
                         pltpu.VMEM((32, batch, 128), F32), pltpu.VMEM((batch, 32, 128), F32),
-                        pltpu.VMEM((1024, 128), F32), pltpu.VMEM((1024, 512), BF),
+                        pltpu.VMEM((1024, 512), BF),
                         pltpu.VMEM((batch, 64, 128), BF), pltpu.VMEM((1024, 512), BF), pltpu.VMEM((512, 4096), BF),
                         pltpu.SemaphoreType.DMA((3,))],
         compiler_params=pltpu.CompilerParams(vmem_limit_bytes=VMEM_BYTES),
@@ -174,17 +175,17 @@
         + [cotangent, projt, w_up, w_down, w_compress, gain]))
 
 
-def weight_kernel(scale, a0_ref, b0_ref, a1_ref, b1_ref, tail0_ref, tail1_ref, w_ref, gus):
+def weight_kernel(scale, a0_ref, b0_ref, a1_ref, b1_ref, tail0_ref, tail1_ref, w_ref):
     acts = jnp.concatenate([a0_ref[...], b0_ref[...], a1_ref[...], b1_ref[...]], axis=0)
     tail = tail0_ref[...] + tail1_ref[...]
     tail = jnp.concatenate([tail[q * 8:(q + 1) * 8, :] for q in range(4)], axis=1)
     tail = jnp.concatenate([tail, jnp.zeros((8, 512), F32)], axis=0).astype(BF)
     up = dot_tn(acts[:, 0:512], acts[:, 512:1024]) * scale
     for q in range(4):
-        for k in range(8):
-            gus[pl.ds(k, 64, stride=8), :] = up[k * 64:(k + 1) * 64, q * 128:(q + 1) * 128]
         for z in range(8):
-            w_ref[z, 0:64, q * 128:(q + 1) * 128] = gus[z * 64:(z + 1) * 64, :].astype(BF)
+            turned = jnp.swapaxes(jnp.stack(
+                [up[k * 64 + z * 8:k * 64 + z * 8 + 8, q * 128:(q + 1) * 128] for k in range(8)], axis=0), 0, 1)
+            w_ref[z, 0:64, q * 128:(q + 1) * 128] = turned.reshape(64, 128).astype(BF)
     hid = acts[:, 1024:1280]
     for q in range(8):
         down = (dot_tn(hid, acts[:, 1280 + q * 512:1792 + q * 512]) * scale).astype(BF)
@@ -198,8 +199,7 @@
     return pl.pallas_call(
         functools.partial(weight_kernel, scale),
         out_shape=jax.ShapeDtypeStruct((8, 336, 512), BF),
-        scratch_shapes=[pltpu.VMEM((512, 128), F32)],
-        compiler_params=pltpu.CompilerParams(vmem_limit_bytes=VMEM_BYTES),
+        compiler_params=pltpu.CompilerParams(vmem_limit_bytes=24 << 20),
         cost_estimate=pl.CostEstimate(flops=3 * 10**9, bytes_accessed=6 << 20, transcendentals=0),
         name="weight_grads",
     )(*acts, *tails)
@@ -257,7 +257,7 @@
         out_specs=pl.BlockSpec((1, 4, 1, 512, 128), lambda j: (j // 2, 0, j % 2, 0, 0)) if last else sums,
         out_shape=jax.ShapeDtypeStruct((2, 4, 2, 512, 128), BF) if last else jax.ShapeDtypeStruct((4, 1024, 256), F32),
         scratch_shapes=[pltpu.VMEM((1024, 256), F32)] if last else [],
-        compiler_params=pltpu.CompilerParams(vmem_limit_bytes=VMEM_BYTES),
+        compiler_params=pltpu.CompilerParams(vmem_limit_bytes=32 << 20),
         cost_estimate=pl.CostEstimate(flops=9 * 10**9, bytes_accessed=5 << 20, transcendentals=0),
         name="table_last" if last else "table_first",
     )(*([core, own_ids, other_ids, own, other] + ([start] if last else [])))

time: 150 us -> 149 us (level)
  local copies, waits for them, and re-layouts: 8.18 us -> 11.5 us
  Pallas kernels: 54.2 us -> 50.9 us
    unnamed x14 -> x16, local copies, waits for them, and re-layouts: 3.92 us -> 7.24 us
    pallas_call x1, Pallas kernels: 4.39 us -> 2.65 us  [weight_call(): pl.pallas_call(functools.partial(weight_kernel, scale), out_shape=jax.Sha...]
    pallas_call x2, Pallas kernels: 25.6 us -> 23.9 us  [table_call(): pl.pallas_call(functools.partial(table_kernel, last), grid=(4,), in_specs...]
  transfers between devices with their start and end apart: 11 -> 11, of which waited for: 7 -> 7; matrix products, arithmetic and copies ran while one was open for 4% -> 4% of each run, Pallas kernels for 28% -> 26%
where the time goes in v8:
time: 149 us; the launch traced here: 148 us
  Pallas kernels  50.9 us (34%)
  waiting for transfers between devices  31.8 us (21%)
  starting transfers between devices  21.5 us (14%)
  blocking collectives  15.9 us (11%)
  between operations  14.3 us (10%)
  local copies, waits for them, and re-layouts  11.5 us (8%)
  other arithmetic  2.53 us (2%)
    pallas_call x2, Pallas kernels, layer_call(): pl.pallas_call(functools.partial(layer_kernel, scale, batch, part, int(wi...  24.3 us
    pallas_call x2, Pallas kernels, table_call(): pl.pallas_call(functools.partial(table_kernel, last), grid=(4,), in_specs...  23.9 us
    all_to_all x1, blocking collectives, shards(): pieces = lax.all_to_all(pieces, ('y', 'x'), 0, 0, tiled=True)  15.9 us
    all_to_all x2, starting transfers between devices, exchange(): return lax.all_to_all(bag, ('y', 'x'), 0, 0, tiled=True)  14.7 us
    reduce_scatter x1, waiting for transfers between devices, shards(): lax.psum_scatter(rows.reshape(8192, 128), ('zh', 'zl'), scatter_dimension...  13.2 us
    unnamed x16, local copies, waits for them, and re-layouts  7.24 us
    reduce_scatter x1, waiting for transfers between devices, shards(): lax.psum_scatter(weights.reshape(8 * 336, 512), ('zh', 'zl'), scatter_dim...  6.41 us
    ppermute x1, waiting for transfers between devices, shards(): lax.ppermute(total[4:20], AXES, down_moves).reshape(8, 2, 512)  4.22 us
  transfers between devices with their start and end apart: 11, of which 7 were waited for; matrix products, arithmetic and copies ran while one was open for 4% of the time, Pallas kernels for 26%

profile of v8, /device:TPU:2, one launch (start us, length us, event | category | flops | bytes accessed | tf_op | source)
XLA Modules:
  0.0 148.4 jit_solution(16983439203640775928)
XLA Ops:
  7.2 12.1 %layer_first.1 = (bf16[64,80,128]{2,1,0:T(8,128)(2,1)}, bf16[64,5376]{1,0:T(8,128)(2,1)}, bf16[64,5376]{1,0:T(8,128)(2,1)}, f32[32,128]{1,0:T(8,128)}) custom-call(s32[64]{0:T(128)} %refs_0_.3, s32[1]{0:T(128)} %bitcast.refs_1_.refs_0_, bf16[128,64,128]{2,1,0:T(8,128)(2,1)} %refs_2_.3, s32[64,2,128]{2,1,0:T(2,128)} %bitcast.40, ...), custom_call_target="tpu_custom_call" | custom-call | flops 15000000512 | bytes 10485760 | tf_op jit(solution)/shard_map/layer_first/pallas_call | solution.py:155
  19.3 7.5 %all-to-all-start = ((bf16[64,80,128]{2,1,0:T(8,128)(2,1)}), bf16[64,80,128]{2,1,0:T(8,128)(2,1)S(1)}, u32[]{:S(2)}, u32[]{:S(2)}) async-start(bf16[64,80,128]{2,1,0:T(8,128)(2,1)} %get-tuple-element.33), calls=%async_computation | async-start | bytes 2621440 | tf_op jit(solution)/shard_map/all_to_all | solution.py:294
  27.1 12.2 %layer_second.1 = (bf16[64,64,128]{2,1,0:T(8,128)(2,1)}, bf16[64,5376]{1,0:T(8,128)(2,1)}, bf16[64,5376]{1,0:T(8,128)(2,1)}, f32[32,128]{1,0:T(8,128)}) custom-call(s32[64]{0:T(128)} %refs_0_.3, s32[1]{0:T(128)} %bitcast.refs_1_.refs_0_, bf16[128,64,128]{2,1,0:T(8,128)(2,1)} %refs_2_.3, bf16[128,64,128]{2,1,0:T(8,128)(2,1)} %refs_4_.1, ...), custom_call_target="tpu_custom_call" | custom-call | flops 15000000512 | bytes 10485760 | tf_op jit(solution)/shard_map/layer_second/pallas_call | solution.py:155
  39.3 0.5 collective-permute-start
  39.8 1.8 %collective-permute-done.1.b1_ref = bf16[64,5376]{1,0:T(8,128)(2,1)S(1)} collective-permute-done((bf16[64,5376]{1,0:T(8,128)(2,1)}, bf16[64,5376]{1,0:T(8,128)(2,1)S(1)}, u32[]{:S(2)}, u32[]{:S(2)}) %collective-permute-start.1) | collective-permute-done | bytes 688160 | tf_op jit(solution)/shard_map/ppermute | solution.py:299
  41.7 0.8 collective-permute-done.b0_ref
  42.5 1.1 copy-done.1
  43.6 0.7 copy-done.5
  44.3 2.7 %weight_grads.1 = bf16[8,336,512]{2,1,0:T(8,128)(2,1)} custom-call(bf16[64,5376]{1,0:T(8,128)(2,1)S(1)} %copy-done, bf16[64,5376]{1,0:T(8,128)(2,1)S(1)} %collective-permute-done.b0_ref, bf16[64,5376]{1,0:T(8,128)(2,1)S(1)} %copy-done.1, bf16[64,5376]{1,0:T(8,128)(2,1)S(1)} %collective-permute-done.1.b1_ref, f32[32,128]{1,0:T(8,128)S(1)} %copy-done.4, ...), custom_call_target="tpu_custom_call" | custom-call | flops 3000000000 | bytes 6291456 | tf_op jit(solution)/shard_map/weight_grads/pallas_call | solution.py:199
  47.2 7.2 %all-to-all-start.1 = ((bf16[64,64,128]{2,1,0:T(8,128)(2,1)}), bf16[64,64,128]{2,1,0:T(8,128)(2,1)S(1)}, u32[]{:S(2)}, u32[]{:S(2)}) async-start(bf16[64,64,128]{2,1,0:T(8,128)(2,1)} %get-tuple-element.35), calls=%async_computation.1 | async-start | bytes 2097152 | tf_op jit(solution)/shard_map/all_to_all | solution.py:294
  54.5 11.6 %table_first.1.refs_5_ = f32[4,1024,256]{2,1,0:T(8,128)S(1)} custom-call(s32[1]{0:T(128)} %bitcast.refs_1_.refs_0_, bf16[8,2,4,80,128]{4,3,2,1,0:T(8,128)(2,1)S(1)} %bitcast.30, bf16[8,2,4,80,128]{4,3,2,1,0:T(8,128)(2,1)} %collective-permute-done.2.refs_2_.refs_4_, bf16[8,2,4,80,128]{4,3,2,1,0:T(8,128)(2,1)S(1)} %bitcast.31, ...), custom_call_target="tpu_custom_call" | custom-call | flops 8999999488 | bytes 5242880 | tf_op jit(solution)/shard_map/table_first/pallas_call | solution.py:253
  66.1 1.9 %copy-done.2 = f32[4,1024,256]{2,1,0:T(8,128)} copy-done((f32[4,1024,256]{2,1,0:T(8,128)}, f32[4,1024,256]{2,1,0:T(8,128)S(1)}, u32[]{:S(2)}) %copy-start.2) | copy-done | bytes 4194328
  68.0 2.7 %all-to-all-done.1 = bf16[64,64,128]{2,1,0:T(8,128)(2,1)S(1)} async-done(((bf16[64,64,128]{2,1,0:T(8,128)(2,1)}), bf16[64,64,128]{2,1,0:T(8,128)(2,1)S(1)}, u32[]{:S(2)}, u32[]{:S(2)}) %all-to-all-start.1) | async-done | bytes 1048608 | tf_op jit(solution)/shard_map/all_to_all | solution.py:294
  70.7 2.7 %collective-permute-done.3.refs_4_ = bf16[8,2,4,64,128]{4,3,2,1,0:T(8,128)(2,1)S(1)} collective-permute-done((bf16[8,2,4,64,128]{4,3,2,1,0:T(8,128)(2,1)S(1)}, bf16[8,2,4,64,128]{4,3,2,1,0:T(8,128)(2,1)S(1)}, u32[]{:S(2)}, u32[]{:S(2)}) %collective-permute-start.3) | collective-permute-done | bytes 1048608 | tf_op jit(solution)/shard_map/ppermute | solution.py:309
  73.4 2.2 %copy-done.3 = f32[4,1024,256]{2,1,0:T(8,128)S(1)} copy-done((f32[4,1024,256]{2,1,0:T(8,128)S(1)}, f32[4,1024,256]{2,1,0:T(8,128)}, u32[]{:S(2)}) %copy-start.3) | copy-done | bytes 4194328
  75.6 12.3 %table_last.1 = bf16[2,4,2,512,128]{4,3,2,1,0:T(8,128)(2,1)} custom-call(s32[1]{0:T(128)} %bitcast.refs_1_.refs_0_, bf16[8,2,4,80,128]{4,3,2,1,0:T(8,128)(2,1)S(1)} %bitcast.32, bf16[8,2,4,80,128]{4,3,2,1,0:T(8,128)(2,1)} %collective-permute-done.2.refs_2_.refs_4_, bf16[8,2,4,64,128]{4,3,2,1,0:T(8,128)(2,1)S(1)} %bitcast.34, ...), custom_call_target="tpu_custom_call" | custom-call | flops 8999999488 | bytes 5242880 | tf_op jit(solution)/shard_map/table_last/pallas_call | solution.py:253
  88.0 6.4 %reduce-scatter.5.cloned.1.call-done = bf16[336,512]{1,0:T(8,128)(2,1)} async-done(((bf16[2688,512]{1,0:T(8,128)(2,1)}), bf16[336,512]{1,0:T(8,128)(2,1)}) %reduce-scatter.5.cloned.1.call-update) | async-done | bytes 344080 | tf_op jit(solution)/shard_map/reduce_scatter | solution.py:302
  94.4 0.7 slice.36
  95.1 0.8 slice.34
  95.9 1.0 slice.35
  97.2 0.3 copy.22
  97.4 15.9 %all_to_all.15 = bf16[16,28,512]{2,1,0:T(8,128)(2,1)S(1)} all-to-all(bf16[16,28,512]{2,1,0:T(8,128)(2,1)S(1)} %copy.22), channel_id=1, replica_groups=mesh['y'=4,'zh'=2,'x'=4,'zl'=4,'c'=2] {'y','x'}, dimensions={0} | all-to-all | bytes 917504 | tf_op jit(solution)/shard_map/all_to_all | solution.py:316
  113.6 3.5 %collective-permute-start.4 = (f32[4,512]{1,0:T(4,128)S(1)}, f32[4,512]{1,0:T(4,128)S(1)}, u32[]{:S(2)}, u32[]{:S(2)}) collective-permute-start(f32[4,512]{1,0:T(4,128)S(1)} %slice.45), channel_id=1, source_target_pairs={{0,0},{1,2},{2,32},{3,34},{4,64},{5,66},{6,96},{7,98},{8,1},{9,3},... | collective-permute-start | bytes 24584 | tf_op jit(solution)/shard_map/ppermute | solution.py:319
  117.0 2.2 %collective-permute-start.5 = (f32[16,512]{1,0:T(8,128)S(1)}, f32[16,512]{1,0:T(8,128)S(1)}, u32[]{:S(2)}, u32[]{:S(2)}) collective-permute-start(f32[16,512]{1,0:T(8,128)S(1)} %slice.46), channel_id=1, source_target_pairs={{0,0},{1,128},{2,16},{3,144},{4,32},{5,160},{6,48},{7,176},{8,1},{... | collective-permute-start | bytes 98312 | tf_op jit(solution)/shard_map/ppermute | solution.py:320
  119.3 0.5 slice_bitcast_fusion.2
  119.8 0.7 slice_bitcast_fusion.1
  120.5 0.6 pad_maximum_fusion.1
  121.1 4.2 %collective-permute-done.5 = f32[16,512]{1,0:T(8,128)S(1)} collective-permute-done((f32[16,512]{1,0:T(8,128)S(1)}, f32[16,512]{1,0:T(8,128)S(1)}, u32[]{:S(2)}, u32[]{:S(2)}) %collective-permute-start.5) | collective-permute-done | bytes 32800 | tf_op jit(solution)/shard_map/ppermute | solution.py:320
  125.4 0.6 copy.24
  126.0 13.2 %reduce-scatter.3.cloned.1.call-done = bf16[1024,128]{1,0:T(8,128)(2,1)} async-done(((bf16[8192,128]{1,0:T(8,128)(2,1)}), bf16[1024,128]{1,0:T(8,128)(2,1)}) %reduce-scatter.3.cloned.1.call-update) | async-done | bytes 262160 | tf_op jit(solution)/shard_map/reduce_scatter | solution.py:311
  139.2 1.8 %convert.1 = f32[2,512,128]{2,1,0:T(8,128)} convert(bf16[2,512,128]{2,1,0:T(8,128)(2,1)} %bitcast.37) | non-fusion elementwise | flops 131072 | bytes 786432 | tf_op jit(solution)/shard_map/reshape | solution.py:326
  141.0 0.6 copy.28
  (36 shorter events, 1.2 us)
Async XLA Ops:
  19.3 27.6 %all-to-all-start = ((bf16[64,80,128]{2,1,0:T(8,128)(2,1)}), bf16[64,80,128]{2,1,0:T(8,128)(2,1)S(1)}, u32[]{:S(2)}, u32[]{:S(2)}) async-start(bf16[64,80,128]{2,1,0:T(8,128)(2,1)} %get-tuple-element.33), calls=%async_computation | async-start | bytes 2621440 | tf_op jit(solution)/shard_map/all_to_all | solution.py:294
  26.8 12.5 %copy-start.6 = (bf16[64,5376]{1,0:T(8,128)(2,1)S(1)}, bf16[64,5376]{1,0:T(8,128)(2,1)}, u32[]{:S(2)}) copy-start(bf16[64,5376]{1,0:T(8,128)(2,1)} %get-tuple-element.28) | copy-start | bytes 2064388
  26.8 15.6 %copy-start = (bf16[64,5376]{1,0:T(8,128)(2,1)S(1)}, bf16[64,5376]{1,0:T(8,128)(2,1)}, u32[]{:S(2)}) copy-start(bf16[64,5376]{1,0:T(8,128)(2,1)} %get-tuple-element.27.a0_ref) | copy-start | bytes 2064388
  26.8 15.6 %copy-start.4 = (f32[32,128]{1,0:T(8,128)S(1)}, f32[32,128]{1,0:T(8,128)}, u32[]{:S(2)}) copy-start(f32[32,128]{1,0:T(8,128)} %get-tuple-element.31.tail0_ref) | copy-start | bytes 49156
  26.8 67.6 %reduce-scatter.5.cloned.1.call-start = ((), (), s32[]{:S(2)}) async-start(), calls=%async_computation.6 | async-start | bytes 3096576 | tf_op jit(solution)/shard_map/reduce_scatter | solution.py:302
  39.2 2.4 %collective-permute-start.1 = (bf16[64,5376]{1,0:T(8,128)(2,1)}, bf16[64,5376]{1,0:T(8,128)(2,1)S(1)}, u32[]{:S(2)}, u32[]{:S(2)}) collective-permute-start(bf16[64,5376]{1,0:T(8,128)(2,1)} %get-tuple-element.30), channel_id=1, source_target_pairs={{0,1},{1,0},{2,3},{3,2},{4,5},{5,4},{6,7},{7,6},{8,9},{9,8},{10,11... | collective-permute-start | bytes 2064392 | tf_op jit(solution)/shard_map/ppermute | solution.py:299
  39.3 3.1 %collective-permute-start = (bf16[64,5376]{1,0:T(8,128)(2,1)S(1)}, bf16[64,5376]{1,0:T(8,128)(2,1)S(1)}, u32[]{:S(2)}, u32[]{:S(2)}) collective-permute-start(bf16[64,5376]{1,0:T(8,128)(2,1)S(1)} %copy-done.6), channel_id=1, source_target_pairs={{0,1},{1,0},{2,3},{3,2},{4,5},{5,4},{6,7},{7,6},{8,9},{9,8},{10,11... | collective-permute-start | bytes 2064392 | tf_op jit(solution)/shard_map/ppermute | solution.py:299
  42.4 1.1 copy-start.1
  43.6 0.7 copy-start.5
  47.0 7.5 %collective-permute-start.2 = (bf16[8,2,4,80,128]{4,3,2,1,0:T(8,128)(2,1)S(1)}, bf16[8,2,4,80,128]{4,3,2,1,0:T(8,128)(2,1)}, u32[]{:S(2)}, u32[]{:S(2)}) collective-permute-start(bf16[8,2,4,80,128]{4,3,2,1,0:T(8,128)(2,1)S(1)} %bitcast.29), channel_id=1, source_target_pairs={{0,1},{1,0},{2,3},{3,2},{4,5},{5,4},{6,7},{7,6},{8,9},{9,8},{10,11... | collective-permute-start | bytes 3932168 | tf_op jit(solution)/shard_map/ppermute | solution.py:305
  47.2 23.5 %all-to-all-start.1 = ((bf16[64,64,128]{2,1,0:T(8,128)(2,1)}), bf16[64,64,128]{2,1,0:T(8,128)(2,1)S(1)}, u32[]{:S(2)}, u32[]{:S(2)}) async-start(bf16[64,64,128]{2,1,0:T(8,128)(2,1)} %get-tuple-element.35), calls=%async_computation.1 | async-start | bytes 2097152 | tf_op jit(solution)/shard_map/all_to_all | solution.py:294
  54.4 84.8 %reduce-scatter.3.cloned.1.call-start = ((), (), s32[]{:S(2)}) async-start(), calls=%async_computation.5 | async-start | bytes 2359296 | tf_op jit(solution)/shard_map/reduce_scatter | solution.py:311
  66.1 2.0 %copy-start.2 = (f32[4,1024,256]{2,1,0:T(8,128)}, f32[4,1024,256]{2,1,0:T(8,128)S(1)}, u32[]{:S(2)}) copy-start(f32[4,1024,256]{2,1,0:T(8,128)S(1)} %table_first.1.refs_5_) | copy-start | bytes 12582916
  70.7 2.7 %collective-permute-start.3 = (bf16[8,2,4,64,128]{4,3,2,1,0:T(8,128)(2,1)S(1)}, bf16[8,2,4,64,128]{4,3,2,1,0:T(8,128)(2,1)S(1)}, u32[]{:S(2)}, u32[]{:S(2)}) collective-permute-start(bf16[8,2,4,64,128]{4,3,2,1,0:T(8,128)(2,1)S(1)} %bitcast.33), channel_id=1, source_target_pairs={{0,1},{1,0},{2,3},{3,2},{4,5},{5,4},{6,7},{7,6},{8,9},{9,8},{10,11... | collective-permute-start | bytes 3145736 | tf_op jit(solution)/shard_map/ppermute | solution.py:309
  73.4 2.2 %copy-start.3 = (f32[4,1024,256]{2,1,0:T(8,128)S(1)}, f32[4,1024,256]{2,1,0:T(8,128)}, u32[]{:S(2)}) copy-start(f32[4,1024,256]{2,1,0:T(8,128)} %copy-done.2) | copy-start | bytes 12582916
  113.5 5.8 %collective-permute-start.6 = (f32[32,128]{1,0:T(8,128)S(1)}, f32[32,128]{1,0:T(8,128)S(1)}, u32[]{:S(2)}, u32[]{:S(2)}) collective-permute-start(f32[32,128]{1,0:T(8,128)S(1)} %slice_bitcast_fusion), channel_id=1, source_target_pairs={{0,1},{1,0},{2,3},{3,2},{4,5},{5,4},{6,7},{7,6},{8,9},{9,8},{10,11... | collective-permute-start | bytes 49160 | tf_op jit(solution)/shard_map/ppermute | solution.py:322
  113.6 12.5 %collective-permute-start.4 = (f32[4,512]{1,0:T(4,128)S(1)}, f32[4,512]{1,0:T(4,128)S(1)}, u32[]{:S(2)}, u32[]{:S(2)}) collective-permute-start(f32[4,512]{1,0:T(4,128)S(1)} %slice.45), channel_id=1, source_target_pairs={{0,0},{1,2},{2,32},{3,34},{4,64},{5,66},{6,96},{7,98},{8,1},{9,3},... | collective-permute-start | bytes 24584 | tf_op jit(solution)/shard_map/ppermute | solution.py:319
  117.0 8.3 %collective-permute-start.5 = (f32[16,512]{1,0:T(8,128)S(1)}, f32[16,512]{1,0:T(8,128)S(1)}, u32[]{:S(2)}, u32[]{:S(2)}) collective-permute-start(f32[16,512]{1,0:T(8,128)S(1)} %slice.46), channel_id=1, source_target_pairs={{0,0},{1,128},{2,16},{3,144},{4,32},{5,160},{6,48},{7,176},{8,1},{... | collective-permute-start | bytes 98312 | tf_op jit(solution)/shard_map/ppermute | solution.py:320
Sparse Core Ops, SparseCore 0:
  47.1 47.2 reduce-scatter.4
  97.1 42.0 reduce-scatter.2
